TPU v7x, 32 devices: a whole 2x2x4 slice. The times are simulated.
32 devices in a mesh: gx: 16 (over z, y, core), gy: 2 (over x).
Axes of the slice: x: 2, y: 2, z: 4, core: 2. Of those that a mesh axis runs over, the one named last changes fastest.
Arguments:
- embed: bfloat16 [32, 8, 128, 128], P('gx', 'gy')
- frac: bfloat16 [32, 8, 3, 128], P('gx', 'gy'), may hold values from 0 to 1
- pair_blocks: int32 [32, 8, 5], P('gx', 'gy'), may hold values from 0 to 8, as said below
- w_in: bfloat16 [128, 128], replicated, may hold values from -0.5 to 0.5
- rbf_mix: float32 [8, 128], replicated, may hold values from -4 to 4
- w_charge: bfloat16 [128, 128], replicated, may hold values from -0.5 to 0.5
- k_index: int32 [3, 512], replicated, may hold values from -8 to 8
- k_weight: float32 [512], replicated, may hold values from 0.2 to 2
Outputs:
- updated: float32 [32, 8, 128, 128], P('gx', 'gy')
Inputs may be any that keep to these rules, and one draw needn't show every extreme that they name: `pair_blocks`: for every column, 5 different codes 3 * (dx + 1) + (dy + 1) of columns at offsets dx, dy in -1, 0, 1 along the first two dimensions; the first code is 4, the column itself, the others name other columns.
All inputs are finite; a program needn't handle non-finite values.
Results may differ from a plain program's by a relative error of at most 0.002.
Values may be sent and summed in bfloat16 or wider, within the bound.
No kernel may reach another device: no remote copies, remote signals or barrier semaphores. Data moves between devices by JAX's collectives and lax.ppermute only.
A program may use at most 64 MiB of HBM per device.

v0:
```python
import functools
import math

import jax
import jax.numpy as jnp
from jax import lax
from jax.experimental import pallas as pl
from jax.experimental.pallas import tpu as pltpu
from jax.sharding import PartitionSpec as P

CELL = 5.0
HEIGHT = 51.2
MSG_SCALE = 0.5
LANES = 128
FRAC_ROWS = 16
TAIL = 32
MIB = 1024 * 1024

COS_POLY = (0.9999992251396179, -19.738981246948242, 64.92865753173828, -85.27162170410156, 58.79049301147461, -21.07110595703125)
SIN_POLY = (6.283185005187988, -41.341590881347656, 81.59994506835938, -76.61447143554688, 41.3428840637207, -12.471243858337402)
ENV_POLY = (0.9999998211860657, -0.23369461297988892, 0.019939105957746506, -0.000846334092784673)


def horner(coefs, s):
    acc = coefs[-1] * s + coefs[-2]
    for c in coefs[-3::-1]:
        acc = acc * s + c
    return acc


def outer_rows(d, nb):
    rhs = jnp.broadcast_to(d[nb : nb + 1], (8, LANES)) * 0.125
    return [
        lax.dot_general(
            jnp.broadcast_to(d[b : b + 1], (8, LANES)),
            rhs,
            (((0,), (0,)), ((), ())),
            precision=lax.Precision.HIGHEST,
            preferred_element_type=jnp.float32,
        )
        for b in range(nb)
    ]


def put_message(send_ref, half, state):
    hi = state.astype(jnp.bfloat16).astype(jnp.float32)
    rest = state - hi
    mid = rest.astype(jnp.bfloat16).astype(jnp.float32)
    low = rest - mid
    send_ref[half : half + TAIL, :] = jnp.concatenate([hi, mid, low, jnp.zeros_like(hi)], axis=0).astype(
        jnp.bfloat16
    )


def tables_kernel(nx, ny, frac_ref, kidx_ref, emb_ref, cs_ref, acc_ref, state_ref, send_ref, k16, x16, sums, states):
    rows, cols, _, atoms = frac_ref.shape
    kvec = kidx_ref.shape[1]
    nb = kvec // LANES
    n = rows * cols * atoms
    me_x, me_y = lax.axis_index("gx"), lax.axis_index("gy")
    kf = kidx_ref[...].astype(jnp.float32)
    k16[...] = jnp.zeros_like(k16)
    x16[...] = jnp.zeros_like(x16)
    k16[0:1, :] = kf[0:1] * (1.0 / nx)
    k16[1:2, :] = kf[0:1] * (1.0 / nx)
    k16[2:3, :] = kf[1:2] * (1.0 / ny)
    k16[3:4, :] = kf[1:2] * (1.0 / ny)
    k16[4:5, :] = kf[2:3]
    for r in range(rows):
        for c in range(cols):
            at = slice((r * cols + c) * atoms, (r * cols + c + 1) * atoms)
            f = frac_ref[r, c].astype(jnp.float32)
            x16[0:1, at] = jnp.full((1, atoms), me_x * rows + r, jnp.int32).astype(jnp.float32)
            x16[1:2, at] = f[0:1]
            x16[2:3, at] = jnp.full((1, atoms), me_y * cols + c, jnp.int32).astype(jnp.float32)
            x16[3:4, at] = f[1:2]
            x16[4:5, at] = f[2:3]
    kb = k16[...].astype(jnp.bfloat16)
    xb = x16[...].astype(jnp.bfloat16)
    for b in range(nb):
        turns = lax.dot_general(
            kb[:, b * LANES : (b + 1) * LANES], xb, (((0,), (0,)), ((), ())), preferred_element_type=jnp.float32
        )
        turns = turns - jnp.round(turns)
        square = turns * turns
        cs_ref[b * LANES : (b + 1) * LANES, :] = horner(COS_POLY, square).astype(jnp.bfloat16)
        cs_ref[kvec + b * LANES : kvec + (b + 1) * LANES, :] = (turns * horner(SIN_POLY, square)).astype(
            jnp.bfloat16
        )
    emb = emb_ref[...]
    ones = jnp.ones((16, n), jnp.bfloat16)
    mean = jnp.dot(ones, emb, preferred_element_type=jnp.float32)[0:1] * (1.0 / n)
    states[...] = jnp.zeros_like(states)
    for h in range(2):
        table = cs_ref[h * kvec : (h + 1) * kvec, :]
        count = lax.dot_general(ones, table, (((1,), (1,)), ((), ())), preferred_element_type=jnp.float32)
        for b in range(nb):
            states[h, b : b + 1, :] = count[0:1, b * LANES : (b + 1) * LANES]
        states[h, nb : nb + 1, :] = mean
        total = jnp.dot(table, emb, preferred_element_type=jnp.float32)
        for b, part in enumerate(outer_rows(states[h], nb)):
            sums[h, b * LANES : (b + 1) * LANES, :] = total[b * LANES : (b + 1) * LANES] - part
    core = lax.rem(me_x, 2)
    acc_ref[...] = sums[core]
    state_ref[...] = states[core]
    send_ref[0:kvec, :] = sums[1 - core].astype(jnp.bfloat16)
    put_message(send_ref, kvec, states[1 - core])


def merge_kernel(last, acc_ref, state_ref, got_ref, *outs):
    half = acc_ref.shape[0]
    nb = half // LANES
    tail = got_ref[half : half + TAIL, :].astype(jnp.float32)
    theirs = tail[0:8] + tail[8:16] + tail[16:24]
    mine = state_ref[...]
    row = lax.broadcasted_iota(jnp.int32, (8, LANES), 0)
    state = (mine + theirs) * jnp.where(row < nb, 1.0, 0.5)
    diff = (mine - theirs) * jnp.where(row < nb, 1.0, 0.5)
    for b, part in enumerate(outer_rows(diff, nb)):
        at = slice(b * LANES, (b + 1) * LANES)
        merged = acc_ref[at, :] + got_ref[at, :].astype(jnp.float32) + part
        if not last:
            outs[1][at, :] = merged
        outs[0][at, :] = merged.astype(jnp.bfloat16)
    if not last:
        outs[2][...] = state
        put_message(outs[0], half, state)


def pair_kernel(codes_ref, ext_ref, got1_ref, got2_ref, w_ref, mix_ref, out_ref, fields, feats, basis, gathered):
    rows, width, packed, channels = ext_ref.shape
    atoms = packed - FRAC_ROWS
    cols = width - 2
    npb = codes_ref.shape[-1]
    nrbf = mix_ref.shape[0]
    core = lax.rem(lax.axis_index("gx"), 2)
    w = w_ref[...]

    def take(slot, block):
        feats[slot] = jnp.dot(block[:atoms], w, preferred_element_type=jnp.float32).astype(jnp.bfloat16)
        fields[slot] = block[atoms:].astype(jnp.float32)[0:8]

    for r in range(rows):
        for c in range(width):
            take((r + 1) * width + c, ext_ref[r, c])

    def halo(before_ref, after_ref):
        for c in range(width):
            take(c, before_ref[c])
            take((rows + 1) * width + c, after_ref[c])

    @pl.when(core == 0)
    def _():
        halo(got2_ref, got1_ref)

    @pl.when(core == 1)
    def _():
        halo(got1_ref, got2_ref)

    order = lax.broadcasted_iota(jnp.int32, (nrbf, channels), 0).astype(jnp.float32) - nrbf // 2
    mix = mix_ref[...] * (jnp.exp(-order * order) * MSG_SCALE)

    def column(index, carry):
        r, c = index // cols, index % cols
        own = fields[(r + 1) * width + c + 1]
        own = jnp.transpose(jnp.concatenate([own] * (LANES // 8), axis=0))
        own_x = jnp.broadcast_to(own[:, 0:1] * CELL, (atoms, atoms))
        own_y = jnp.broadcast_to(own[:, 1:2] * CELL, (atoms, atoms))
        own_z = jnp.broadcast_to(own[:, 2:3] * HEIGHT, (atoms, atoms))
        for p in range(npb):
            code = codes_ref[index, p]
            step_x, step_y = code // 3 - 1, code % 3 - 1
            slot = (r + 1 + step_x) * width + c + 1 + step_y
            near = fields[slot]
            dx = (near[0:1] + step_x.astype(jnp.float32)) * CELL - own_x
            dy = (near[1:2] + step_y.astype(jnp.float32)) * CELL - own_y
            dz = jnp.abs(near[2:3] * HEIGHT - own_z)
            dz = jnp.minimum(dz, HEIGHT - dz)
            s = jnp.minimum((dx * dx + dy * dy + dz * dz) * (1.0 / (CELL * CELL)), 1.0)
            root = s * lax.rsqrt(jnp.maximum(s, 1e-30))
            z = root * (nrbf - 1.0) - nrbf // 2
            env = (1.0 - s) * horner(ENV_POLY, s)
            mid = env * env * jnp.exp(-z * z)
            up, down = jnp.exp(2.0 * z), jnp.exp(-2.0 * z)
            at = slice(p * atoms, (p + 1) * atoms)
            value = mid
            for q in range(nrbf // 2, nrbf):
                basis[q * atoms : (q + 1) * atoms, at] = value.astype(jnp.bfloat16)
                value = value * up
            value = mid
            for q in range(nrbf // 2 - 1, -1, -1):
                value = value * down
                basis[q * atoms : (q + 1) * atoms, at] = value.astype(jnp.bfloat16)
            gathered[at, :] = feats[slot]
        parts = jnp.dot(basis[...], gathered[...], preferred_element_type=jnp.float32)
        total = parts[0:atoms] * mix[0:1]
        for q in range(1, nrbf):
            total = total + parts[q * atoms : (q + 1) * atoms] * mix[q : q + 1]
        out_ref[index] = total
        return carry

    lax.fori_loop(0, rows * cols, column, 0)


def field_kernel(scale, mine_ref, theirs_ref, weight_ref, w_ref, cs_ref, emb_ref, msg_ref, out_ref):
    kvec = mine_ref.shape[0]
    cells, atoms, _ = out_ref.shape
    first = lax.rem(lax.axis_index("gx"), 2) == 0
    mine, theirs = mine_ref[...].astype(jnp.float32), theirs_ref[...].astype(jnp.float32)
    w_t = jnp.transpose(w_ref[...].astype(jnp.float32)).astype(jnp.bfloat16)
    weight = weight_ref[...] * scale
    total = None
    for h in range(2):
        half = jnp.where(first, mine, theirs) if h == 0 else jnp.where(first, theirs, mine)
        factors = lax.dot_general(
            w_t, half.astype(jnp.bfloat16), (((1,), (1,)), ((), ())), preferred_element_type=jnp.float32
        )
        part = jnp.dot(
            (factors * weight).astype(jnp.bfloat16),
            cs_ref[h * kvec : (h + 1) * kvec, :],
            preferred_element_type=jnp.float32,
        )
        total = part if total is None else total + part
    for i in range(cells):
        out_ref[i] = (
            emb_ref[i * atoms : (i + 1) * atoms, :].astype(jnp.float32)
            + msg_ref[i]
            + jnp.transpose(total[:, i * atoms : (i + 1) * atoms])
        )


def vmem(count):
    return [pl.BlockSpec(memory_space=pltpu.VMEM)] * count


def shards(embed, frac, pair_blocks, w_in, rbf_mix, w_charge, k_index, k_weight):
    f32, bf16 = jnp.float32, jnp.bfloat16
    rows, cols, atoms, channels = embed.shape
    kvec = k_weight.shape[0]
    size_x, size_y = lax.axis_size("gx"), lax.axis_size("gy")
    count = size_x * size_y
    both = ("gx", "gy")
    cells = rows * cols
    atoms_all = cells * count * atoms
    flat = embed.reshape(-1, channels)
    params = functools.partial(pltpu.CompilerParams, vmem_limit_bytes=32 * MIB)

    packed = jnp.concatenate([embed, jnp.pad(frac, ((0, 0), (0, 0), (0, FRAC_ROWS - frac.shape[2]), (0, 0)))], axis=2)
    if size_y == 2:
        got = lax.ppermute(jnp.stack([packed[:, -1], packed[:, 0]], axis=1), "gy", [(0, 1), (1, 0)])
        west, east = got[:, 0:1], got[:, 1:2]
    else:
        west = lax.ppermute(packed[:, -1:], "gy", [(i, (i + 1) % size_y) for i in range(size_y)])
        east = lax.ppermute(packed[:, :1], "gy", [((i + 1) % size_y, i) for i in range(size_y)])
    ext = jnp.concatenate([west, packed, east], axis=1)
    core = lax.rem(lax.axis_index("gx"), 2)
    toward_1 = lax.dynamic_index_in_dim(ext, jnp.where(core == 0, rows - 1, 0), 0, keepdims=False)
    toward_2 = lax.dynamic_index_in_dim(ext, jnp.where(core == 0, 0, rows - 1), 0, keepdims=False)
    got_1 = lax.ppermute(toward_1, "gx", [(i, i ^ 1) for i in range(size_x)])
    got_2 = lax.ppermute(
        toward_2, "gx", [(i, (i - 1) % size_x if i % 2 == 0 else (i + 1) % size_x) for i in range(size_x)]
    )

    table, acc, state, send = pl.pallas_call(
        functools.partial(tables_kernel, rows * size_x, cols * size_y),
        out_shape=[
            jax.ShapeDtypeStruct((2 * kvec, cells * atoms), bf16),
            jax.ShapeDtypeStruct((kvec, channels), f32),
            jax.ShapeDtypeStruct((8, LANES), f32),
            jax.ShapeDtypeStruct((kvec + TAIL, channels), bf16),
        ],
        in_specs=vmem(3),
        out_specs=vmem(4),
        scratch_shapes=[
            pltpu.VMEM((16, kvec), f32),
            pltpu.VMEM((16, cells * atoms), f32),
            pltpu.VMEM((2, kvec, channels), f32),
            pltpu.VMEM((2, 8, LANES), f32),
        ],
        compiler_params=params(),
        name="tables",
    )(frac, k_index, flat)

    def merge(acc, state, got, last):
        out_shape = [jax.ShapeDtypeStruct((kvec if last else kvec + TAIL, channels), bf16)]
        if not last:
            out_shape += [jax.ShapeDtypeStruct(acc.shape, f32), jax.ShapeDtypeStruct(state.shape, f32)]
        return pl.pallas_call(
            functools.partial(merge_kernel, last),
            out_shape=out_shape,
            in_specs=vmem(3),
            out_specs=vmem(len(out_shape)),
            compiler_params=params(),
            name="merge",
        )(acc, state, got)

    def exchange(values, mask_of):
        return lax.ppermute(values, both, [(i, i ^ mask_of(i)) for i in range(count)])

    core_bit = size_y
    masks = [1 << b for b in range(count.bit_length() - 1) if 1 << b != core_bit]
    swapped = [masks[t ^ 1] if t ^ 1 < len(masks) else masks[t] for t in range(len(masks))]
    send, acc, state = merge(acc, state, exchange(send, lambda i: core_bit), False)
    for t in range(len(masks)):
        last = t == len(masks) - 1
        got = exchange(send, lambda i, t=t: swapped[t] if i & core_bit else masks[t])
        if last:
            (mine,) = merge(acc, state, got, True)
        else:
            send, acc, state = merge(acc, state, got, False)
    theirs = exchange(mine, lambda i: core_bit)

    width = cols + 2
    npb = pair_blocks.shape[-1]
    nrbf = rbf_mix.shape[0]
    slots = (rows + 2) * width
    messages = pl.pallas_call(
        pair_kernel,
        out_shape=jax.ShapeDtypeStruct((cells, atoms, channels), f32),
        in_specs=[pl.BlockSpec(memory_space=pltpu.SMEM)] + vmem(5),
        out_specs=pl.BlockSpec(memory_space=pltpu.VMEM),
        scratch_shapes=[
            pltpu.VMEM((slots, 8, atoms), f32),
            pltpu.VMEM((slots, atoms, channels), bf16),
            pltpu.VMEM((nrbf * atoms, npb * atoms), bf16),
            pltpu.VMEM((npb * atoms, channels), bf16),
        ],
        compiler_params=params(),
        name="pairs",
    )(pair_blocks.reshape(cells, npb), ext, got_1, got_2, w_in, rbf_mix)

    updated = pl.pallas_call(
        functools.partial(field_kernel, 1.0 / math.sqrt(atoms_all * kvec)),
        out_shape=jax.ShapeDtypeStruct((cells, atoms, channels), f32),
        in_specs=vmem(7),
        out_specs=pl.BlockSpec(memory_space=pltpu.VMEM),
        compiler_params=params(),
        name="field",
    )(mine, theirs, k_weight.reshape(1, kvec), w_charge, table, flat, messages)
    return updated.reshape(embed.shape)


def solution(mesh):
    in_specs = (
        P("gx", "gy", None, None),
        P("gx", "gy", None, None),
        P("gx", "gy", None),
        P(),
        P(),
        P(),
        P(),
        P(),
    )
    out_specs = P("gx", "gy", None, None)
    return jax.shard_map(shards, mesh=mesh, in_specs=in_specs, out_specs=out_specs, check_vma=False)
```

profile of v0, /device:TPU:0, one launch (start us, length us, event | category | flops | bytes accessed | tf_op | source)
XLA Modules:
  0.0 49.4 jit_solution(4491671751992273706)
XLA Ops:
  0.0 0.7 %copy.9.frac_ref = bf16[2,4,3,128]{3,2,1,0:T(4,128)(2,1)S(1)} copy(bf16[2,4,3,128]{3,1,2,0:T(4,128)(2,1)} %param.9) | data formatting | bytes 12288 | tf_op args[1]
  0.7 0.9 %copy-done = bf16[2,4,128,128]{3,2,1,0:T(8,128)(2,1)S(1)} copy-done((bf16[2,4,128,128]{3,2,1,0:T(8,128)(2,1)S(1)}, bf16[2,4,128,128]{3,2,1,0:T(8,128)(2,1)}, u32[]{:S(2)}) %copy-start) | copy-done | bytes 262168
  1.6 0.7 %copy-done.4 = s32[3,512]{1,0:T(4,128)S(1)} copy-done((s32[3,512]{1,0:T(4,128)S(1)}, s32[3,512]{1,0:T(4,128)}, u32[]{:S(2)}) %copy-start.4) | copy-done | bytes 6168
  2.3 3.6 %tables.1 = (bf16[1024,1024]{1,0:T(8,128)(2,1)S(1)}, f32[512,128]{1,0:T(8,128)S(1)}, f32[8,128]{1,0:T(8,128)S(1)}, bf16[544,128]{1,0:T(8,128)(2,1)S(1)}) custom-call(bf16[2,4,3,128]{3,2,1,0:T(4,128)(2,1)S(1)} %copy.9.frac_ref, s32[3,512]{1,0:T(4,128)S(1)} %copy-done.4, bf16[1024,128]{1,0:T(8,128)(2,1)S(1)} %bitcast.8), custom_call_target="tpu_custom_call" | custom-call | tf_op jit(solution)/shard_map/tables/pallas_call | solution.py:264
  6.0 0.5 %collective-permute-start = (bf16[544,128]{1,0:T(8,128)(2,1)S(1)}, bf16[544,128]{1,0:T(8,128)(2,1)S(1)}, u32[]{:S(2)}, u32[]{:S(2)}) collective-permute-start(bf16[544,128]{1,0:T(8,128)(2,1)S(1)} %get-tuple-element.23), channel_id=1, source_target_pairs={{0,2},{1,3},{2,0},{3,1},{4,6},{5,7},{6,4},{7,5},{8,10},{9,11},{10,... | collective-permute-start | bytes 417800 | tf_op jit(solution)/shard_map/ppermute | solution.py:298
  6.5 1.0 %collective-permute-done.got_ref = bf16[544,128]{1,0:T(8,128)(2,1)S(1)} collective-permute-done((bf16[544,128]{1,0:T(8,128)(2,1)S(1)}, bf16[544,128]{1,0:T(8,128)(2,1)S(1)}, u32[]{:S(2)}, u32[]{:S(2)}) %collective-permute-start) | collective-permute-done | bytes 139296 | tf_op jit(solution)/shard_map/ppermute | solution.py:298
  7.5 0.4 merge.5
  8.0 2.9 %collective-permute-start.1 = (bf16[544,128]{1,0:T(8,128)(2,1)S(1)}, bf16[544,128]{1,0:T(8,128)(2,1)S(1)}, u32[]{:S(2)}, u32[]{:S(2)}) collective-permute-start(bf16[544,128]{1,0:T(8,128)(2,1)S(1)} %get-tuple-element.26), channel_id=1, source_target_pairs={{0,1},{1,0},{2,6},{3,7},{4,5},{5,4},{6,2},{7,3},{8,9},{9,8},{10,14... | collective-permute-start | bytes 417800 | tf_op jit(solution)/shard_map/ppermute | solution.py:298
  10.9 0.0 copy-start.3
  10.9 0.0 copy-start.5
  10.9 0.0 copy-start.6
  10.9 0.1 collective-permute-start.6
  11.0 3.4 %collective-permute-done.1.got_ref = bf16[544,128]{1,0:T(8,128)(2,1)S(1)} collective-permute-done((bf16[544,128]{1,0:T(8,128)(2,1)S(1)}, bf16[544,128]{1,0:T(8,128)(2,1)S(1)}, u32[]{:S(2)}, u32[]{:S(2)}) %collective-permute-start.1) | collective-permute-done | bytes 139296 | tf_op jit(solution)/shard_map/ppermute | solution.py:298
  14.4 0.4 merge.6
  14.9 2.5 %collective-permute-start.2 = (bf16[544,128]{1,0:T(8,128)(2,1)S(1)}, bf16[544,128]{1,0:T(8,128)(2,1)S(1)}, u32[]{:S(2)}, u32[]{:S(2)}) collective-permute-start(bf16[544,128]{1,0:T(8,128)(2,1)S(1)} %get-tuple-element.29), channel_id=1, source_target_pairs={{0,4},{1,5},{2,3},{3,2},{4,0},{5,1},{6,7},{7,6},{8,12},{9,13},{10,... | collective-permute-start | bytes 417800 | tf_op jit(solution)/shard_map/ppermute | solution.py:298
  17.4 3.0 %collective-permute-done.2.got_ref = bf16[544,128]{1,0:T(8,128)(2,1)S(1)} collective-permute-done((bf16[544,128]{1,0:T(8,128)(2,1)S(1)}, bf16[544,128]{1,0:T(8,128)(2,1)S(1)}, u32[]{:S(2)}, u32[]{:S(2)}) %collective-permute-start.2) | collective-permute-done | bytes 139296 | tf_op jit(solution)/shard_map/ppermute | solution.py:298
  20.4 0.4 merge.7
  20.9 2.2 %collective-permute-start.3 = (bf16[544,128]{1,0:T(8,128)(2,1)S(1)}, bf16[544,128]{1,0:T(8,128)(2,1)S(1)}, u32[]{:S(2)}, u32[]{:S(2)}) collective-permute-start(bf16[544,128]{1,0:T(8,128)(2,1)S(1)} %get-tuple-element.32), channel_id=1, source_target_pairs={{0,8},{1,9},{2,18},{3,19},{4,12},{5,13},{6,22},{7,23},{8,0},{9,1},... | collective-permute-start | bytes 417800 | tf_op jit(solution)/shard_map/ppermute | solution.py:298
  23.1 0.0 collective-permute-done.6
  23.1 0.0 copy-start.2
  23.1 0.0 copy-start.7
  23.2 3.3 %collective-permute-done.3.got_ref = bf16[544,128]{1,0:T(8,128)(2,1)S(1)} collective-permute-done((bf16[544,128]{1,0:T(8,128)(2,1)S(1)}, bf16[544,128]{1,0:T(8,128)(2,1)S(1)}, u32[]{:S(2)}, u32[]{:S(2)}) %collective-permute-start.3) | collective-permute-done | bytes 139296 | tf_op jit(solution)/shard_map/ppermute | solution.py:298
  26.5 0.4 merge.8
  26.9 2.8 %collective-permute-start.4 = (bf16[544,128]{1,0:T(8,128)(2,1)S(1)}, bf16[544,128]{1,0:T(8,128)(2,1)S(1)}, u32[]{:S(2)}, u32[]{:S(2)}) collective-permute-start(bf16[544,128]{1,0:T(8,128)(2,1)S(1)} %get-tuple-element.35), channel_id=1, source_target_pairs={{0,16},{1,17},{2,10},{3,11},{4,20},{5,21},{6,14},{7,15},{8,24},{9,... | collective-permute-start | bytes 417800 | tf_op jit(solution)/shard_map/ppermute | solution.py:298
  29.7 0.2 collective-permute-start.8
  30.0 1.6 %collective-permute-start.7 = (bf16[6,144,128]{2,1,0:T(8,128)(2,1)S(1)}, bf16[6,144,128]{2,1,0:T(8,128)(2,1)S(1)}, u32[]{:S(2)}, u32[]{:S(2)}) collective-permute-start(bf16[6,144,128]{2,1,0:T(8,128)(2,1)S(1)} %get-tuple-element.38), channel_id=1, source_target_pairs={{0,2},{2,0},{4,6},{6,4},{8,10},{10,8},{12,14},{14,12},{16,18},{18,... | collective-permute-start | bytes 663560 | tf_op jit(solution)/shard_map/ppermute | solution.py:259
  31.5 1.4 %collective-permute-done.4.got_ref = bf16[544,128]{1,0:T(8,128)(2,1)S(1)} collective-permute-done((bf16[544,128]{1,0:T(8,128)(2,1)S(1)}, bf16[544,128]{1,0:T(8,128)(2,1)S(1)}, u32[]{:S(2)}, u32[]{:S(2)}) %collective-permute-start.4) | collective-permute-done | bytes 139296 | tf_op jit(solution)/shard_map/ppermute | solution.py:298
  32.9 0.4 merge.9.mine_ref
  33.4 0.1 collective-permute-start.5
  33.5 4.4 %collective-permute-done.8.got2_ref = bf16[6,144,128]{2,1,0:T(8,128)(2,1)S(1)} collective-permute-done((bf16[6,144,128]{2,1,0:T(8,128)(2,1)S(1)}, bf16[6,144,128]{2,1,0:T(8,128)(2,1)S(1)}, u32[]{:S(2)}, u32[]{:S(2)}) %collective-permute-start.8) | collective-permute-done | bytes 221216 | tf_op jit(solution)/shard_map/ppermute | solution.py:260
  37.9 9.9 %pairs.1.msg_ref = f32[8,128,128]{2,1,0:T(8,128)S(1)} custom-call(s32[8,5]{1,0:T(8,128)S(1)} %bitcast.10, bf16[2,6,144,128]{3,2,1,0:T(8,128)(2,1)S(1)} %pad_maximum_fusion.ext_ref, bf16[6,144,128]{2,1,0:T(8,128)(2,1)S(1)} %collective-permute-done.7.got1_ref, bf16[6,144,128]{2,1,0:T(8,128)(2,1)S(1)} %collective-permute-done.8.got2_ref, ...), custom_call_target="tpu_custom_call" | custom-call | tf_op jit(solution)/shard_map/pairs/pallas_call | solution.py:317
  47.9 1.6 %field.1 = f32[8,128,128]{2,1,0:T(8,128)} custom-call(bf16[512,128]{1,0:T(8,128)(2,1)S(1)} %merge.9.mine_ref, bf16[512,128]{1,0:T(8,128)(2,1)S(1)} %collective-permute-done.5.theirs_ref, f32[1,512]{1,0:T(1,128)S(1)} %bitcast.11, bf16[128,128]{1,0:T(8,128)(2,1)S(1)} %copy-done.2, bf16[1024,1024]{1,0:T(8,128)(2,1)S(1)} %get-tuple-element.36.cs_ref, ...), custom_call_target="tpu_custom_call" | custom-call | tf_op jit(solution)/shard_map/field/pallas_call | solution.py:332
  (16 shorter events, 0.1 us)
Async XLA Ops:
  0.7 0.9 %copy-start = (bf16[2,4,128,128]{3,2,1,0:T(8,128)(2,1)S(1)}, bf16[2,4,128,128]{3,2,1,0:T(8,128)(2,1)}, u32[]{:S(2)}) copy-start(bf16[2,4,128,128]{3,2,1,0:T(8,128)(2,1)} %param.8) | copy-start | bytes 786436
  1.6 0.7 %copy-start.4 = (s32[3,512]{1,0:T(4,128)S(1)}, s32[3,512]{1,0:T(4,128)}, u32[]{:S(2)}) copy-start(s32[3,512]{1,0:T(4,128)} %kidx_ref.1) | copy-start | bytes 18436
  2.3 20.8 %copy-start.1 = (bf16[2,4,128,128]{3,2,1,0:T(8,128)(2,1)S(1)}, bf16[2,4,128,128]{3,2,1,0:T(8,128)(2,1)}, u32[]{:S(2)}) copy-start(bf16[2,4,128,128]{3,2,1,0:T(8,128)(2,1)} %param.8) | copy-start | bytes 786436
  6.0 1.5 %collective-permute-start = (bf16[544,128]{1,0:T(8,128)(2,1)S(1)}, bf16[544,128]{1,0:T(8,128)(2,1)S(1)}, u32[]{:S(2)}, u32[]{:S(2)}) collective-permute-start(bf16[544,128]{1,0:T(8,128)(2,1)S(1)} %get-tuple-element.23), channel_id=1, source_target_pairs={{0,2},{1,3},{2,0},{3,1},{4,6},{5,7},{6,4},{7,5},{8,10},{9,11},{10,... | collective-permute-start | bytes 417800 | tf_op jit(solution)/shard_map/ppermute | solution.py:298
  8.0 6.5 %collective-permute-start.1 = (bf16[544,128]{1,0:T(8,128)(2,1)S(1)}, bf16[544,128]{1,0:T(8,128)(2,1)S(1)}, u32[]{:S(2)}, u32[]{:S(2)}) collective-permute-start(bf16[544,128]{1,0:T(8,128)(2,1)S(1)} %get-tuple-element.26), channel_id=1, source_target_pairs={{0,1},{1,0},{2,6},{3,7},{4,5},{5,4},{6,2},{7,3},{8,9},{9,8},{10,14... | collective-permute-start | bytes 417800 | tf_op jit(solution)/shard_map/ppermute | solution.py:298
  10.9 27.0 %copy-start.3 = (bf16[128,128]{1,0:T(8,128)(2,1)S(1)}, bf16[128,128]{1,0:T(8,128)(2,1)}, u32[]{:S(2)}) copy-start(bf16[128,128]{1,0:T(8,128)(2,1)} %w_ref.2) | copy-start | bytes 98308
  10.9 27.0 %copy-start.5 = (s32[2,4,5]{2,1,0:T(4,128)S(1)}, s32[2,4,5]{2,1,0:T(4,128)}, u32[]{:S(2)}) copy-start(s32[2,4,5]{2,1,0:T(4,128)} %param.10) | copy-start | bytes 484
  10.9 27.0 %copy-start.6 = (f32[8,128]{1,0:T(8,128)S(1)}, f32[8,128]{1,0:T(8,128)}, u32[]{:S(2)}) copy-start(f32[8,128]{1,0:T(8,128)} %mix_ref.1) | copy-start | bytes 12292
  10.9 12.2 %collective-permute-start.6 = (bf16[2,2,144,128]{3,2,1,0:T(8,128)(2,1)S(1)}, bf16[2,2,144,128]{3,2,1,0:T(8,128)(2,1)S(1)}, u32[]{:S(2)}, u32[]{:S(2)}) collective-permute-start(bf16[2,2,144,128]{3,2,1,0:T(8,128)(2,1)S(1)} %fusion), channel_id=1, source_target_pairs={{0,1},{1,0},{2,3},{3,2},{4,5},{5,4},{6,7},{7,6},{8,9},{9,8},{10,11... | collective-permute-start | bytes 442376 | tf_op jit(solution)/shard_map/ppermute | solution.py:250
  14.9 5.5 %collective-permute-start.2 = (bf16[544,128]{1,0:T(8,128)(2,1)S(1)}, bf16[544,128]{1,0:T(8,128)(2,1)S(1)}, u32[]{:S(2)}, u32[]{:S(2)}) collective-permute-start(bf16[544,128]{1,0:T(8,128)(2,1)S(1)} %get-tuple-element.29), channel_id=1, source_target_pairs={{0,4},{1,5},{2,3},{3,2},{4,0},{5,1},{6,7},{7,6},{8,12},{9,13},{10,... | collective-permute-start | bytes 417800 | tf_op jit(solution)/shard_map/ppermute | solution.py:298
  20.9 5.6 %collective-permute-start.3 = (bf16[544,128]{1,0:T(8,128)(2,1)S(1)}, bf16[544,128]{1,0:T(8,128)(2,1)S(1)}, u32[]{:S(2)}, u32[]{:S(2)}) collective-permute-start(bf16[544,128]{1,0:T(8,128)(2,1)S(1)} %get-tuple-element.32), channel_id=1, source_target_pairs={{0,8},{1,9},{2,18},{3,19},{4,12},{5,13},{6,22},{7,23},{8,0},{9,1},... | collective-permute-start | bytes 417800 | tf_op jit(solution)/shard_map/ppermute | solution.py:298
  23.1 24.7 %copy-start.2 = (bf16[128,128]{1,0:T(8,128)(2,1)S(1)}, bf16[128,128]{1,0:T(8,128)(2,1)}, u32[]{:S(2)}) copy-start(bf16[128,128]{1,0:T(8,128)(2,1)} %w_ref.3) | copy-start | bytes 98308
  23.1 24.7 %copy-start.7 = (f32[512]{0:T(512)S(1)}, f32[512]{0:T(512)}, u32[]{:S(2)}) copy-start(f32[512]{0:T(512)} %param.15) | copy-start | bytes 6148
  26.9 6.0 %collective-permute-start.4 = (bf16[544,128]{1,0:T(8,128)(2,1)S(1)}, bf16[544,128]{1,0:T(8,128)(2,1)S(1)}, u32[]{:S(2)}, u32[]{:S(2)}) collective-permute-start(bf16[544,128]{1,0:T(8,128)(2,1)S(1)} %get-tuple-element.35), channel_id=1, source_target_pairs={{0,16},{1,17},{2,10},{3,11},{4,20},{5,21},{6,14},{7,15},{8,24},{9,... | collective-permute-start | bytes 417800 | tf_op jit(solution)/shard_map/ppermute | solution.py:298
  29.7 8.1 %collective-permute-start.8 = (bf16[6,144,128]{2,1,0:T(8,128)(2,1)S(1)}, bf16[6,144,128]{2,1,0:T(8,128)(2,1)S(1)}, u32[]{:S(2)}, u32[]{:S(2)}) collective-permute-start(bf16[6,144,128]{2,1,0:T(8,128)(2,1)S(1)} %get-tuple-element.37), channel_id=1, source_target_pairs={{0,30},{2,4},{4,2},{6,8},{8,6},{10,12},{12,10},{14,16},{16,14},{18... | collective-permute-start | bytes 663560 | tf_op jit(solution)/shard_map/ppermute | solution.py:260
  30.0 7.9 %collective-permute-start.7 = (bf16[6,144,128]{2,1,0:T(8,128)(2,1)S(1)}, bf16[6,144,128]{2,1,0:T(8,128)(2,1)S(1)}, u32[]{:S(2)}, u32[]{:S(2)}) collective-permute-start(bf16[6,144,128]{2,1,0:T(8,128)(2,1)S(1)} %get-tuple-element.38), channel_id=1, source_target_pairs={{0,2},{2,0},{4,6},{6,4},{8,10},{10,8},{12,14},{14,12},{16,18},{18,... | collective-permute-start | bytes 663560 | tf_op jit(solution)/shard_map/ppermute | solution.py:259
  33.4 14.4 %collective-permute-start.5 = (bf16[512,128]{1,0:T(8,128)(2,1)S(1)}, bf16[512,128]{1,0:T(8,128)(2,1)S(1)}, u32[]{:S(2)}, u32[]{:S(2)}) collective-permute-start(bf16[512,128]{1,0:T(8,128)(2,1)S(1)} %merge.9.mine_ref), channel_id=1, source_target_pairs={{0,2},{1,3},{2,0},{3,1},{4,6},{5,7},{6,4},{7,5},{8,10},{9,11},{10,... | collective-permute-start | bytes 393224 | tf_op jit(solution)/shard_map/ppermute | solution.py:298
where the time goes:
time: 49.7 us; the launch traced here: 49.4 us
  Pallas kernels  17.4 us (35%)
  waiting for transfers between devices  16.5 us (33%)
  starting transfers between devices  12.9 us (26%)
  local copies, waits for them, and re-layouts  2.43 us (5%)
    ppermute x6, waiting for transfers between devices, exchange(): lax.ppermute(values, both, [(i, i ^ mask_of(i)) for i in range(count)])  12.1 us
    ppermute x6, starting transfers between devices, exchange(): lax.ppermute(values, both, [(i, i ^ mask_of(i)) for i in range(count)])  11 us
    pallas_call x1, Pallas kernels, shards(): pl.pallas_call(pair_kernel, out_shape=jax.ShapeDtypeStruct((cells, atoms,...  9.94 us
    ppermute x1, waiting for transfers between devices, shards(): lax.ppermute(toward_2, 'gx', [(i, (i - 1) % size_x if i % 2 == 0 else (i...  4.38 us
    pallas_call x1, Pallas kernels, shards(): pl.pallas_call(functools.partial(tables_kernel, rows * size_x, cols * siz...  3.64 us
    unnamed x17, local copies, waits for them, and re-layouts  2.38 us
    pallas_call x5, Pallas kernels, merge(): pl.pallas_call(functools.partial(merge_kernel, last), out_shape=out_shape...  2.23 us
    ppermute x1, starting transfers between devices, shards(): got_1 = lax.ppermute(toward_1, 'gx', [(i, i ^ 1) for i in range(size_x)])  1.58 us
  transfers between devices with their start and end apart: 9, of which 6 were waited for; matrix products, arithmetic and copies ran while one was open for 0% of the time, Pallas kernels for 23%

commit v1 on v0

v1 whole, which is shorter than its diff:
```python
import functools
import math

import jax
import jax.numpy as jnp
from jax import lax
from jax.experimental import pallas as pl
from jax.experimental.pallas import tpu as pltpu
from jax.sharding import PartitionSpec as P

CELL = 5.0
HEIGHT = 51.2
MSG_SCALE = 0.5
LANES = 128
FRAC_ROWS = 16
TAIL = 32
MIB = 1024 * 1024

COS_POLY = (0.9999992251396179, -19.738981246948242, 64.92865753173828, -85.27162170410156, 58.79049301147461, -21.07110595703125)
SIN_POLY = (6.283185005187988, -41.341590881347656, 81.59994506835938, -76.61447143554688, 41.3428840637207, -12.471243858337402)
ENV_POLY = (0.9999998211860657, -0.23369461297988892, 0.019939105957746506, -0.000846334092784673)


def horner(coefs, s):
    acc = coefs[-1] * s + coefs[-2]
    for c in coefs[-3::-1]:
        acc = acc * s + c
    return acc


def outer_row(column, row):
    return lax.dot_general(
        jnp.broadcast_to(column, (8, LANES)),
        jnp.broadcast_to(row, (8, LANES)) * 0.125,
        (((0,), (0,)), ((), ())),
        precision=lax.Precision.HIGHEST,
        preferred_element_type=jnp.float32,
    )


def put_message(send_ref, half, state):
    hi = state.astype(jnp.bfloat16).astype(jnp.float32)
    rest = state - hi
    mid = rest.astype(jnp.bfloat16).astype(jnp.float32)
    low = rest - mid
    send_ref[half : half + TAIL, :] = jnp.concatenate([hi, mid, low, jnp.zeros_like(hi)], axis=0).astype(
        jnp.bfloat16
    )


def tables_kernel(sent, nx, ny, frac_ref, kidx_ref, emb_ref, after_ref, *refs):
    del after_ref
    if sent:
        table_ref, send_ref, k16, x16, state_ref = refs
    else:
        table_ref, acc_ref, state_ref, k16, x16 = refs
    rows, cols, _, atoms = frac_ref.shape
    kvec = kidx_ref.shape[1]
    nb = kvec // LANES
    n = rows * cols * atoms
    me_x, me_y = lax.axis_index("gx"), lax.axis_index("gy")
    core = lax.rem(me_x, 2)
    half = 1 - core if sent else core
    offset = half.astype(jnp.float32) * 0.25
    kf = kidx_ref[...].astype(jnp.float32)
    k16[...] = jnp.zeros_like(k16)
    x16[...] = jnp.zeros_like(x16)
    k16[0:1, :] = kf[0:1] * (1.0 / nx)
    k16[1:2, :] = kf[0:1] * (1.0 / nx)
    k16[2:3, :] = kf[1:2] * (1.0 / ny)
    k16[3:4, :] = kf[1:2] * (1.0 / ny)
    k16[4:5, :] = kf[2:3]
    for r in range(rows):
        for c in range(cols):
            at = slice((r * cols + c) * atoms, (r * cols + c + 1) * atoms)
            f = frac_ref[r, c].astype(jnp.float32)
            x16[0:1, at] = jnp.full((1, atoms), me_x * rows + r, jnp.int32).astype(jnp.float32)
            x16[1:2, at] = f[0:1]
            x16[2:3, at] = jnp.full((1, atoms), me_y * cols + c, jnp.int32).astype(jnp.float32)
            x16[3:4, at] = f[1:2]
            x16[4:5, at] = f[2:3]
    kb = k16[...].astype(jnp.bfloat16)
    xb = x16[...].astype(jnp.bfloat16)
    emb = emb_ref[...]
    ones = jnp.ones((16, n), jnp.bfloat16)
    mean = jnp.dot(ones, emb, preferred_element_type=jnp.float32)[0:1] * (1.0 / n)
    state_ref[...] = jnp.zeros_like(state_ref)
    state_ref[nb : nb + 1, :] = mean
    for b in range(nb):
        at = slice(b * LANES, (b + 1) * LANES)
        turns = lax.dot_general(kb[:, at], xb, (((0,), (0,)), ((), ())), preferred_element_type=jnp.float32)
        turns = turns - offset
        turns = turns - jnp.round(turns)
        table = horner(COS_POLY, turns * turns).astype(jnp.bfloat16)
        table_ref[at, :] = table
        count = lax.dot_general(ones, table, (((1,), (1,)), ((), ())), preferred_element_type=jnp.float32)
        state_ref[b : b + 1, :] = count[0:1]
        centred = jnp.dot(table, emb, preferred_element_type=jnp.float32) - outer_row(count[0:1], mean)
        if sent:
            send_ref[at, :] = centred.astype(jnp.bfloat16)
        else:
            acc_ref[at, :] = centred
    if sent:
        put_message(send_ref, kvec, state_ref[...])


def merge_kernel(last, acc_ref, state_ref, got_ref, after_ref, *outs):
    del after_ref
    half = acc_ref.shape[0]
    nb = half // LANES
    tail = got_ref[half : half + TAIL, :].astype(jnp.float32)
    theirs = tail[0:8] + tail[8:16] + tail[16:24]
    mine = state_ref[...]
    weight = jnp.where(lax.broadcasted_iota(jnp.int32, (8, LANES), 0) < nb, 1.0, 0.5)
    state = (mine + theirs) * weight
    diff = (mine - theirs) * weight
    for b in range(nb):
        at = slice(b * LANES, (b + 1) * LANES)
        part = outer_row(diff[b : b + 1], diff[nb : nb + 1])
        merged = acc_ref[at, :] + got_ref[at, :].astype(jnp.float32) + part
        if not last:
            outs[1][at, :] = merged
        outs[0][at, :] = merged.astype(jnp.bfloat16)
    if not last:
        outs[2][...] = state
        put_message(outs[0], half, state)


def feats_kernel(frac_ref, emb_ref, w_ref, after_ref, out_ref):
    del after_ref
    rows, cols, parts, atoms = frac_ref.shape
    feats = jnp.dot(emb_ref[...], w_ref[...], preferred_element_type=jnp.float32).astype(jnp.bfloat16)
    for r in range(rows):
        for c in range(cols):
            at = (r * cols + c) * atoms
            out_ref[r, c, 0:atoms, :] = feats[at : at + atoms]
            f = frac_ref[r, c].astype(jnp.float32)
            f = jnp.concatenate([f, jnp.zeros((FRAC_ROWS - parts, atoms), jnp.float32)], axis=0)
            out_ref[r, c, atoms : atoms + FRAC_ROWS, :] = f.astype(jnp.bfloat16)


def pair_kernel(first, codes_ref, ext_ref, got_ref, mix_ref, after_ref, out_ref, near3, fields, basis, gathered):
    del after_ref
    rows, width, packed, channels = ext_ref.shape
    atoms = packed - FRAC_ROWS
    cols = width - 2
    npb = codes_ref.shape[-1]
    nrbf = mix_ref.shape[0]
    core = lax.rem(lax.axis_index("gx"), 2)
    above = core if first else 1 - core
    row = 1 - above

    @pl.when(above == 0)
    def _():
        near3[0:rows] = ext_ref[...]
        near3[rows] = got_ref[...]

    @pl.when(above == 1)
    def _():
        near3[0] = got_ref[...]
        near3[1 : rows + 1] = ext_ref[...]

    for r in range(rows + 1):
        for c in range(width):
            fields[r * width + c] = near3[r, c, atoms:packed, :].astype(jnp.float32)[0:8]

    order = lax.broadcasted_iota(jnp.int32, (nrbf, channels), 0).astype(jnp.float32) - nrbf // 2
    mix = mix_ref[...] * (jnp.exp(-order * order) * MSG_SCALE)
    bits = math.sqrt(math.log2(math.e))

    for c in range(cols):
        own = fields[width + c + 1]
        own = jnp.transpose(jnp.concatenate([own] * (LANES // 8), axis=0))
        own_x = jnp.broadcast_to(own[:, 0:1], (atoms, atoms))
        own_y = jnp.broadcast_to(own[:, 1:2], (atoms, atoms))
        own_z = jnp.broadcast_to(own[:, 2:3] * (HEIGHT / CELL), (atoms, atoms))
        slot = c % 2
        for p in range(npb):
            code = codes_ref[row, c, p]
            step_x, step_y = code // 3 - 1, code % 3 - 1
            near = fields[(1 + step_x) * width + c + 1 + step_y]
            dx = (near[0:1] + step_x.astype(jnp.float32)) - own_x
            dy = (near[1:2] + step_y.astype(jnp.float32)) - own_y
            dz = jnp.abs(near[2:3] * (HEIGHT / CELL) - own_z)
            dz = jnp.minimum(dz, HEIGHT / CELL - dz)
            s = jnp.minimum(dx * dx + dy * dy + dz * dz, 1.0)
            root = s * lax.rsqrt(jnp.maximum(s, 1e-30))
            z = root * (bits * (nrbf - 1)) - bits * (nrbf // 2)
            env = (1.0 - s) * horner(ENV_POLY, s)
            mid = env * env * jnp.exp2(-(z * z))
            up, down = jnp.exp2((2.0 * bits) * z), jnp.exp2((-2.0 * bits) * z)
            at = slice(p * atoms, (p + 1) * atoms)
            value = mid
            for q in range(nrbf // 2, nrbf):
                basis[slot, q * atoms : (q + 1) * atoms, at] = value.astype(jnp.bfloat16)
                value = value * up
            value = mid
            for q in range(nrbf // 2 - 1, -1, -1):
                value = value * down
                basis[slot, q * atoms : (q + 1) * atoms, at] = value.astype(jnp.bfloat16)
            gathered[slot, at, :] = near3[1 + step_x, c + 1 + step_y, 0:atoms, :]
        parts = jnp.dot(basis[slot], gathered[slot], preferred_element_type=jnp.float32)
        total = parts[0:atoms] * mix[0:1]
        for q in range(1, nrbf):
            total = total + parts[q * atoms : (q + 1) * atoms] * mix[q : q + 1]
        out_ref[c] = total


def field_part(scale, half_ref, weight_ref, w_ref, table_ref):
    w_t = jnp.transpose(w_ref[...].astype(jnp.float32)).astype(jnp.bfloat16)
    factors = lax.dot_general(w_t, half_ref[...], (((1,), (1,)), ((), ())), preferred_element_type=jnp.float32)
    factors = (factors * (weight_ref[...] * scale)).astype(jnp.bfloat16)
    return jnp.dot(factors, table_ref[...], preferred_element_type=jnp.float32)


def own_field_kernel(scale, half_ref, weight_ref, w_ref, table_ref, emb_ref, msg1_ref, msg2_ref, out_ref):
    cols, atoms, _ = msg1_ref.shape
    row1 = 1 - lax.rem(lax.axis_index("gx"), 2)
    total = field_part(scale, half_ref, weight_ref, w_ref, table_ref)
    for r in range(2):
        for c in range(cols):
            i = r * cols + c
            at = slice(i * atoms, (i + 1) * atoms)
            msg = jnp.where(row1 == r, msg1_ref[c], msg2_ref[c])
            out_ref[i] = emb_ref[at, :].astype(jnp.float32) + msg + jnp.transpose(total[:, at])


def other_field_kernel(scale, half_ref, weight_ref, w_ref, table_ref, part_ref, out_ref):
    cells, atoms, _ = out_ref.shape
    total = field_part(scale, half_ref, weight_ref, w_ref, table_ref)
    for i in range(cells):
        out_ref[i] = part_ref[i] + jnp.transpose(total[:, i * atoms : (i + 1) * atoms])


def vmem(count):
    return [pl.BlockSpec(memory_space=pltpu.VMEM)] * count


def shards(embed, frac, pair_blocks, w_in, rbf_mix, w_charge, k_index, k_weight):
    f32, bf16 = jnp.float32, jnp.bfloat16
    rows, cols, atoms, channels = embed.shape
    kvec = k_weight.shape[0]
    npb = pair_blocks.shape[-1]
    nrbf = rbf_mix.shape[0]
    size_x, size_y = lax.axis_size("gx"), lax.axis_size("gy")
    count = size_x * size_y
    cells = rows * cols
    width = cols + 2
    flat = embed.reshape(-1, channels)
    unread = [pl.BlockSpec(memory_space=pl.ANY)]

    def call(body, name, ins, outs, scratch=(), smem=0, after=None):
        specs = [pl.BlockSpec(memory_space=pltpu.SMEM)] * smem + vmem(len(ins) - smem)
        if after is not None:
            ins, specs = [*ins, after], specs + unread
        return pl.pallas_call(
            body,
            out_shape=[jax.ShapeDtypeStruct(*o) for o in outs],
            in_specs=specs,
            out_specs=vmem(len(outs)),
            scratch_shapes=[pltpu.VMEM(*s) for s in scratch],
            compiler_params=pltpu.CompilerParams(vmem_limit_bytes=32 * MIB),
            name=name,
        )(*ins)

    def exchange(values, mask_of):
        return lax.ppermute(values, ("gx", "gy"), [(i, i ^ mask_of(i)) for i in range(count)])

    acc_out, state_out = ((kvec, channels), f32), ((8, LANES), f32)
    send_out = ((kvec + TAIL, channels), bf16)
    table_out = ((kvec, cells * atoms), bf16)
    k16, x16 = ((16, kvec), f32), ((16, cells * atoms), f32)
    shape = (rows * size_x, cols * size_y)
    table_theirs, send = call(
        functools.partial(tables_kernel, True, *shape), "sent_half",
        [frac, k_index, flat], [table_out, send_out], [k16, x16, state_out], after=k_weight,
    )
    table_mine, acc, state = call(
        functools.partial(tables_kernel, False, *shape), "kept_half",
        [frac, k_index, flat], [table_out, acc_out, state_out], [k16, x16], after=table_theirs,
    )

    def merge(acc, state, got, after, last=False):
        outs = [((kvec, channels), bf16)] if last else [send_out, acc_out, state_out]
        return call(functools.partial(merge_kernel, last), "merge", [acc, state, got], outs, after=after)

    core_bit = size_y
    masks = [1 << b for b in range(count.bit_length() - 1) if 1 << b != core_bit]
    swapped = [masks[t ^ 1] if t ^ 1 < len(masks) else masks[t] for t in range(len(masks))]

    def cross(send, t):
        return exchange(send, lambda i: swapped[t] if i & core_bit else masks[t])

    send, acc, state = merge(acc, state, exchange(send, lambda i: core_bit), table_mine)

    got = cross(send, 0)
    (packed,) = call(
        feats_kernel, "feats", [frac, flat, w_in], [((rows, cols, atoms + FRAC_ROWS, channels), bf16)], after=state
    )
    if size_y == 2:
        edges = lax.ppermute(jnp.stack([packed[:, -1], packed[:, 0]], axis=1), "gy", [(0, 1), (1, 0)])
        west, east = edges[:, 0:1], edges[:, 1:2]
    else:
        west = lax.ppermute(packed[:, -1:], "gy", [(i, (i + 1) % size_y) for i in range(size_y)])
        east = lax.ppermute(packed[:, :1], "gy", [((i + 1) % size_y, i) for i in range(size_y)])
    send, acc, state = merge(acc, state, got, packed)

    got = cross(send, 1)
    ext = jnp.concatenate([west, packed, east], axis=1)
    core = lax.rem(lax.axis_index("gx"), 2)
    toward_1 = lax.dynamic_index_in_dim(ext, 1 - core, 0, keepdims=False)
    toward_2 = lax.dynamic_index_in_dim(ext, core, 0, keepdims=False)
    got_1 = lax.ppermute(toward_1, "gx", [(i, i ^ 1) for i in range(size_x)])
    got_2 = lax.ppermute(
        toward_2, "gx", [(i, (i - 1) % size_x if i % 2 == 0 else (i + 1) % size_x) for i in range(size_x)]
    )
    send, acc, state = merge(acc, state, got, ext)

    def pairs(first, got_row, after):
        (out,) = call(
            functools.partial(pair_kernel, first), "pairs",
            [pair_blocks, ext, got_row, rbf_mix], [((cols, atoms, channels), f32)],
            [
                ((rows + 1, width, atoms + FRAC_ROWS, channels), bf16),
                (((rows + 1) * width, 8, atoms), f32),
                ((2, nrbf * atoms, npb * atoms), bf16),
                ((2, npb * atoms, channels), bf16),
            ],
            smem=1, after=after,
        )
        return out

    messages = [None, None]
    for t in range(2, len(masks)):
        got = cross(send, t)
        after = state
        if t < 4:
            after = messages[t - 2] = pairs(t == 2, got_1 if t == 2 else got_2, state)
        if t < len(masks) - 1:
            send, acc, state = merge(acc, state, got, after)
    (mine,) = merge(acc, state, got, after, last=True)
    theirs = exchange(mine, lambda i: core_bit)

    scale = 1.0 / math.sqrt(cells * count * atoms * kvec)
    weight = k_weight.reshape(1, kvec)
    out = ((cells, atoms, channels), f32)
    (part,) = call(
        functools.partial(own_field_kernel, scale), "own_field",
        [mine, weight, w_charge, table_mine, flat, *messages], [out],
    )
    (updated,) = call(
        functools.partial(other_field_kernel, scale), "other_field",
        [theirs, weight, w_charge, table_theirs, part], [out],
    )
    return updated.reshape(embed.shape)


def solution(mesh):
    in_specs = (
        P("gx", "gy", None, None),
        P("gx", "gy", None, None),
        P("gx", "gy", None),
        P(),
        P(),
        P(),
        P(),
        P(),
    )
    out_specs = P("gx", "gy", None, None)
    return jax.shard_map(shards, mesh=mesh, in_specs=in_specs, out_specs=out_specs, check_vma=False)
```

time: 49.7 us -> 41.6 us (0.84)
  waiting for transfers between devices: 16.5 us -> 11.1 us
  starting transfers between devices: 12.9 us -> 9.68 us
  Pallas kernels: 17.4 us -> 17.9 us
    ppermute x6, starting transfers between devices: 11 us -> 7.04 us  [exchange(): lax.ppermute(values, ('gx', 'gy'), [(i, i ^ mask_of(i)) for i in range(co...]
    ppermute x1, waiting for transfers between devices: 4.38 us -> 1.54 us  [shards(): lax.ppermute(toward_2, 'gx', [(i, (i - 1) % size_x if i % 2 == 0 else (i...]
    ppermute x6, waiting for transfers between devices: 12.1 us -> 9.52 us  [exchange(): lax.ppermute(values, ('gx', 'gy'), [(i, i ^ mask_of(i)) for i in range(co...]
    ppermute x1, starting transfers between devices: 0.08 us -> 2.57 us  [shards(): lax.ppermute(jnp.stack([packed[:, -1], packed[:, 0]], axis=1), 'gy', [(0,...]
    ppermute x1, starting transfers between devices: 1.58 us -> 0.07 us  [shards(): got_1 = lax.ppermute(toward_1, 'gx', [(i, i ^ 1) for i in range(size_x)])]
    pallas_call x8 -> x12, Pallas kernels: 17.4 us -> 17.9 us  [call(): pl.pallas_call(body, out_shape=[jax.ShapeDtypeStruct(*o) for o in outs],...]
  transfers between devices with their start and end apart: 9 -> 9, of which waited for: 6 -> 4; matrix products, arithmetic and copies ran while one was open for 0% -> 0% of each run, Pallas kernels for 23% -> 31%
where the time goes in v1:
time: 41.6 us; the launch traced here: 41.4 us
  Pallas kernels  17.9 us (43%)
  waiting for transfers between devices  11.1 us (27%)
  starting transfers between devices  9.68 us (23%)
  local copies, waits for them, and re-layouts  2.46 us (6%)
    pallas_call x12, Pallas kernels, call(): pl.pallas_call(body, out_shape=[jax.ShapeDtypeStruct(*o) for o in outs],...  17.9 us
    ppermute x6, waiting for transfers between devices, exchange(): lax.ppermute(values, ('gx', 'gy'), [(i, i ^ mask_of(i)) for i in range(co...  9.52 us
    ppermute x6, starting transfers between devices, exchange(): lax.ppermute(values, ('gx', 'gy'), [(i, i ^ mask_of(i)) for i in range(co...  7.04 us
    ppermute x1, starting transfers between devices, shards(): lax.ppermute(jnp.stack([packed[:, -1], packed[:, 0]], axis=1), 'gy', [(0,...  2.57 us
    unnamed x17, local copies, waits for them, and re-layouts  2.39 us
    ppermute x1, waiting for transfers between devices, shards(): lax.ppermute(toward_2, 'gx', [(i, (i - 1) % size_x if i % 2 == 0 else (i...  1.54 us
  transfers between devices with their start and end apart: 9, of which 4 were waited for; matrix products, arithmetic and copies ran while one was open for 0% of the time, Pallas kernels for 31%

profile of v1, /device:TPU:0, one launch (start us, length us, event | category | flops | bytes accessed | tf_op | source)
XLA Modules:
  0.0 41.4 jit_solution(5786501841958476179)
XLA Ops:
  0.0 0.7 %copy.10.frac_ref = bf16[2,4,3,128]{3,2,1,0:T(4,128)(2,1)S(1)} copy(bf16[2,4,3,128]{3,1,2,0:T(4,128)(2,1)} %param.9) | data formatting | bytes 12288 | tf_op args[1]
  0.7 0.9 %copy-done = bf16[2,4,128,128]{3,2,1,0:T(8,128)(2,1)S(1)} copy-done((bf16[2,4,128,128]{3,2,1,0:T(8,128)(2,1)S(1)}, bf16[2,4,128,128]{3,2,1,0:T(8,128)(2,1)}, u32[]{:S(2)}) %copy-start) | copy-done | bytes 262168
  1.7 2.5 %sent_half.1 = (bf16[512,1024]{1,0:T(8,128)(2,1)S(1)}, bf16[544,128]{1,0:T(8,128)(2,1)S(1)}) custom-call(bf16[2,4,3,128]{3,2,1,0:T(4,128)(2,1)S(1)} %copy.10.frac_ref, s32[3,512]{1,0:T(4,128)S(1)} %copy-done.4, bf16[1024,128]{1,0:T(8,128)(2,1)S(1)} %bitcast.7, f32[512]{0:T(512)S(1)} %copy-done.5), custom_call_target="tpu_custom_call" | custom-call | tf_op jit(solution)/shard_map/sent_half/pallas_call | solution.py:256
  4.2 0.5 %collective-permute-start = (bf16[544,128]{1,0:T(8,128)(2,1)S(1)}, bf16[544,128]{1,0:T(8,128)(2,1)S(1)}, u32[]{:S(2)}, u32[]{:S(2)}) collective-permute-start(bf16[544,128]{1,0:T(8,128)(2,1)S(1)} %get-tuple-element.25), channel_id=1, source_target_pairs={{0,2},{1,3},{2,0},{3,1},{4,6},{5,7},{6,4},{7,5},{8,10},{9,11},{10,... | collective-permute-start | bytes 417800 | tf_op jit(solution)/shard_map/ppermute | solution.py:267
  4.7 2.5 %kept_half.1 = (bf16[512,1024]{1,0:T(8,128)(2,1)S(1)}, f32[512,128]{1,0:T(8,128)S(1)}, f32[8,128]{1,0:T(8,128)S(1)}) custom-call(bf16[2,4,3,128]{3,2,1,0:T(4,128)(2,1)S(1)} %copy.10.frac_ref, s32[3,512]{1,0:T(4,128)S(1)} %copy-done.4, bf16[1024,128]{1,0:T(8,128)(2,1)S(1)} %bitcast.8, bf16[512,1024]{1,0:T(8,128)(2,1)S(1)} %get-tuple-element.22.after_ref.table_ref), custom_call_target="tpu_custom_call" | custom-call | tf_op jit(solution)/shard_map/kept_half/pallas_call | solution.py:256
  7.2 0.0 copy-start.1
  7.2 0.0 copy-start.3
  7.3 0.4 %merge.5 = (bf16[544,128]{1,0:T(8,128)(2,1)S(1)}, f32[512,128]{1,0:T(8,128)S(1)}, f32[8,128]{1,0:T(8,128)S(1)}) custom-call(f32[512,128]{1,0:T(8,128)S(1)} %get-tuple-element.23.acc_ref, f32[8,128]{1,0:T(8,128)S(1)} %get-tuple-element.24.state_ref, bf16[544,128]{1,0:T(8,128)(2,1)S(1)} %collective-permute-done.got_ref, ...), custom_call_target="tpu_custom_call" | custom-call | tf_op jit(solution)/shard_map/merge/pallas_call | solution.py:256
  7.7 0.5 %copy-done.1 = bf16[2,4,128,128]{3,2,1,0:T(8,128)(2,1)S(1)} copy-done((bf16[2,4,128,128]{3,2,1,0:T(8,128)(2,1)S(1)}, bf16[2,4,128,128]{3,2,1,0:T(8,128)(2,1)}, u32[]{:S(2)}) %copy-start.1) | copy-done | bytes 262168
  8.2 0.2 feats.1.after_ref
  8.4 2.6 %collective-permute-start.3 = (bf16[2,2,144,128]{3,2,1,0:T(8,128)(2,1)S(1)}, bf16[2,2,144,128]{3,2,1,0:T(8,128)(2,1)S(1)}, u32[]{:S(2)}, u32[]{:S(2)}) collective-permute-start(bf16[2,2,144,128]{3,2,1,0:T(8,128)(2,1)S(1)} %pad_maximum_fusion.1), channel_id=1, source_target_pairs={{0,1},{1,0},{2,3},{3,2},{4,5},{5,4},{6,7},{7,6},{8,9},{9,8},{10,11... | collective-permute-start | bytes 442376 | tf_op jit(solution)/shard_map/ppermute | solution.py:301
  11.0 0.1 collective-permute-start.1
  11.1 5.9 %collective-permute-done.1.got_ref = bf16[544,128]{1,0:T(8,128)(2,1)S(1)} collective-permute-done((bf16[544,128]{1,0:T(8,128)(2,1)S(1)}, bf16[544,128]{1,0:T(8,128)(2,1)S(1)}, u32[]{:S(2)}, u32[]{:S(2)}) %collective-permute-start.1) | collective-permute-done | bytes 139296 | tf_op jit(solution)/shard_map/ppermute | solution.py:267
  17.0 0.4 %merge.6 = (bf16[544,128]{1,0:T(8,128)(2,1)S(1)}, f32[512,128]{1,0:T(8,128)S(1)}, f32[8,128]{1,0:T(8,128)S(1)}) custom-call(f32[512,128]{1,0:T(8,128)S(1)} %get-tuple-element.27.acc_ref, f32[8,128]{1,0:T(8,128)S(1)} %get-tuple-element.28.after_ref.state_ref, bf16[544,128]{1,0:T(8,128)(2,1)S(1)} %collective-permute-done.1.got_ref, ...), custom_call_target="tpu_custom_call" | custom-call | tf_op jit(solution)/shard_map/merge/pallas_call | solution.py:256
  17.5 1.8 %collective-permute-start.2 = (bf16[544,128]{1,0:T(8,128)(2,1)S(1)}, bf16[544,128]{1,0:T(8,128)(2,1)S(1)}, u32[]{:S(2)}, u32[]{:S(2)}) collective-permute-start(bf16[544,128]{1,0:T(8,128)(2,1)S(1)} %get-tuple-element.32), channel_id=1, source_target_pairs={{0,4},{1,5},{2,3},{3,2},{4,0},{5,1},{6,7},{7,6},{8,12},{9,13},{10,... | collective-permute-start | bytes 417800 | tf_op jit(solution)/shard_map/ppermute | solution.py:267
  19.3 0.1 pad_maximum_fusion.after_ref.ext_ref
  19.4 0.1 collective-permute-start.5
  19.5 3.1 %collective-permute-done.2.got_ref = bf16[544,128]{1,0:T(8,128)(2,1)S(1)} collective-permute-done((bf16[544,128]{1,0:T(8,128)(2,1)S(1)}, bf16[544,128]{1,0:T(8,128)(2,1)S(1)}, u32[]{:S(2)}, u32[]{:S(2)}) %collective-permute-start.2) | collective-permute-done | bytes 139296 | tf_op jit(solution)/shard_map/ppermute | solution.py:267
  22.6 0.4 %merge.7 = (bf16[544,128]{1,0:T(8,128)(2,1)S(1)}, f32[512,128]{1,0:T(8,128)S(1)}, f32[8,128]{1,0:T(8,128)S(1)}) custom-call(f32[512,128]{1,0:T(8,128)S(1)} %get-tuple-element.30.acc_ref, f32[8,128]{1,0:T(8,128)S(1)} %get-tuple-element.31.state_ref, bf16[544,128]{1,0:T(8,128)(2,1)S(1)} %collective-permute-done.2.got_ref, ...), custom_call_target="tpu_custom_call" | custom-call | tf_op jit(solution)/shard_map/merge/pallas_call | solution.py:256
  23.0 0.0 copy-start.6
  23.0 1.9 %collective-permute-start.4 = (bf16[544,128]{1,0:T(8,128)(2,1)S(1)}, bf16[544,128]{1,0:T(8,128)(2,1)S(1)}, u32[]{:S(2)}, u32[]{:S(2)}) collective-permute-start(bf16[544,128]{1,0:T(8,128)(2,1)S(1)} %get-tuple-element.35), channel_id=1, source_target_pairs={{0,8},{1,9},{2,18},{3,19},{4,12},{5,13},{6,22},{7,23},{8,0},{9,1},... | collective-permute-start | bytes 417800 | tf_op jit(solution)/shard_map/ppermute | solution.py:267
  25.0 4.1 %pairs.2.after_ref.msg1_ref = f32[4,128,128]{2,1,0:T(8,128)S(1)} custom-call(s32[2,4,5]{2,1,0:T(4,128)S(1)} %copy-done.6, bf16[2,6,144,128]{3,2,1,0:T(8,128)(2,1)S(1)} %pad_maximum_fusion.after_ref.ext_ref, bf16[6,144,128]{2,1,0:T(8,128)(2,1)S(1)} %collective-permute-done.5.got_ref, f32[8,128]{1,0:T(8,128)S(1)} %copy-done.7, ...), custom_call_target="tpu_custom_call" | custom-call | tf_op jit(solution)/shard_map/pairs/pallas_call | solution.py:256
  29.1 0.4 %merge.8 = (bf16[544,128]{1,0:T(8,128)(2,1)S(1)}, f32[512,128]{1,0:T(8,128)S(1)}, f32[8,128]{1,0:T(8,128)S(1)}) custom-call(f32[512,128]{1,0:T(8,128)S(1)} %get-tuple-element.33.acc_ref, f32[8,128]{1,0:T(8,128)S(1)} %get-tuple-element.34.after_ref.state_ref, bf16[544,128]{1,0:T(8,128)(2,1)S(1)} %collective-permute-done.4.got_ref, ...), custom_call_target="tpu_custom_call" | custom-call | tf_op jit(solution)/shard_map/merge/pallas_call | solution.py:256
  29.6 2.6 %collective-permute-start.6 = (bf16[544,128]{1,0:T(8,128)(2,1)S(1)}, bf16[544,128]{1,0:T(8,128)(2,1)S(1)}, u32[]{:S(2)}, u32[]{:S(2)}) collective-permute-start(bf16[544,128]{1,0:T(8,128)(2,1)S(1)} %get-tuple-element.38), channel_id=1, source_target_pairs={{0,16},{1,17},{2,10},{3,11},{4,20},{5,21},{6,14},{7,15},{8,24},{9,... | collective-permute-start | bytes 417800 | tf_op jit(solution)/shard_map/ppermute | solution.py:267
  32.2 1.5 %collective-permute-done.7.got_ref = bf16[6,144,128]{2,1,0:T(8,128)(2,1)S(1)} collective-permute-done((bf16[6,144,128]{2,1,0:T(8,128)(2,1)S(1)}, bf16[6,144,128]{2,1,0:T(8,128)(2,1)S(1)}, u32[]{:S(2)}, u32[]{:S(2)}) %collective-permute-start.7) | collective-permute-done | bytes 221216 | tf_op jit(solution)/shard_map/ppermute | solution.py:314
  33.8 4.3 %pairs.3.after_ref.msg2_ref = f32[4,128,128]{2,1,0:T(8,128)S(1)} custom-call(s32[2,4,5]{2,1,0:T(4,128)S(1)} %copy-done.6, bf16[2,6,144,128]{3,2,1,0:T(8,128)(2,1)S(1)} %pad_maximum_fusion.after_ref.ext_ref, bf16[6,144,128]{2,1,0:T(8,128)(2,1)S(1)} %collective-permute-done.7.got_ref, f32[8,128]{1,0:T(8,128)S(1)} %copy-done.7, ...), custom_call_target="tpu_custom_call" | custom-call | tf_op jit(solution)/shard_map/pairs/pallas_call | solution.py:256
  38.1 0.4 %merge.9.half_ref = bf16[512,128]{1,0:T(8,128)(2,1)S(1)} custom-call(f32[512,128]{1,0:T(8,128)S(1)} %get-tuple-element.36.acc_ref, f32[8,128]{1,0:T(8,128)S(1)} %get-tuple-element.37.after_ref.state_ref, bf16[544,128]{1,0:T(8,128)(2,1)S(1)} %collective-permute-done.6.got_ref, f32[4,128,128]{2,1,0:T(8,128)S(1)} %pairs.3.after_ref.msg2_ref), custom_call_target="tpu_custom_call" | custom-call | tf_op jit(solution)/shard_map/merge/pallas_call | solution.py:256
  38.6 0.1 collective-permute-start.8
  38.7 0.2 copy-done.2
  38.9 0.6 %own_field.1.part_ref = f32[8,128,128]{2,1,0:T(8,128)S(1)} custom-call(bf16[512,128]{1,0:T(8,128)(2,1)S(1)} %merge.9.half_ref, f32[1,512]{1,0:T(1,128)S(1)} %bitcast.11, bf16[128,128]{1,0:T(8,128)(2,1)S(1)} %copy-done.2, bf16[512,1024]{1,0:T(8,128)(2,1)S(1)} %get-tuple-element.26.after_ref.table_ref, bf16[1024,128]{1,0:T(8,128)(2,1)S(1)} %bitcast.10, ...), custom_call_target="tpu_custom_call" | custom-call | tf_op jit(solution)/shard_map/own_field/pallas_call | solution.py:256
  39.5 0.5 %collective-permute-done.8.half_ref = bf16[512,128]{1,0:T(8,128)(2,1)S(1)} collective-permute-done((bf16[512,128]{1,0:T(8,128)(2,1)S(1)}, bf16[512,128]{1,0:T(8,128)(2,1)S(1)}, u32[]{:S(2)}, u32[]{:S(2)}) %collective-permute-start.8) | collective-permute-done | bytes 131104 | tf_op jit(solution)/shard_map/ppermute | solution.py:267
  40.0 1.4 %other_field.1 = f32[8,128,128]{2,1,0:T(8,128)} custom-call(bf16[512,128]{1,0:T(8,128)(2,1)S(1)} %collective-permute-done.8.half_ref, f32[1,512]{1,0:T(1,128)S(1)} %bitcast.12, bf16[128,128]{1,0:T(8,128)(2,1)S(1)} %copy-done.2, bf16[512,1024]{1,0:T(8,128)(2,1)S(1)} %get-tuple-element.22.after_ref.table_ref, f32[8,128,128]{2,1,0:T(8,128)S(1)} %own_field.1.part_ref), custom_call_target="tpu_custom_call" | custom-call | tf_op jit(solution)/shard_map/other_field/pallas_call | solution.py:256
  (20 shorter events, 0.1 us)
Async XLA Ops:
  0.0 0.7 %copy-start.4 = (s32[3,512]{1,0:T(4,128)S(1)}, s32[3,512]{1,0:T(4,128)}, u32[]{:S(2)}) copy-start(s32[3,512]{1,0:T(4,128)} %kidx_ref.3) | copy-start | bytes 18436
  0.0 0.7 %copy-start.5 = (f32[512]{0:T(512)S(1)}, f32[512]{0:T(512)}, u32[]{:S(2)}) copy-start(f32[512]{0:T(512)} %after_ref.1) | copy-start | bytes 6148
  0.7 1.0 %copy-start = (bf16[2,4,128,128]{3,2,1,0:T(8,128)(2,1)S(1)}, bf16[2,4,128,128]{3,2,1,0:T(8,128)(2,1)}, u32[]{:S(2)}) copy-start(bf16[2,4,128,128]{3,2,1,0:T(8,128)(2,1)} %param.8) | copy-start | bytes 786436
  4.2 3.0 %collective-permute-start = (bf16[544,128]{1,0:T(8,128)(2,1)S(1)}, bf16[544,128]{1,0:T(8,128)(2,1)S(1)}, u32[]{:S(2)}, u32[]{:S(2)}) collective-permute-start(bf16[544,128]{1,0:T(8,128)(2,1)S(1)} %get-tuple-element.25), channel_id=1, source_target_pairs={{0,2},{1,3},{2,0},{3,1},{4,6},{5,7},{6,4},{7,5},{8,10},{9,11},{10,... | collective-permute-start | bytes 417800 | tf_op jit(solution)/shard_map/ppermute | solution.py:267
  7.2 1.0 %copy-start.1 = (bf16[2,4,128,128]{3,2,1,0:T(8,128)(2,1)S(1)}, bf16[2,4,128,128]{3,2,1,0:T(8,128)(2,1)}, u32[]{:S(2)}) copy-start(bf16[2,4,128,128]{3,2,1,0:T(8,128)(2,1)} %param.8) | copy-start | bytes 786436
  7.2 0.9 %copy-start.3 = (bf16[128,128]{1,0:T(8,128)(2,1)S(1)}, bf16[128,128]{1,0:T(8,128)(2,1)}, u32[]{:S(2)}) copy-start(bf16[128,128]{1,0:T(8,128)(2,1)} %w_ref.3) | copy-start | bytes 98308
  8.4 10.9 %collective-permute-start.3 = (bf16[2,2,144,128]{3,2,1,0:T(8,128)(2,1)S(1)}, bf16[2,2,144,128]{3,2,1,0:T(8,128)(2,1)S(1)}, u32[]{:S(2)}, u32[]{:S(2)}) collective-permute-start(bf16[2,2,144,128]{3,2,1,0:T(8,128)(2,1)S(1)} %pad_maximum_fusion.1), channel_id=1, source_target_pairs={{0,1},{1,0},{2,3},{3,2},{4,5},{5,4},{6,7},{7,6},{8,9},{9,8},{10,11... | collective-permute-start | bytes 442376 | tf_op jit(solution)/shard_map/ppermute | solution.py:301
  11.0 6.0 %collective-permute-start.1 = (bf16[544,128]{1,0:T(8,128)(2,1)S(1)}, bf16[544,128]{1,0:T(8,128)(2,1)S(1)}, u32[]{:S(2)}, u32[]{:S(2)}) collective-permute-start(bf16[544,128]{1,0:T(8,128)(2,1)S(1)} %get-tuple-element.29), channel_id=1, source_target_pairs={{0,1},{1,0},{2,6},{3,7},{4,5},{5,4},{6,2},{7,3},{8,9},{9,8},{10,14... | collective-permute-start | bytes 417800 | tf_op jit(solution)/shard_map/ppermute | solution.py:267
  17.5 5.1 %collective-permute-start.2 = (bf16[544,128]{1,0:T(8,128)(2,1)S(1)}, bf16[544,128]{1,0:T(8,128)(2,1)S(1)}, u32[]{:S(2)}, u32[]{:S(2)}) collective-permute-start(bf16[544,128]{1,0:T(8,128)(2,1)S(1)} %get-tuple-element.32), channel_id=1, source_target_pairs={{0,4},{1,5},{2,3},{3,2},{4,0},{5,1},{6,7},{7,6},{8,12},{9,13},{10,... | collective-permute-start | bytes 417800 | tf_op jit(solution)/shard_map/ppermute | solution.py:267
  19.4 5.5 %collective-permute-start.5 = (bf16[6,144,128]{2,1,0:T(8,128)(2,1)S(1)}, bf16[6,144,128]{2,1,0:T(8,128)(2,1)S(1)}, u32[]{:S(2)}, u32[]{:S(2)}) collective-permute-start(bf16[6,144,128]{2,1,0:T(8,128)(2,1)S(1)} %get-tuple-element.40), channel_id=1, source_target_pairs={{0,2},{2,0},{4,6},{6,4},{8,10},{10,8},{12,14},{14,12},{16,18},{18,... | collective-permute-start | bytes 663560 | tf_op jit(solution)/shard_map/ppermute | solution.py:313
  22.6 2.4 %copy-start.7 = (f32[8,128]{1,0:T(8,128)S(1)}, f32[8,128]{1,0:T(8,128)}, u32[]{:S(2)}) copy-start(f32[8,128]{1,0:T(8,128)} %mix_ref.3) | copy-start | bytes 12292
  23.0 1.9 %copy-start.6 = (s32[2,4,5]{2,1,0:T(4,128)S(1)}, s32[2,4,5]{2,1,0:T(4,128)}, u32[]{:S(2)}) copy-start(s32[2,4,5]{2,1,0:T(4,128)} %codes_ref.3) | copy-start | bytes 484
  23.0 6.1 %collective-permute-start.4 = (bf16[544,128]{1,0:T(8,128)(2,1)S(1)}, bf16[544,128]{1,0:T(8,128)(2,1)S(1)}, u32[]{:S(2)}, u32[]{:S(2)}) collective-permute-start(bf16[544,128]{1,0:T(8,128)(2,1)S(1)} %get-tuple-element.35), channel_id=1, source_target_pairs={{0,8},{1,9},{2,18},{3,19},{4,12},{5,13},{6,22},{7,23},{8,0},{9,1},... | collective-permute-start | bytes 417800 | tf_op jit(solution)/shard_map/ppermute | solution.py:267
  24.9 8.8 %collective-permute-start.7 = (bf16[6,144,128]{2,1,0:T(8,128)(2,1)S(1)}, bf16[6,144,128]{2,1,0:T(8,128)(2,1)S(1)}, u32[]{:S(2)}, u32[]{:S(2)}) collective-permute-start(bf16[6,144,128]{2,1,0:T(8,128)(2,1)S(1)} %get-tuple-element.39), channel_id=1, source_target_pairs={{0,30},{2,4},{4,2},{6,8},{8,6},{10,12},{12,10},{14,16},{16,14},{18... | collective-permute-start | bytes 663560 | tf_op jit(solution)/shard_map/ppermute | solution.py:314
  29.6 8.5 %collective-permute-start.6 = (bf16[544,128]{1,0:T(8,128)(2,1)S(1)}, bf16[544,128]{1,0:T(8,128)(2,1)S(1)}, u32[]{:S(2)}, u32[]{:S(2)}) collective-permute-start(bf16[544,128]{1,0:T(8,128)(2,1)S(1)} %get-tuple-element.38), channel_id=1, source_target_pairs={{0,16},{1,17},{2,10},{3,11},{4,20},{5,21},{6,14},{7,15},{8,24},{9,... | collective-permute-start | bytes 417800 | tf_op jit(solution)/shard_map/ppermute | solution.py:267
  38.1 0.8 %copy-start.2 = (bf16[128,128]{1,0:T(8,128)(2,1)S(1)}, bf16[128,128]{1,0:T(8,128)(2,1)}, u32[]{:S(2)}) copy-start(bf16[128,128]{1,0:T(8,128)(2,1)} %w_ref.5) | copy-start | bytes 98308
  38.6 1.4 %collective-permute-start.8 = (bf16[512,128]{1,0:T(8,128)(2,1)S(1)}, bf16[512,128]{1,0:T(8,128)(2,1)S(1)}, u32[]{:S(2)}, u32[]{:S(2)}) collective-permute-start(bf16[512,128]{1,0:T(8,128)(2,1)S(1)} %merge.9.half_ref), channel_id=1, source_target_pairs={{0,2},{1,3},{2,0},{3,1},{4,6},{5,7},{6,4},{7,5},{8,10},{9,11},{10,... | collective-permute-start | bytes 393224 | tf_op jit(solution)/shard_map/ppermute | solution.py:267

commit v2 on v1

--- a/solution.py
+++ b/solution.py
@@ -28,24 +28,34 @@
     return acc
 
 
+def pieces(x):
+    hi = x.astype(jnp.bfloat16).astype(jnp.float32)
+    rest = x - hi
+    mid = rest.astype(jnp.bfloat16).astype(jnp.float32)
+    return hi, mid, rest - mid
+
+
+def stack(rows, order):
+    row = lax.broadcasted_iota(jnp.int32, (16, LANES), 0)
+    out = jnp.zeros((16, LANES), jnp.float32)
+    for at, which in enumerate(order):
+        out = jnp.where(row == at, jnp.broadcast_to(rows[which], (16, LANES)), out)
+    return out.astype(jnp.bfloat16)
+
+
 def outer_row(column, row):
     return lax.dot_general(
-        jnp.broadcast_to(column, (8, LANES)),
-        jnp.broadcast_to(row, (8, LANES)) * 0.125,
-        (((0,), (0,)), ((), ())),
-        precision=lax.Precision.HIGHEST,
-        preferred_element_type=jnp.float32,
-    )
+        stack(column, (0, 0, 0, 1, 1, 2)), row, (((0,), (0,)), ((), ())), preferred_element_type=jnp.float32
+    )
+
+
+def row_stack(row):
+    return stack(pieces(row), (0, 1, 2, 0, 1, 0))
 
 
 def put_message(send_ref, half, state):
-    hi = state.astype(jnp.bfloat16).astype(jnp.float32)
-    rest = state - hi
-    mid = rest.astype(jnp.bfloat16).astype(jnp.float32)
-    low = rest - mid
-    send_ref[half : half + TAIL, :] = jnp.concatenate([hi, mid, low, jnp.zeros_like(hi)], axis=0).astype(
-        jnp.bfloat16
-    )
+    parts = [*pieces(state), jnp.zeros_like(state)]
+    send_ref[half : half + TAIL, :] = jnp.concatenate(parts, axis=0).astype(jnp.bfloat16)
 
 
 def tables_kernel(sent, nx, ny, frac_ref, kidx_ref, emb_ref, after_ref, *refs):
@@ -86,6 +96,7 @@
     mean = jnp.dot(ones, emb, preferred_element_type=jnp.float32)[0:1] * (1.0 / n)
     state_ref[...] = jnp.zeros_like(state_ref)
     state_ref[nb : nb + 1, :] = mean
+    mean = row_stack(mean)
     for b in range(nb):
         at = slice(b * LANES, (b + 1) * LANES)
         turns = lax.dot_general(kb[:, at], xb, (((0,), (0,)), ((), ())), preferred_element_type=jnp.float32)
@@ -95,7 +106,7 @@
         table_ref[at, :] = table
         count = lax.dot_general(ones, table, (((1,), (1,)), ((), ())), preferred_element_type=jnp.float32)
         state_ref[b : b + 1, :] = count[0:1]
-        centred = jnp.dot(table, emb, preferred_element_type=jnp.float32) - outer_row(count[0:1], mean)
+        centred = jnp.dot(table, emb, preferred_element_type=jnp.float32) - outer_row(pieces(count[0:1]), mean)
         if sent:
             send_ref[at, :] = centred.astype(jnp.bfloat16)
         else:
@@ -114,9 +125,11 @@
     weight = jnp.where(lax.broadcasted_iota(jnp.int32, (8, LANES), 0) < nb, 1.0, 0.5)
     state = (mine + theirs) * weight
     diff = (mine - theirs) * weight
+    split = pieces(diff)
+    means = row_stack(diff[nb : nb + 1])
     for b in range(nb):
         at = slice(b * LANES, (b + 1) * LANES)
-        part = outer_row(diff[b : b + 1], diff[nb : nb + 1])
+        part = outer_row([piece[b : b + 1] for piece in split], means)
         merged = acc_ref[at, :] + got_ref[at, :].astype(jnp.float32) + part
         if not last:
             outs[1][at, :] = merged
@@ -225,11 +238,17 @@
             out_ref[i] = emb_ref[at, :].astype(jnp.float32) + msg + jnp.transpose(total[:, at])
 
 
-def other_field_kernel(scale, half_ref, weight_ref, w_ref, table_ref, part_ref, out_ref):
-    cells, atoms, _ = out_ref.shape
+def other_field_kernel(scale, half_ref, weight_ref, w_ref, table_ref, part_ref, out_ref, done, sems):
+    cells, atoms, _ = done.shape
     total = field_part(scale, half_ref, weight_ref, w_ref, table_ref)
+    copies = []
     for i in range(cells):
-        out_ref[i] = part_ref[i] + jnp.transpose(total[:, i * atoms : (i + 1) * atoms])
+        done[i] = part_ref[i] + jnp.transpose(total[:, i * atoms : (i + 1) * atoms])
+        copy = pltpu.make_async_copy(done.at[i], out_ref.at[i], sems.at[i])
+        copy.start()
+        copies.append(copy)
+    for copy in copies:
+        copy.wait()
 
 
 def vmem(count):
@@ -249,7 +268,7 @@
     flat = embed.reshape(-1, channels)
     unread = [pl.BlockSpec(memory_space=pl.ANY)]
 
-    def call(body, name, ins, outs, scratch=(), smem=0, after=None):
+    def call(body, name, ins, outs, scratch=(), smem=0, after=None, us=1.0, out_space=pltpu.VMEM):
         specs = [pl.BlockSpec(memory_space=pltpu.SMEM)] * smem + vmem(len(ins) - smem)
         if after is not None:
             ins, specs = [*ins, after], specs + unread
@@ -257,9 +276,10 @@
             body,
             out_shape=[jax.ShapeDtypeStruct(*o) for o in outs],
             in_specs=specs,
-            out_specs=vmem(len(outs)),
-            scratch_shapes=[pltpu.VMEM(*s) for s in scratch],
+            out_specs=[pl.BlockSpec(memory_space=out_space)] * len(outs),
+            scratch_shapes=[pltpu.VMEM(*s) if isinstance(s, tuple) else s for s in scratch],
             compiler_params=pltpu.CompilerParams(vmem_limit_bytes=32 * MIB),
+            cost_estimate=pl.CostEstimate(flops=int(us * 1.15e9), bytes_accessed=0, transcendentals=0),
             name=name,
         )(*ins)
 
@@ -273,20 +293,22 @@
     shape = (rows * size_x, cols * size_y)
     table_theirs, send = call(
         functools.partial(tables_kernel, True, *shape), "sent_half",
-        [frac, k_index, flat], [table_out, send_out], [k16, x16, state_out], after=k_weight,
+        [frac, k_index, flat], [table_out, send_out], [k16, x16, state_out], after=k_weight, us=2.5,
     )
     table_mine, acc, state = call(
         functools.partial(tables_kernel, False, *shape), "kept_half",
-        [frac, k_index, flat], [table_out, acc_out, state_out], [k16, x16], after=table_theirs,
+        [frac, k_index, flat], [table_out, acc_out, state_out], [k16, x16], after=table_theirs, us=2.5,
     )
 
     def merge(acc, state, got, after, last=False):
         outs = [((kvec, channels), bf16)] if last else [send_out, acc_out, state_out]
-        return call(functools.partial(merge_kernel, last), "merge", [acc, state, got], outs, after=after)
+        return call(functools.partial(merge_kernel, last), "merge", [acc, state, got], outs, after=after, us=5.0)
 
     core_bit = size_y
-    masks = [1 << b for b in range(count.bit_length() - 1) if 1 << b != core_bit]
-    swapped = [masks[t ^ 1] if t ^ 1 < len(masks) else masks[t] for t in range(len(masks))]
+    along_y = [1 << b for b in range(size_y.bit_length() - 1)]
+    along_x = [core_bit << b for b in range(1, size_x.bit_length() - 1)]
+    masks = [along_x[1], *along_y, along_x[0], *along_x[2:]]
+    swapped = [along_x[0], *along_y, *along_x[2:], along_x[1]]
 
     def cross(send, t):
         return exchange(send, lambda i: swapped[t] if i & core_bit else masks[t])
@@ -326,7 +348,7 @@
                 ((2, nrbf * atoms, npb * atoms), bf16),
                 ((2, npb * atoms, channels), bf16),
             ],
-            smem=1, after=after,
+            smem=1, after=after, us=4.0,
         )
         return out
 
@@ -350,7 +372,8 @@
     )
     (updated,) = call(
         functools.partial(other_field_kernel, scale), "other_field",
-        [theirs, weight, w_charge, table_theirs, part], [out],
+        [theirs, weight, w_charge, table_theirs, part], [out], [out, pltpu.SemaphoreType.DMA((cells,))],
+        out_space=pl.ANY,
     )
     return updated.reshape(embed.shape)
 

time: 41.6 us -> 37.4 us (0.90)
  waiting for transfers between devices: 11.1 us -> 6.03 us
  starting transfers between devices: 9.68 us -> 12 us
  Pallas kernels: 17.9 us -> 16.5 us
    ppermute x6, waiting for transfers between devices: 9.52 us -> 4.62 us  [exchange(): lax.ppermute(values, ('gx', 'gy'), [(i, i ^ mask_of(i)) for i in range(co...]
    ppermute x1, starting transfers between devices: 0.01 us -> 2.73 us  [shards(): lax.ppermute(toward_2, 'gx', [(i, (i - 1) % size_x if i % 2 == 0 else (i...]
    ppermute x1, waiting for transfers between devices: 1.54 us -> 0.01 us  [shards(): lax.ppermute(toward_2, 'gx', [(i, (i - 1) % size_x if i % 2 == 0 else (i...]
    pallas_call x12, Pallas kernels: 17.9 us -> 16.5 us  [call(): pl.pallas_call(body, out_shape=[jax.ShapeDtypeStruct(*o) for o in outs],...]
    ppermute x1, waiting for transfers between devices: 0.01 us -> 1.31 us  [shards(): lax.ppermute(jnp.stack([packed[:, -1], packed[:, 0]], axis=1), 'gy', [(0,...]
    ppermute x1, starting transfers between devices: 2.57 us -> 1.56 us  [shards(): lax.ppermute(jnp.stack([packed[:, -1], packed[:, 0]], axis=1), 'gy', [(0,...]
    ppermute x6, starting transfers between devices: 7.04 us -> 7.72 us  [exchange(): lax.ppermute(values, ('gx', 'gy'), [(i, i ^ mask_of(i)) for i in range(co...]
  transfers between devices with their start and end apart: 9 -> 9, of which waited for: 4 -> 6; matrix products, arithmetic and copies ran while one was open for 0% -> 0% of each run, Pallas kernels for 31% -> 33%
where the time goes in v2:
time: 37.4 us; the launch traced here: 37.1 us
  Pallas kernels  16.5 us (44%)
  starting transfers between devices  12 us (32%)
  waiting for transfers between devices  6.03 us (16%)
  local copies, waits for them, and re-layouts  2.19 us (6%)
    pallas_call x12, Pallas kernels, call(): pl.pallas_call(body, out_shape=[jax.ShapeDtypeStruct(*o) for o in outs],...  16.5 us
    ppermute x6, starting transfers between devices, exchange(): lax.ppermute(values, ('gx', 'gy'), [(i, i ^ mask_of(i)) for i in range(co...  7.72 us
    ppermute x6, waiting for transfers between devices, exchange(): lax.ppermute(values, ('gx', 'gy'), [(i, i ^ mask_of(i)) for i in range(co...  4.62 us
    ppermute x1, starting transfers between devices, shards(): lax.ppermute(toward_2, 'gx', [(i, (i - 1) % size_x if i % 2 == 0 else (i...  2.73 us
    unnamed x17, local copies, waits for them, and re-layouts  2.13 us
    ppermute x1, starting transfers between devices, shards(): lax.ppermute(jnp.stack([packed[:, -1], packed[:, 0]], axis=1), 'gy', [(0,...  1.56 us
    ppermute x1, waiting for transfers between devices, shards(): lax.ppermute(jnp.stack([packed[:, -1], packed[:, 0]], axis=1), 'gy', [(0,...  1.31 us
  transfers between devices with their start and end apart: 9, of which 6 were waited for; matrix products, arithmetic and copies ran while one was open for 0% of the time, Pallas kernels for 33%

profile of v2, /device:TPU:0, one launch (start us, length us, event | category | flops | bytes accessed | tf_op | source)
XLA Modules:
  0.0 37.1 jit_solution(18183742030273115360)
XLA Ops:
  0.0 0.7 %copy.10.frac_ref = bf16[2,4,3,128]{3,2,1,0:T(4,128)(2,1)S(1)} copy(bf16[2,4,3,128]{3,1,2,0:T(4,128)(2,1)} %param.9) | data formatting | bytes 12288 | tf_op args[1]
  0.7 0.0 copy-start
  0.7 0.9 %copy-done = bf16[2,4,128,128]{3,2,1,0:T(8,128)(2,1)S(1)} copy-done((bf16[2,4,128,128]{3,2,1,0:T(8,128)(2,1)S(1)}, bf16[2,4,128,128]{3,2,1,0:T(8,128)(2,1)}, u32[]{:S(2)}) %copy-start) | copy-done | bytes 262168
  1.7 2.4 %sent_half.1 = (bf16[512,1024]{1,0:T(8,128)(2,1)S(1)}, bf16[544,128]{1,0:T(8,128)(2,1)S(1)}) custom-call(bf16[2,4,3,128]{3,2,1,0:T(4,128)(2,1)S(1)} %copy.10.frac_ref, s32[3,512]{1,0:T(4,128)S(1)} %copy-done.4, bf16[1024,128]{1,0:T(8,128)(2,1)S(1)} %bitcast.7, f32[512]{0:T(512)S(1)} %copy-done.7), custom_call_target="tpu_custom_call" | custom-call | flops 2875000064 | tf_op jit(solution)/shard_map/sent_half/pallas_call | solution.py:275
  4.1 0.5 %collective-permute-start = (bf16[544,128]{1,0:T(8,128)(2,1)S(1)}, bf16[544,128]{1,0:T(8,128)(2,1)S(1)}, u32[]{:S(2)}, u32[]{:S(2)}) collective-permute-start(bf16[544,128]{1,0:T(8,128)(2,1)S(1)} %get-tuple-element.25), channel_id=1, source_target_pairs={{0,2},{1,3},{2,0},{3,1},{4,6},{5,7},{6,4},{7,5},{8,10},{9,11},{10,... | collective-permute-start | bytes 417800 | tf_op jit(solution)/shard_map/ppermute | solution.py:287
  4.6 2.4 %kept_half.1 = (bf16[512,1024]{1,0:T(8,128)(2,1)S(1)}, f32[512,128]{1,0:T(8,128)S(1)}, f32[8,128]{1,0:T(8,128)S(1)}) custom-call(bf16[2,4,3,128]{3,2,1,0:T(4,128)(2,1)S(1)} %copy.10.frac_ref, s32[3,512]{1,0:T(4,128)S(1)} %copy-done.4, bf16[1024,128]{1,0:T(8,128)(2,1)S(1)} %bitcast.8, bf16[512,1024]{1,0:T(8,128)(2,1)S(1)} %get-tuple-element.22.after_ref.table_ref), custom_call_target="tpu_custom_call" | custom-call | flops 2875000064 | tf_op jit(solution)/shard_map/kept_half/pallas_call | solution.py:275
  7.0 0.0 copy-start.2
  7.0 0.2 merge.5
  7.2 2.7 %collective-permute-start.1 = (bf16[544,128]{1,0:T(8,128)(2,1)S(1)}, bf16[544,128]{1,0:T(8,128)(2,1)S(1)}, u32[]{:S(2)}, u32[]{:S(2)}) collective-permute-start(bf16[544,128]{1,0:T(8,128)(2,1)S(1)} %get-tuple-element.29), channel_id=1, source_target_pairs={{0,8},{1,9},{2,6},{3,7},{4,12},{5,13},{6,2},{7,3},{8,0},{9,1},{10,... | collective-permute-start | bytes 417800 | tf_op jit(solution)/shard_map/ppermute | solution.py:287
  9.9 0.2 feats.1.after_ref
  10.1 1.6 %collective-permute-start.3 = (bf16[2,2,144,128]{3,2,1,0:T(8,128)(2,1)S(1)}, bf16[2,2,144,128]{3,2,1,0:T(8,128)(2,1)S(1)}, u32[]{:S(2)}, u32[]{:S(2)}) collective-permute-start(bf16[2,2,144,128]{3,2,1,0:T(8,128)(2,1)S(1)} %pad_maximum_fusion.1), channel_id=1, source_target_pairs={{0,1},{1,0},{2,3},{3,2},{4,5},{5,4},{6,7},{7,6},{8,9},{9,8},{10,11... | collective-permute-start | bytes 442376 | tf_op jit(solution)/shard_map/ppermute | solution.py:323
  11.7 1.2 %collective-permute-done.1.got_ref = bf16[544,128]{1,0:T(8,128)(2,1)S(1)} collective-permute-done((bf16[544,128]{1,0:T(8,128)(2,1)S(1)}, bf16[544,128]{1,0:T(8,128)(2,1)S(1)}, u32[]{:S(2)}, u32[]{:S(2)}) %collective-permute-start.1) | collective-permute-done | bytes 139296 | tf_op jit(solution)/shard_map/ppermute | solution.py:287
  12.9 0.2 merge.6
  13.2 2.0 %collective-permute-start.2 = (bf16[544,128]{1,0:T(8,128)(2,1)S(1)}, bf16[544,128]{1,0:T(8,128)(2,1)S(1)}, u32[]{:S(2)}, u32[]{:S(2)}) collective-permute-start(bf16[544,128]{1,0:T(8,128)(2,1)S(1)} %get-tuple-element.32), channel_id=1, source_target_pairs={{0,1},{1,0},{2,3},{3,2},{4,5},{5,4},{6,7},{7,6},{8,9},{9,8},{10,11... | collective-permute-start | bytes 417800 | tf_op jit(solution)/shard_map/ppermute | solution.py:287
  15.2 1.3 %collective-permute-done.3 = bf16[2,2,144,128]{3,2,1,0:T(8,128)(2,1)S(1)} collective-permute-done((bf16[2,2,144,128]{3,2,1,0:T(8,128)(2,1)S(1)}, bf16[2,2,144,128]{3,2,1,0:T(8,128)(2,1)S(1)}, u32[]{:S(2)}, u32[]{:S(2)}) %collective-permute-start.3) | collective-permute-done | bytes 147488 | tf_op jit(solution)/shard_map/ppermute | solution.py:323
  16.5 0.1 pad_maximum_fusion.after_ref.ext_ref
  16.6 2.7 %collective-permute-start.7 = (bf16[6,144,128]{2,1,0:T(8,128)(2,1)S(1)}, bf16[6,144,128]{2,1,0:T(8,128)(2,1)S(1)}, u32[]{:S(2)}, u32[]{:S(2)}) collective-permute-start(bf16[6,144,128]{2,1,0:T(8,128)(2,1)S(1)} %get-tuple-element.39), channel_id=1, source_target_pairs={{0,30},{2,4},{4,2},{6,8},{8,6},{10,12},{12,10},{14,16},{16,14},{18... | collective-permute-start | bytes 663560 | tf_op jit(solution)/shard_map/ppermute | solution.py:336
  19.4 0.2 merge.7
  19.6 1.1 %collective-permute-start.4 = (bf16[544,128]{1,0:T(8,128)(2,1)S(1)}, bf16[544,128]{1,0:T(8,128)(2,1)S(1)}, u32[]{:S(2)}, u32[]{:S(2)}) collective-permute-start(bf16[544,128]{1,0:T(8,128)(2,1)S(1)} %get-tuple-element.35), channel_id=1, source_target_pairs={{0,4},{1,5},{2,18},{3,19},{4,0},{5,1},{6,22},{7,23},{8,12},{9,13},... | collective-permute-start | bytes 417800 | tf_op jit(solution)/shard_map/ppermute | solution.py:287
  20.7 0.1 collective-permute-done.5.got_ref
  20.8 4.1 %pairs.2.after_ref.msg1_ref = f32[4,128,128]{2,1,0:T(8,128)S(1)} custom-call(s32[2,4,5]{2,1,0:T(4,128)S(1)} %copy-done.5, bf16[2,6,144,128]{3,2,1,0:T(8,128)(2,1)S(1)} %pad_maximum_fusion.after_ref.ext_ref, bf16[6,144,128]{2,1,0:T(8,128)(2,1)S(1)} %collective-permute-done.5.got_ref, f32[8,128]{1,0:T(8,128)S(1)} %copy-done.6, ...), custom_call_target="tpu_custom_call" | custom-call | flops 4600000000 | tf_op jit(solution)/shard_map/pairs/pallas_call | solution.py:275
  25.0 1.3 %collective-permute-done.4.got_ref = bf16[544,128]{1,0:T(8,128)(2,1)S(1)} collective-permute-done((bf16[544,128]{1,0:T(8,128)(2,1)S(1)}, bf16[544,128]{1,0:T(8,128)(2,1)S(1)}, u32[]{:S(2)}, u32[]{:S(2)}) %collective-permute-start.4) | collective-permute-done | bytes 139296 | tf_op jit(solution)/shard_map/ppermute | solution.py:287
  26.3 0.2 merge.8
  26.5 1.4 %collective-permute-start.6 = (bf16[544,128]{1,0:T(8,128)(2,1)S(1)}, bf16[544,128]{1,0:T(8,128)(2,1)S(1)}, u32[]{:S(2)}, u32[]{:S(2)}) collective-permute-start(bf16[544,128]{1,0:T(8,128)(2,1)S(1)} %get-tuple-element.38), channel_id=1, source_target_pairs={{0,16},{1,17},{2,10},{3,11},{4,20},{5,21},{6,14},{7,15},{8,24},{9,... | collective-permute-start | bytes 417800 | tf_op jit(solution)/shard_map/ppermute | solution.py:287
  27.9 4.3 %pairs.3.after_ref.msg2_ref = f32[4,128,128]{2,1,0:T(8,128)S(1)} custom-call(s32[2,4,5]{2,1,0:T(4,128)S(1)} %copy-done.5, bf16[2,6,144,128]{3,2,1,0:T(8,128)(2,1)S(1)} %pad_maximum_fusion.after_ref.ext_ref, bf16[6,144,128]{2,1,0:T(8,128)(2,1)S(1)} %collective-permute-done.7.got_ref, f32[8,128]{1,0:T(8,128)S(1)} %copy-done.6, ...), custom_call_target="tpu_custom_call" | custom-call | flops 4600000000 | tf_op jit(solution)/shard_map/pairs/pallas_call | solution.py:275
  32.2 1.8 %collective-permute-done.6.got_ref = bf16[544,128]{1,0:T(8,128)(2,1)S(1)} collective-permute-done((bf16[544,128]{1,0:T(8,128)(2,1)S(1)}, bf16[544,128]{1,0:T(8,128)(2,1)S(1)}, u32[]{:S(2)}, u32[]{:S(2)}) %collective-permute-start.6) | collective-permute-done | bytes 139296 | tf_op jit(solution)/shard_map/ppermute | solution.py:287
  34.0 0.2 merge.9.half_ref
  34.2 0.1 collective-permute-start.8
  34.3 0.4 %copy-done.3 = bf16[128,128]{1,0:T(8,128)(2,1)S(1)} copy-done((bf16[128,128]{1,0:T(8,128)(2,1)S(1)}, bf16[128,128]{1,0:T(8,128)(2,1)}, u32[]{:S(2)}) %copy-start.3) | copy-done | bytes 32792
  34.8 0.6 %own_field.1.part_ref = f32[8,128,128]{2,1,0:T(8,128)S(1)} custom-call(bf16[512,128]{1,0:T(8,128)(2,1)S(1)} %merge.9.half_ref, f32[1,512]{1,0:T(1,128)S(1)} %bitcast.11, bf16[128,128]{1,0:T(8,128)(2,1)S(1)} %copy-done.3, bf16[512,1024]{1,0:T(8,128)(2,1)S(1)} %get-tuple-element.26.after_ref.table_ref, bf16[1024,128]{1,0:T(8,128)(2,1)S(1)} %bitcast.10, ...), custom_call_target="tpu_custom_call" | custom-call | flops 1150000000 | tf_op jit(solution)/shard_map/own_field/pallas_call | solution.py:275
  35.3 0.3 collective-permute-done.8.half_ref
  35.7 1.3 %other_field.1 = f32[8,128,128]{2,1,0:T(8,128)} custom-call(bf16[512,128]{1,0:T(8,128)(2,1)S(1)} %collective-permute-done.8.half_ref, f32[1,512]{1,0:T(1,128)S(1)} %bitcast.12, bf16[128,128]{1,0:T(8,128)(2,1)S(1)} %copy-done.3, bf16[512,1024]{1,0:T(8,128)(2,1)S(1)} %get-tuple-element.22.after_ref.table_ref, f32[8,128,128]{2,1,0:T(8,128)S(1)} %own_field.1.part_ref), custom_call_target="tpu_custom_call" | custom-call | flops 1150000000 | tf_op jit(solution)/shard_map/other_field/pallas_call | solution.py:275
  (20 shorter events, 0.1 us)
Async XLA Ops:
  0.0 0.7 %copy-start.7 = (f32[512]{0:T(512)S(1)}, f32[512]{0:T(512)}, u32[]{:S(2)}) copy-start(f32[512]{0:T(512)} %after_ref.1) | copy-start | bytes 6148
  0.0 0.7 %copy-start.4 = (s32[3,512]{1,0:T(4,128)S(1)}, s32[3,512]{1,0:T(4,128)}, u32[]{:S(2)}) copy-start(s32[3,512]{1,0:T(4,128)} %kidx_ref.3) | copy-start | bytes 18436
  0.7 1.0 %copy-start = (bf16[2,4,128,128]{3,2,1,0:T(8,128)(2,1)S(1)}, bf16[2,4,128,128]{3,2,1,0:T(8,128)(2,1)}, u32[]{:S(2)}) copy-start(bf16[2,4,128,128]{3,2,1,0:T(8,128)(2,1)} %param.8) | copy-start | bytes 786436
  1.7 2.9 %copy-start.1 = (bf16[2,4,128,128]{3,2,1,0:T(8,128)(2,1)S(1)}, bf16[2,4,128,128]{3,2,1,0:T(8,128)(2,1)}, u32[]{:S(2)}) copy-start(bf16[2,4,128,128]{3,2,1,0:T(8,128)(2,1)} %param.8) | copy-start | bytes 786436
  4.1 2.9 %collective-permute-start = (bf16[544,128]{1,0:T(8,128)(2,1)S(1)}, bf16[544,128]{1,0:T(8,128)(2,1)S(1)}, u32[]{:S(2)}, u32[]{:S(2)}) collective-permute-start(bf16[544,128]{1,0:T(8,128)(2,1)S(1)} %get-tuple-element.25), channel_id=1, source_target_pairs={{0,2},{1,3},{2,0},{3,1},{4,6},{5,7},{6,4},{7,5},{8,10},{9,11},{10,... | collective-permute-start | bytes 417800 | tf_op jit(solution)/shard_map/ppermute | solution.py:287
  7.0 2.9 %copy-start.2 = (bf16[128,128]{1,0:T(8,128)(2,1)S(1)}, bf16[128,128]{1,0:T(8,128)(2,1)}, u32[]{:S(2)}) copy-start(bf16[128,128]{1,0:T(8,128)(2,1)} %w_ref.3) | copy-start | bytes 98308
  7.2 5.7 %collective-permute-start.1 = (bf16[544,128]{1,0:T(8,128)(2,1)S(1)}, bf16[544,128]{1,0:T(8,128)(2,1)S(1)}, u32[]{:S(2)}, u32[]{:S(2)}) collective-permute-start(bf16[544,128]{1,0:T(8,128)(2,1)S(1)} %get-tuple-element.29), channel_id=1, source_target_pairs={{0,8},{1,9},{2,6},{3,7},{4,12},{5,13},{6,2},{7,3},{8,0},{9,1},{10,... | collective-permute-start | bytes 417800 | tf_op jit(solution)/shard_map/ppermute | solution.py:287
  10.1 6.3 %collective-permute-start.3 = (bf16[2,2,144,128]{3,2,1,0:T(8,128)(2,1)S(1)}, bf16[2,2,144,128]{3,2,1,0:T(8,128)(2,1)S(1)}, u32[]{:S(2)}, u32[]{:S(2)}) collective-permute-start(bf16[2,2,144,128]{3,2,1,0:T(8,128)(2,1)S(1)} %pad_maximum_fusion.1), channel_id=1, source_target_pairs={{0,1},{1,0},{2,3},{3,2},{4,5},{5,4},{6,7},{7,6},{8,9},{9,8},{10,11... | collective-permute-start | bytes 442376 | tf_op jit(solution)/shard_map/ppermute | solution.py:323
  13.2 6.2 %collective-permute-start.2 = (bf16[544,128]{1,0:T(8,128)(2,1)S(1)}, bf16[544,128]{1,0:T(8,128)(2,1)S(1)}, u32[]{:S(2)}, u32[]{:S(2)}) collective-permute-start(bf16[544,128]{1,0:T(8,128)(2,1)S(1)} %get-tuple-element.32), channel_id=1, source_target_pairs={{0,1},{1,0},{2,3},{3,2},{4,5},{5,4},{6,7},{7,6},{8,9},{9,8},{10,11... | collective-permute-start | bytes 417800 | tf_op jit(solution)/shard_map/ppermute | solution.py:287
  16.6 11.3 %collective-permute-start.7 = (bf16[6,144,128]{2,1,0:T(8,128)(2,1)S(1)}, bf16[6,144,128]{2,1,0:T(8,128)(2,1)S(1)}, u32[]{:S(2)}, u32[]{:S(2)}) collective-permute-start(bf16[6,144,128]{2,1,0:T(8,128)(2,1)S(1)} %get-tuple-element.39), channel_id=1, source_target_pairs={{0,30},{2,4},{4,2},{6,8},{8,6},{10,12},{12,10},{14,16},{16,14},{18... | collective-permute-start | bytes 663560 | tf_op jit(solution)/shard_map/ppermute | solution.py:336
  19.3 1.5 %collective-permute-start.5 = (bf16[6,144,128]{2,1,0:T(8,128)(2,1)S(1)}, bf16[6,144,128]{2,1,0:T(8,128)(2,1)S(1)}, u32[]{:S(2)}, u32[]{:S(2)}) collective-permute-start(bf16[6,144,128]{2,1,0:T(8,128)(2,1)S(1)} %get-tuple-element.40), channel_id=1, source_target_pairs={{0,2},{2,0},{4,6},{6,4},{8,10},{10,8},{12,14},{14,12},{16,18},{18,... | collective-permute-start | bytes 663560 | tf_op jit(solution)/shard_map/ppermute | solution.py:335
  19.3 1.5 %copy-start.5 = (s32[2,4,5]{2,1,0:T(4,128)S(1)}, s32[2,4,5]{2,1,0:T(4,128)}, u32[]{:S(2)}) copy-start(s32[2,4,5]{2,1,0:T(4,128)} %codes_ref.3) | copy-start | bytes 484
  19.3 1.5 %copy-start.6 = (f32[8,128]{1,0:T(8,128)S(1)}, f32[8,128]{1,0:T(8,128)}, u32[]{:S(2)}) copy-start(f32[8,128]{1,0:T(8,128)} %mix_ref.3) | copy-start | bytes 12292
  19.6 6.7 %collective-permute-start.4 = (bf16[544,128]{1,0:T(8,128)(2,1)S(1)}, bf16[544,128]{1,0:T(8,128)(2,1)S(1)}, u32[]{:S(2)}, u32[]{:S(2)}) collective-permute-start(bf16[544,128]{1,0:T(8,128)(2,1)S(1)} %get-tuple-element.35), channel_id=1, source_target_pairs={{0,4},{1,5},{2,18},{3,19},{4,0},{5,1},{6,22},{7,23},{8,12},{9,13},... | collective-permute-start | bytes 417800 | tf_op jit(solution)/shard_map/ppermute | solution.py:287
  26.5 7.5 %collective-permute-start.6 = (bf16[544,128]{1,0:T(8,128)(2,1)S(1)}, bf16[544,128]{1,0:T(8,128)(2,1)S(1)}, u32[]{:S(2)}, u32[]{:S(2)}) collective-permute-start(bf16[544,128]{1,0:T(8,128)(2,1)S(1)} %get-tuple-element.38), channel_id=1, source_target_pairs={{0,16},{1,17},{2,10},{3,11},{4,20},{5,21},{6,14},{7,15},{8,24},{9,... | collective-permute-start | bytes 417800 | tf_op jit(solution)/shard_map/ppermute | solution.py:287
  34.0 0.8 %copy-start.3 = (bf16[128,128]{1,0:T(8,128)(2,1)S(1)}, bf16[128,128]{1,0:T(8,128)(2,1)}, u32[]{:S(2)}) copy-start(bf16[128,128]{1,0:T(8,128)(2,1)} %w_ref.5) | copy-start | bytes 98308
  34.2 1.4 %collective-permute-start.8 = (bf16[512,128]{1,0:T(8,128)(2,1)S(1)}, bf16[512,128]{1,0:T(8,128)(2,1)S(1)}, u32[]{:S(2)}, u32[]{:S(2)}) collective-permute-start(bf16[512,128]{1,0:T(8,128)(2,1)S(1)} %merge.9.half_ref), channel_id=1, source_target_pairs={{0,2},{1,3},{2,0},{3,1},{4,6},{5,7},{6,4},{7,5},{8,10},{9,11},{10,... | collective-permute-start | bytes 393224 | tf_op jit(solution)/shard_map/ppermute | solution.py:287

commit v3 on v2

--- a/solution.py
+++ b/solution.py
@@ -58,61 +58,83 @@
     send_ref[half : half + TAIL, :] = jnp.concatenate(parts, axis=0).astype(jnp.bfloat16)
 
 
-def tables_kernel(sent, nx, ny, frac_ref, kidx_ref, emb_ref, after_ref, *refs):
-    del after_ref
-    if sent:
-        table_ref, send_ref, k16, x16, state_ref = refs
-    else:
-        table_ref, acc_ref, state_ref, k16, x16 = refs
-    rows, cols, _, atoms = frac_ref.shape
-    kvec = kidx_ref.shape[1]
+def half_table(half, k16, x16, sums_rhs, mean, state_ref, table_ref, store):
+    kvec = table_ref.shape[0]
     nb = kvec // LANES
-    n = rows * cols * atoms
-    me_x, me_y = lax.axis_index("gx"), lax.axis_index("gy")
-    core = lax.rem(me_x, 2)
-    half = 1 - core if sent else core
     offset = half.astype(jnp.float32) * 0.25
-    kf = kidx_ref[...].astype(jnp.float32)
-    k16[...] = jnp.zeros_like(k16)
-    x16[...] = jnp.zeros_like(x16)
-    k16[0:1, :] = kf[0:1] * (1.0 / nx)
-    k16[1:2, :] = kf[0:1] * (1.0 / nx)
-    k16[2:3, :] = kf[1:2] * (1.0 / ny)
-    k16[3:4, :] = kf[1:2] * (1.0 / ny)
-    k16[4:5, :] = kf[2:3]
-    for r in range(rows):
-        for c in range(cols):
-            at = slice((r * cols + c) * atoms, (r * cols + c + 1) * atoms)
-            f = frac_ref[r, c].astype(jnp.float32)
-            x16[0:1, at] = jnp.full((1, atoms), me_x * rows + r, jnp.int32).astype(jnp.float32)
-            x16[1:2, at] = f[0:1]
-            x16[2:3, at] = jnp.full((1, atoms), me_y * cols + c, jnp.int32).astype(jnp.float32)
-            x16[3:4, at] = f[1:2]
-            x16[4:5, at] = f[2:3]
-    kb = k16[...].astype(jnp.bfloat16)
-    xb = x16[...].astype(jnp.bfloat16)
-    emb = emb_ref[...]
-    ones = jnp.ones((16, n), jnp.bfloat16)
-    mean = jnp.dot(ones, emb, preferred_element_type=jnp.float32)[0:1] * (1.0 / n)
     state_ref[...] = jnp.zeros_like(state_ref)
     state_ref[nb : nb + 1, :] = mean
-    mean = row_stack(mean)
     for b in range(nb):
         at = slice(b * LANES, (b + 1) * LANES)
-        turns = lax.dot_general(kb[:, at], xb, (((0,), (0,)), ((), ())), preferred_element_type=jnp.float32)
+        turns = lax.dot_general(k16[:, at], x16, (((0,), (0,)), ((), ())), preferred_element_type=jnp.float32)
         turns = turns - offset
         turns = turns - jnp.round(turns)
         table = horner(COS_POLY, turns * turns).astype(jnp.bfloat16)
         table_ref[at, :] = table
-        count = lax.dot_general(ones, table, (((1,), (1,)), ((), ())), preferred_element_type=jnp.float32)
-        state_ref[b : b + 1, :] = count[0:1]
-        centred = jnp.dot(table, emb, preferred_element_type=jnp.float32) - outer_row(pieces(count[0:1]), mean)
-        if sent:
-            send_ref[at, :] = centred.astype(jnp.bfloat16)
-        else:
-            acc_ref[at, :] = centred
-    if sent:
-        put_message(send_ref, kvec, state_ref[...])
+        total = jnp.dot(table, sums_rhs(), preferred_element_type=jnp.float32)
+        count = total[:, LANES:]
+        state_ref[b : b + 1, :] = jnp.transpose(count)[0:1]
+        store(at, total[:, :LANES] - count * mean)
+
+
+def sent_kernel(
+    nx, ny, frac_hbm, kidx_hbm, emb_hbm, table_ref, send_ref, k16_ref, x16_ref, rhs, mean_ref, frac_ref,
+    kf32, xf32, state, kidx_ref, sems,
+):
+    rows, _, cols, atoms = frac_ref.shape
+    kvec = kidx_ref.shape[1]
+    n = rows * cols * atoms
+    fetches = [
+        pltpu.make_async_copy(kidx_hbm, kidx_ref, sems.at[0]),
+        pltpu.make_async_copy(frac_hbm, frac_ref, sems.at[1]),
+        pltpu.make_async_copy(emb_hbm, rhs.at[:, 0:LANES], sems.at[2]),
+    ]
+    for fetch in fetches:
+        fetch.start()
+    me_x, me_y = lax.axis_index("gx"), lax.axis_index("gy")
+    kf32[...] = jnp.zeros_like(kf32)
+    xf32[...] = jnp.zeros_like(xf32)
+    rhs[:, LANES:] = jnp.ones((n, LANES), jnp.bfloat16)
+    fetches[0].wait()
+    fetches[1].wait()
+    kf = kidx_ref[...].astype(jnp.float32)
+    kf32[0:1, :] = kf[0:1] * (1.0 / nx)
+    kf32[1:2, :] = kf[0:1] * (1.0 / nx)
+    kf32[2:3, :] = kf[1:2] * (1.0 / ny)
+    kf32[3:4, :] = kf[1:2] * (1.0 / ny)
+    kf32[4:5, :] = kf[2:3]
+    for r in range(rows):
+        f = [frac_ref[r, q].astype(jnp.float32) for q in range(3)]
+        for c in range(cols):
+            at = slice((r * cols + c) * atoms, (r * cols + c + 1) * atoms)
+            xf32[0:1, at] = jnp.full((1, atoms), me_x * rows + r, jnp.int32).astype(jnp.float32)
+            xf32[1:2, at] = f[0][c : c + 1]
+            xf32[2:3, at] = jnp.full((1, atoms), me_y * cols + c, jnp.int32).astype(jnp.float32)
+            xf32[3:4, at] = f[1][c : c + 1]
+            xf32[4:5, at] = f[2][c : c + 1]
+    k16 = kf32[...].astype(jnp.bfloat16)
+    x16 = xf32[...].astype(jnp.bfloat16)
+    k16_ref[...] = k16
+    x16_ref[...] = x16
+    fetches[2].wait()
+    mean = jnp.sum(rhs[:, 0:LANES].astype(jnp.float32), axis=0, keepdims=True) * (1.0 / n)
+    mean_ref[...] = jnp.broadcast_to(mean, mean_ref.shape)
+
+    def store(at, centred):
+        send_ref[at, :] = centred.astype(jnp.bfloat16)
+
+    half_table(1 - lax.rem(me_x, 2), k16, x16, lambda: rhs[...], mean, state, table_ref, store)
+    put_message(send_ref, kvec, state[...])
+
+
+def kept_kernel(k16_ref, x16_ref, rhs_ref, mean_ref, table_ref, acc_ref, state_ref):
+    def store(at, centred):
+        acc_ref[at, :] = centred
+
+    core = lax.rem(lax.axis_index("gx"), 2)
+    half_table(
+        core, k16_ref[...], x16_ref[...], lambda: rhs_ref[...], mean_ref[0:1], state_ref, table_ref, store
+    )
 
 
 def merge_kernel(last, acc_ref, state_ref, got_ref, after_ref, *outs):
@@ -139,17 +161,22 @@
         put_message(outs[0], half, state)
 
 
-def feats_kernel(frac_ref, emb_ref, w_ref, after_ref, out_ref):
+def feats_kernel(scale, frac_ref, emb_ref, w_ref, charge_ref, weight_ref, after_ref, out_ref, charge_t_ref, scaled_ref):
     del after_ref
-    rows, cols, parts, atoms = frac_ref.shape
-    feats = jnp.dot(emb_ref[...], w_ref[...], preferred_element_type=jnp.float32).astype(jnp.bfloat16)
+    rows, parts, cols, atoms = frac_ref.shape
+    feats = jnp.dot(emb_ref[:, 0:LANES], w_ref[...], preferred_element_type=jnp.float32).astype(jnp.bfloat16)
+    row = lax.broadcasted_iota(jnp.int32, (FRAC_ROWS, atoms), 0)
     for r in range(rows):
+        f = [frac_ref[r, q].astype(jnp.float32) for q in range(parts)]
         for c in range(cols):
             at = (r * cols + c) * atoms
             out_ref[r, c, 0:atoms, :] = feats[at : at + atoms]
-            f = frac_ref[r, c].astype(jnp.float32)
-            f = jnp.concatenate([f, jnp.zeros((FRAC_ROWS - parts, atoms), jnp.float32)], axis=0)
-            out_ref[r, c, atoms : atoms + FRAC_ROWS, :] = f.astype(jnp.bfloat16)
+            packed = jnp.zeros((FRAC_ROWS, atoms), jnp.float32)
+            for q in range(parts):
+                packed = jnp.where(row == q, jnp.broadcast_to(f[q][c : c + 1], (FRAC_ROWS, atoms)), packed)
+            out_ref[r, c, atoms : atoms + FRAC_ROWS, :] = packed.astype(jnp.bfloat16)
+    charge_t_ref[...] = jnp.transpose(charge_ref[...].astype(jnp.float32)).astype(jnp.bfloat16)
+    scaled_ref[...] = weight_ref[...] * scale
 
 
 def pair_kernel(first, codes_ref, ext_ref, got_ref, mix_ref, after_ref, out_ref, near3, fields, basis, gathered):
@@ -219,28 +246,29 @@
         out_ref[c] = total
 
 
-def field_part(scale, half_ref, weight_ref, w_ref, table_ref):
-    w_t = jnp.transpose(w_ref[...].astype(jnp.float32)).astype(jnp.bfloat16)
-    factors = lax.dot_general(w_t, half_ref[...], (((1,), (1,)), ((), ())), preferred_element_type=jnp.float32)
-    factors = (factors * (weight_ref[...] * scale)).astype(jnp.bfloat16)
+def field_part(half_ref, weight_ref, charge_t_ref, table_ref):
+    factors = lax.dot_general(
+        charge_t_ref[...], half_ref[...], (((1,), (1,)), ((), ())), preferred_element_type=jnp.float32
+    )
+    factors = (factors * weight_ref[...]).astype(jnp.bfloat16)
     return jnp.dot(factors, table_ref[...], preferred_element_type=jnp.float32)
 
 
-def own_field_kernel(scale, half_ref, weight_ref, w_ref, table_ref, emb_ref, msg1_ref, msg2_ref, out_ref):
+def own_field_kernel(half_ref, weight_ref, charge_t_ref, table_ref, emb_ref, msg1_ref, msg2_ref, out_ref):
     cols, atoms, _ = msg1_ref.shape
     row1 = 1 - lax.rem(lax.axis_index("gx"), 2)
-    total = field_part(scale, half_ref, weight_ref, w_ref, table_ref)
+    total = field_part(half_ref, weight_ref, charge_t_ref, table_ref)
     for r in range(2):
         for c in range(cols):
             i = r * cols + c
             at = slice(i * atoms, (i + 1) * atoms)
             msg = jnp.where(row1 == r, msg1_ref[c], msg2_ref[c])
-            out_ref[i] = emb_ref[at, :].astype(jnp.float32) + msg + jnp.transpose(total[:, at])
-
-
-def other_field_kernel(scale, half_ref, weight_ref, w_ref, table_ref, part_ref, out_ref, done, sems):
+            out_ref[i] = emb_ref[at, 0:LANES].astype(jnp.float32) + msg + jnp.transpose(total[:, at])
+
+
+def other_field_kernel(half_ref, weight_ref, charge_t_ref, table_ref, part_ref, out_ref, done, sems):
     cells, atoms, _ = done.shape
-    total = field_part(scale, half_ref, weight_ref, w_ref, table_ref)
+    total = field_part(half_ref, weight_ref, charge_t_ref, table_ref)
     copies = []
     for i in range(cells):
         done[i] = part_ref[i] + jnp.transpose(total[:, i * atoms : (i + 1) * atoms])
@@ -249,6 +277,10 @@
         copies.append(copy)
     for copy in copies:
         copy.wait()
+
+
+def in_hbm(x):
+    return pltpu.with_memory_space_constraint(x, pltpu.HBM)
 
 
 def vmem(count):
@@ -265,11 +297,11 @@
     count = size_x * size_y
     cells = rows * cols
     width = cols + 2
-    flat = embed.reshape(-1, channels)
     unread = [pl.BlockSpec(memory_space=pl.ANY)]
 
-    def call(body, name, ins, outs, scratch=(), smem=0, after=None, us=1.0, out_space=pltpu.VMEM):
-        specs = [pl.BlockSpec(memory_space=pltpu.SMEM)] * smem + vmem(len(ins) - smem)
+    def call(body, name, ins, outs, scratch=(), smem=0, after=None, us=1.0, out_space=pltpu.VMEM, hbm=0):
+        specs = [pl.BlockSpec(memory_space=pltpu.SMEM)] * smem + vmem(len(ins) - smem - hbm)
+        specs += [pl.BlockSpec(memory_space=pltpu.HBM)] * hbm
         if after is not None:
             ins, specs = [*ins, after], specs + unread
         return pl.pallas_call(
@@ -289,16 +321,17 @@
     acc_out, state_out = ((kvec, channels), f32), ((8, LANES), f32)
     send_out = ((kvec + TAIL, channels), bf16)
     table_out = ((kvec, cells * atoms), bf16)
-    k16, x16 = ((16, kvec), f32), ((16, cells * atoms), f32)
-    shape = (rows * size_x, cols * size_y)
-    table_theirs, send = call(
-        functools.partial(tables_kernel, True, *shape), "sent_half",
-        [frac, k_index, flat], [table_out, send_out], [k16, x16, state_out], after=k_weight, us=2.5,
-    )
-    table_mine, acc, state = call(
-        functools.partial(tables_kernel, False, *shape), "kept_half",
-        [frac, k_index, flat], [table_out, acc_out, state_out], [k16, x16], after=table_theirs, us=2.5,
-    )
+    k16, x16 = (16, kvec), (16, cells * atoms)
+    table_theirs, send, *operands, parts = call(
+        functools.partial(sent_kernel, rows * size_x, cols * size_y), "sent_half",
+        [in_hbm(jnp.transpose(frac, (0, 2, 1, 3))), in_hbm(k_index), in_hbm(embed.reshape(-1, channels))],
+        [table_out, send_out, (k16, bf16), (x16, bf16), ((cells * atoms, 2 * LANES), bf16), state_out,
+         ((rows, frac.shape[2], cols, atoms), bf16)],
+        [(k16, f32), (x16, f32), state_out, (k_index.shape, jnp.int32), pltpu.SemaphoreType.DMA((3,))],
+        hbm=3, us=2.5,
+    )
+    embedded = operands[2]
+    table_mine, acc, state = call(kept_kernel, "kept_half", operands, [table_out, acc_out, state_out], us=2.5)
 
     def merge(acc, state, got, after, last=False):
         outs = [((kvec, channels), bf16)] if last else [send_out, acc_out, state_out]
@@ -307,8 +340,8 @@
     core_bit = size_y
     along_y = [1 << b for b in range(size_y.bit_length() - 1)]
     along_x = [core_bit << b for b in range(1, size_x.bit_length() - 1)]
-    masks = [along_x[1], *along_y, along_x[0], *along_x[2:]]
-    swapped = [along_x[0], *along_y, *along_x[2:], along_x[1]]
+    masks = [along_x[1], along_x[0], *along_y, *along_x[2:]]
+    swapped = [along_x[0], *along_x[2:], *along_y, along_x[1]]
 
     def cross(send, t):
         return exchange(send, lambda i: swapped[t] if i & core_bit else masks[t])
@@ -316,8 +349,10 @@
     send, acc, state = merge(acc, state, exchange(send, lambda i: core_bit), table_mine)
 
     got = cross(send, 0)
-    (packed,) = call(
-        feats_kernel, "feats", [frac, flat, w_in], [((rows, cols, atoms + FRAC_ROWS, channels), bf16)], after=state
+    packed, charge_t, weight = call(
+        functools.partial(feats_kernel, 1.0 / math.sqrt(cells * count * atoms * kvec)), "feats",
+        [parts, embedded, w_in, w_charge, k_weight.reshape(1, kvec)],
+        [((rows, cols, atoms + FRAC_ROWS, channels), bf16), (w_charge.shape, bf16), ((1, kvec), f32)], after=state,
     )
     if size_y == 2:
         edges = lax.ppermute(jnp.stack([packed[:, -1], packed[:, 0]], axis=1), "gy", [(0, 1), (1, 0)])
@@ -363,17 +398,13 @@
     (mine,) = merge(acc, state, got, after, last=True)
     theirs = exchange(mine, lambda i: core_bit)
 
-    scale = 1.0 / math.sqrt(cells * count * atoms * kvec)
-    weight = k_weight.reshape(1, kvec)
     out = ((cells, atoms, channels), f32)
     (part,) = call(
-        functools.partial(own_field_kernel, scale), "own_field",
-        [mine, weight, w_charge, table_mine, flat, *messages], [out],
+        own_field_kernel, "own_field", [mine, weight, charge_t, table_mine, embedded, *messages], [out]
     )
     (updated,) = call(
-        functools.partial(other_field_kernel, scale), "other_field",
-        [theirs, weight, w_charge, table_theirs, part], [out], [out, pltpu.SemaphoreType.DMA((cells,))],
-        out_space=pl.ANY,
+        other_field_kernel, "other_field", [theirs, weight, charge_t, table_theirs, part], [out],
+        [out, pltpu.SemaphoreType.DMA((cells,))], out_space=pl.ANY,
     )
     return updated.reshape(embed.shape)
 

time: 37.4 us -> 34.3 us (0.917)
  local copies, waits for them, and re-layouts: 2.19 us -> 0.76 us
  Pallas kernels: 16.5 us -> 15.4 us
  waiting for transfers between devices: 6.03 us -> 5.32 us
  starting transfers between devices: 12 us -> 12.4 us
    unnamed x17 -> x10, local copies, waits for them, and re-layouts: 2.13 us -> 0.69 us
    pallas_call x12, Pallas kernels: 16.5 us -> 15.4 us  [call(): pl.pallas_call(body, out_shape=[jax.ShapeDtypeStruct(*o) for o in outs],...]
    ppermute x6, waiting for transfers between devices: 4.62 us -> 3.71 us  [exchange(): lax.ppermute(values, ('gx', 'gy'), [(i, i ^ mask_of(i)) for i in range(co...]
    ppermute x6, starting transfers between devices: 7.72 us -> 8.22 us  [exchange(): lax.ppermute(values, ('gx', 'gy'), [(i, i ^ mask_of(i)) for i in range(co...]
  transfers between devices with their start and end apart: 9 -> 9, of which waited for: 6 -> 5; matrix products, arithmetic and copies ran while one was open for 0% -> 0% of each run, Pallas kernels for 33% -> 33%
where the time goes in v3:
time: 34.3 us; the launch traced here: 34.1 us
  Pallas kernels  15.4 us (45%)
  starting transfers between devices  12.4 us (36%)
  waiting for transfers between devices  5.32 us (16%)
  local copies, waits for them, and re-layouts  0.76 us (2%)
    pallas_call x12, Pallas kernels, call(): pl.pallas_call(body, out_shape=[jax.ShapeDtypeStruct(*o) for o in outs],...  15.4 us
    ppermute x6, starting transfers between devices, exchange(): lax.ppermute(values, ('gx', 'gy'), [(i, i ^ mask_of(i)) for i in range(co...  8.22 us
    ppermute x6, waiting for transfers between devices, exchange(): lax.ppermute(values, ('gx', 'gy'), [(i, i ^ mask_of(i)) for i in range(co...  3.71 us
    ppermute x1, starting transfers between devices, shards(): lax.ppermute(toward_2, 'gx', [(i, (i - 1) % size_x if i % 2 == 0 else (i...  2.67 us
    ppermute x1, waiting for transfers between devices, shards(): lax.ppermute(jnp.stack([packed[:, -1], packed[:, 0]], axis=1), 'gy', [(0,...  1.6 us
    ppermute x1, starting transfers between devices, shards(): lax.ppermute(jnp.stack([packed[:, -1], packed[:, 0]], axis=1), 'gy', [(0,...  1.55 us
    unnamed x10, local copies, waits for them, and re-layouts  0.69 us
  transfers between devices with their start and end apart: 9, of which 5 were waited for; matrix products, arithmetic and copies ran while one was open for 0% of the time, Pallas kernels for 33%

profile of v3, /device:TPU:0, one launch (start us, length us, event | category | flops | bytes accessed | tf_op | source)
XLA Modules:
  0.0 34.1 jit_solution(2050414661593500398)
XLA Ops:
  0.0 2.4 %sent_half.1 = (bf16[512,1024]{1,0:T(8,128)(2,1)S(1)}, bf16[544,128]{1,0:T(8,128)(2,1)S(1)}, bf16[16,512]{1,0:T(8,128)(2,1)S(1)}, bf16[16,1024]{1,0:T(8,128)(2,1...) custom-call(bf16[2,3,4,128]{3,2,1,0:T(4,128)(2,1)} %bitcast.10, ...), custom_call_target="tpu_custom_call" | custom-call | flops 2875000064 | tf_op jit(solution)/shard_map/sent_half/pallas_call | solution.py:307
  2.4 0.5 %collective-permute-start = (bf16[544,128]{1,0:T(8,128)(2,1)S(1)}, bf16[544,128]{1,0:T(8,128)(2,1)S(1)}, u32[]{:S(2)}, u32[]{:S(2)}) collective-permute-start(bf16[544,128]{1,0:T(8,128)(2,1)S(1)} %get-tuple-element.36), channel_id=1, source_target_pairs={{0,2},{1,3},{2,0},{3,1},{4,6},{5,7},{6,4},{7,5},{8,10},{9,11},{10,... | collective-permute-start | bytes 417800 | tf_op jit(solution)/shard_map/ppermute | solution.py:319
  2.9 1.4 %kept_half.1 = (bf16[512,1024]{1,0:T(8,128)(2,1)S(1)}, f32[512,128]{1,0:T(8,128)S(1)}, f32[8,128]{1,0:T(8,128)S(1)}) custom-call(bf16[16,512]{1,0:T(8,128)(2,1)S(1)} %get-tuple-element.30.k16_ref, bf16[16,1024]{1,0:T(8,128)(2,1)S(1)} %get-tuple-element.31.x16_ref, bf16[1024,256]{1,0:T(8,128)(2,1)S(1)} %get-tuple-element.32.rhs_ref.emb_ref, ...), custom_call_target="tpu_custom_call" | custom-call | flops 2875000064 | tf_op jit(solution)/shard_map/kept_half/pallas_call | solution.py:307
  4.3 0.0 collective-permute-done.got_ref
  4.3 0.2 merge.5
  4.6 2.7 %collective-permute-start.1 = (bf16[544,128]{1,0:T(8,128)(2,1)S(1)}, bf16[544,128]{1,0:T(8,128)(2,1)S(1)}, u32[]{:S(2)}, u32[]{:S(2)}) collective-permute-start(bf16[544,128]{1,0:T(8,128)(2,1)S(1)} %get-tuple-element.40), channel_id=1, source_target_pairs={{0,8},{1,9},{2,6},{3,7},{4,12},{5,13},{6,2},{7,3},{8,0},{9,1},{10,... | collective-permute-start | bytes 417800 | tf_op jit(solution)/shard_map/ppermute | solution.py:319
  7.3 0.7 %copy-done.4 = f32[512]{0:T(512)S(1)} copy-done((f32[512]{0:T(512)S(1)}, f32[512]{0:T(512)}, u32[]{:S(2)}) %copy-start.4) | copy-done | bytes 2072
  7.9 0.2 feats.1
  8.2 1.6 %collective-permute-start.3 = (bf16[2,2,144,128]{3,2,1,0:T(8,128)(2,1)S(1)}, bf16[2,2,144,128]{3,2,1,0:T(8,128)(2,1)S(1)}, u32[]{:S(2)}, u32[]{:S(2)}) collective-permute-start(bf16[2,2,144,128]{3,2,1,0:T(8,128)(2,1)S(1)} %pad_maximum_fusion.1), channel_id=1, source_target_pairs={{0,1},{1,0},{2,3},{3,2},{4,5},{5,4},{6,7},{7,6},{8,9},{9,8},{10,11... | collective-permute-start | bytes 442376 | tf_op jit(solution)/shard_map/ppermute | solution.py:358
  9.8 0.5 %collective-permute-done.1.got_ref = bf16[544,128]{1,0:T(8,128)(2,1)S(1)} collective-permute-done((bf16[544,128]{1,0:T(8,128)(2,1)S(1)}, bf16[544,128]{1,0:T(8,128)(2,1)S(1)}, u32[]{:S(2)}, u32[]{:S(2)}) %collective-permute-start.1) | collective-permute-done | bytes 139296 | tf_op jit(solution)/shard_map/ppermute | solution.py:319
  10.3 0.2 merge.6
  10.5 2.0 %collective-permute-start.2 = (bf16[544,128]{1,0:T(8,128)(2,1)S(1)}, bf16[544,128]{1,0:T(8,128)(2,1)S(1)}, u32[]{:S(2)}, u32[]{:S(2)}) collective-permute-start(bf16[544,128]{1,0:T(8,128)(2,1)S(1)} %get-tuple-element.45), channel_id=1, source_target_pairs={{0,4},{1,5},{2,18},{3,19},{4,0},{5,1},{6,22},{7,23},{8,12},{9,13},... | collective-permute-start | bytes 417800 | tf_op jit(solution)/shard_map/ppermute | solution.py:319
  12.6 1.6 %collective-permute-done.3 = bf16[2,2,144,128]{3,2,1,0:T(8,128)(2,1)S(1)} collective-permute-done((bf16[2,2,144,128]{3,2,1,0:T(8,128)(2,1)S(1)}, bf16[2,2,144,128]{3,2,1,0:T(8,128)(2,1)S(1)}, u32[]{:S(2)}, u32[]{:S(2)}) %collective-permute-start.3) | collective-permute-done | bytes 147488 | tf_op jit(solution)/shard_map/ppermute | solution.py:358
  14.2 0.1 pad_maximum_fusion.after_ref.ext_ref
  14.3 2.7 %collective-permute-start.7 = (bf16[6,144,128]{2,1,0:T(8,128)(2,1)S(1)}, bf16[6,144,128]{2,1,0:T(8,128)(2,1)S(1)}, u32[]{:S(2)}, u32[]{:S(2)}) collective-permute-start(bf16[6,144,128]{2,1,0:T(8,128)(2,1)S(1)} %get-tuple-element.55), channel_id=1, source_target_pairs={{0,30},{2,4},{4,2},{6,8},{8,6},{10,12},{12,10},{14,16},{16,14},{18... | collective-permute-start | bytes 663560 | tf_op jit(solution)/shard_map/ppermute | solution.py:371
  17.0 0.0 collective-permute-start.5
  17.0 0.0 collective-permute-done.2.got_ref
  17.0 0.0 copy-start.3
  17.0 0.2 merge.7
  17.2 1.6 %collective-permute-start.4 = (bf16[544,128]{1,0:T(8,128)(2,1)S(1)}, bf16[544,128]{1,0:T(8,128)(2,1)S(1)}, u32[]{:S(2)}, u32[]{:S(2)}) collective-permute-start(bf16[544,128]{1,0:T(8,128)(2,1)S(1)} %get-tuple-element.48), channel_id=1, source_target_pairs={{0,1},{1,0},{2,3},{3,2},{4,5},{5,4},{6,7},{7,6},{8,9},{9,8},{10,11... | collective-permute-start | bytes 417800 | tf_op jit(solution)/shard_map/ppermute | solution.py:319
  18.8 0.0 collective-permute-done.5.got_ref
  18.8 4.1 %pairs.2.after_ref.msg1_ref = f32[4,128,128]{2,1,0:T(8,128)S(1)} custom-call(s32[2,4,5]{2,1,0:T(4,128)S(1)} %copy-done.2, bf16[2,6,144,128]{3,2,1,0:T(8,128)(2,1)S(1)} %pad_maximum_fusion.after_ref.ext_ref, bf16[6,144,128]{2,1,0:T(8,128)(2,1)S(1)} %collective-permute-done.5.got_ref, f32[8,128]{1,0:T(8,128)S(1)} %copy-done.3, ...), custom_call_target="tpu_custom_call" | custom-call | flops 4600000000 | tf_op jit(solution)/shard_map/pairs/pallas_call | solution.py:307
  23.0 0.4 %collective-permute-done.4.got_ref = bf16[544,128]{1,0:T(8,128)(2,1)S(1)} collective-permute-done((bf16[544,128]{1,0:T(8,128)(2,1)S(1)}, bf16[544,128]{1,0:T(8,128)(2,1)S(1)}, u32[]{:S(2)}, u32[]{:S(2)}) %collective-permute-start.4) | collective-permute-done | bytes 139296 | tf_op jit(solution)/shard_map/ppermute | solution.py:319
  23.4 0.2 merge.8
  23.6 1.4 %collective-permute-start.6 = (bf16[544,128]{1,0:T(8,128)(2,1)S(1)}, bf16[544,128]{1,0:T(8,128)(2,1)S(1)}, u32[]{:S(2)}, u32[]{:S(2)}) collective-permute-start(bf16[544,128]{1,0:T(8,128)(2,1)S(1)} %get-tuple-element.51), channel_id=1, source_target_pairs={{0,16},{1,17},{2,10},{3,11},{4,20},{5,21},{6,14},{7,15},{8,24},{9,... | collective-permute-start | bytes 417800 | tf_op jit(solution)/shard_map/ppermute | solution.py:319
  25.0 4.1 %pairs.3.after_ref.msg2_ref = f32[4,128,128]{2,1,0:T(8,128)S(1)} custom-call(s32[2,4,5]{2,1,0:T(4,128)S(1)} %copy-done.2, bf16[2,6,144,128]{3,2,1,0:T(8,128)(2,1)S(1)} %pad_maximum_fusion.after_ref.ext_ref, bf16[6,144,128]{2,1,0:T(8,128)(2,1)S(1)} %collective-permute-done.7.got_ref, f32[8,128]{1,0:T(8,128)S(1)} %copy-done.3, ...), custom_call_target="tpu_custom_call" | custom-call | flops 4600000000 | tf_op jit(solution)/shard_map/pairs/pallas_call | solution.py:307
  29.1 2.0 %collective-permute-done.6.got_ref = bf16[544,128]{1,0:T(8,128)(2,1)S(1)} collective-permute-done((bf16[544,128]{1,0:T(8,128)(2,1)S(1)}, bf16[544,128]{1,0:T(8,128)(2,1)S(1)}, u32[]{:S(2)}, u32[]{:S(2)}) %collective-permute-start.6) | collective-permute-done | bytes 139296 | tf_op jit(solution)/shard_map/ppermute | solution.py:319
  31.1 0.2 merge.9.half_ref
  31.4 0.1 collective-permute-start.8
  31.5 0.6 %own_field.1.part_ref = f32[8,128,128]{2,1,0:T(8,128)S(1)} custom-call(bf16[512,128]{1,0:T(8,128)(2,1)S(1)} %merge.9.half_ref, f32[1,512]{1,0:T(1,128)S(1)} %get-tuple-element.52.weight_ref, bf16[128,128]{1,0:T(8,128)(2,1)S(1)} %get-tuple-element.53.charge_t_ref, bf16[512,1024]{1,0:T(8,128)(2,1)S(1)} %get-tuple-element.37.after_ref.table_ref, ...), custom_call_target="tpu_custom_call" | custom-call | flops 1150000000 | tf_op jit(solution)/shard_map/own_field/pallas_call | solution.py:307
  32.0 0.8 %collective-permute-done.8.half_ref = bf16[512,128]{1,0:T(8,128)(2,1)S(1)} collective-permute-done((bf16[512,128]{1,0:T(8,128)(2,1)S(1)}, bf16[512,128]{1,0:T(8,128)(2,1)S(1)}, u32[]{:S(2)}, u32[]{:S(2)}) %collective-permute-start.8) | collective-permute-done | bytes 131104 | tf_op jit(solution)/shard_map/ppermute | solution.py:319
  32.8 1.3 %other_field.1 = f32[8,128,128]{2,1,0:T(8,128)} custom-call(bf16[512,128]{1,0:T(8,128)(2,1)S(1)} %collective-permute-done.8.half_ref, f32[1,512]{1,0:T(1,128)S(1)} %get-tuple-element.52.weight_ref, bf16[128,128]{1,0:T(8,128)(2,1)S(1)} %get-tuple-element.53.charge_t_ref, bf16[512,1024]{1,0:T(8,128)(2,1)S(1)} %get-tuple-element.54.table_ref, ...), custom_call_target="tpu_custom_call" | custom-call | flops 1150000000 | tf_op jit(solution)/shard_map/other_field/pallas_call | solution.py:307
  (13 shorter events, 0.1 us)
Async XLA Ops:
  2.4 1.9 %collective-permute-start = (bf16[544,128]{1,0:T(8,128)(2,1)S(1)}, bf16[544,128]{1,0:T(8,128)(2,1)S(1)}, u32[]{:S(2)}, u32[]{:S(2)}) collective-permute-start(bf16[544,128]{1,0:T(8,128)(2,1)S(1)} %get-tuple-element.36), channel_id=1, source_target_pairs={{0,2},{1,3},{2,0},{3,1},{4,6},{5,7},{6,4},{7,5},{8,10},{9,11},{10,... | collective-permute-start | bytes 417800 | tf_op jit(solution)/shard_map/ppermute | solution.py:319
  4.3 2.9 %copy-start = (bf16[128,128]{1,0:T(8,128)(2,1)S(1)}, bf16[128,128]{1,0:T(8,128)(2,1)}, u32[]{:S(2)}) copy-start(bf16[128,128]{1,0:T(8,128)(2,1)} %w_ref.1) | copy-start | bytes 98308
  4.3 2.9 %copy-start.1 = (bf16[128,128]{1,0:T(8,128)(2,1)S(1)}, bf16[128,128]{1,0:T(8,128)(2,1)}, u32[]{:S(2)}) copy-start(bf16[128,128]{1,0:T(8,128)(2,1)} %charge_ref.1) | copy-start | bytes 98308
  4.6 5.7 %collective-permute-start.1 = (bf16[544,128]{1,0:T(8,128)(2,1)S(1)}, bf16[544,128]{1,0:T(8,128)(2,1)S(1)}, u32[]{:S(2)}, u32[]{:S(2)}) collective-permute-start(bf16[544,128]{1,0:T(8,128)(2,1)S(1)} %get-tuple-element.40), channel_id=1, source_target_pairs={{0,8},{1,9},{2,6},{3,7},{4,12},{5,13},{6,2},{7,3},{8,0},{9,1},{10,... | collective-permute-start | bytes 417800 | tf_op jit(solution)/shard_map/ppermute | solution.py:319
  7.3 0.7 %copy-start.4 = (f32[512]{0:T(512)S(1)}, f32[512]{0:T(512)}, u32[]{:S(2)}) copy-start(f32[512]{0:T(512)} %param.15) | copy-start | bytes 6148
  8.2 6.0 %collective-permute-start.3 = (bf16[2,2,144,128]{3,2,1,0:T(8,128)(2,1)S(1)}, bf16[2,2,144,128]{3,2,1,0:T(8,128)(2,1)S(1)}, u32[]{:S(2)}, u32[]{:S(2)}) collective-permute-start(bf16[2,2,144,128]{3,2,1,0:T(8,128)(2,1)S(1)} %pad_maximum_fusion.1), channel_id=1, source_target_pairs={{0,1},{1,0},{2,3},{3,2},{4,5},{5,4},{6,7},{7,6},{8,9},{9,8},{10,11... | collective-permute-start | bytes 442376 | tf_op jit(solution)/shard_map/ppermute | solution.py:358
  10.5 6.4 %collective-permute-start.2 = (bf16[544,128]{1,0:T(8,128)(2,1)S(1)}, bf16[544,128]{1,0:T(8,128)(2,1)S(1)}, u32[]{:S(2)}, u32[]{:S(2)}) collective-permute-start(bf16[544,128]{1,0:T(8,128)(2,1)S(1)} %get-tuple-element.45), channel_id=1, source_target_pairs={{0,4},{1,5},{2,18},{3,19},{4,0},{5,1},{6,22},{7,23},{8,12},{9,13},... | collective-permute-start | bytes 417800 | tf_op jit(solution)/shard_map/ppermute | solution.py:319
  14.3 10.7 %collective-permute-start.7 = (bf16[6,144,128]{2,1,0:T(8,128)(2,1)S(1)}, bf16[6,144,128]{2,1,0:T(8,128)(2,1)S(1)}, u32[]{:S(2)}, u32[]{:S(2)}) collective-permute-start(bf16[6,144,128]{2,1,0:T(8,128)(2,1)S(1)} %get-tuple-element.55), channel_id=1, source_target_pairs={{0,30},{2,4},{4,2},{6,8},{8,6},{10,12},{12,10},{14,16},{16,14},{18... | collective-permute-start | bytes 663560 | tf_op jit(solution)/shard_map/ppermute | solution.py:371
  17.0 1.8 %collective-permute-start.5 = (bf16[6,144,128]{2,1,0:T(8,128)(2,1)S(1)}, bf16[6,144,128]{2,1,0:T(8,128)(2,1)S(1)}, u32[]{:S(2)}, u32[]{:S(2)}) collective-permute-start(bf16[6,144,128]{2,1,0:T(8,128)(2,1)S(1)} %get-tuple-element.56), channel_id=1, source_target_pairs={{0,2},{2,0},{4,6},{6,4},{8,10},{10,8},{12,14},{14,12},{16,18},{18,... | collective-permute-start | bytes 663560 | tf_op jit(solution)/shard_map/ppermute | solution.py:370
  17.0 1.8 %copy-start.2 = (s32[2,4,5]{2,1,0:T(4,128)S(1)}, s32[2,4,5]{2,1,0:T(4,128)}, u32[]{:S(2)}) copy-start(s32[2,4,5]{2,1,0:T(4,128)} %codes_ref.3) | copy-start | bytes 484
  17.0 1.8 %copy-start.3 = (f32[8,128]{1,0:T(8,128)S(1)}, f32[8,128]{1,0:T(8,128)}, u32[]{:S(2)}) copy-start(f32[8,128]{1,0:T(8,128)} %mix_ref.3) | copy-start | bytes 12292
  17.2 6.1 %collective-permute-start.4 = (bf16[544,128]{1,0:T(8,128)(2,1)S(1)}, bf16[544,128]{1,0:T(8,128)(2,1)S(1)}, u32[]{:S(2)}, u32[]{:S(2)}) collective-permute-start(bf16[544,128]{1,0:T(8,128)(2,1)S(1)} %get-tuple-element.48), channel_id=1, source_target_pairs={{0,1},{1,0},{2,3},{3,2},{4,5},{5,4},{6,7},{7,6},{8,9},{9,8},{10,11... | collective-permute-start | bytes 417800 | tf_op jit(solution)/shard_map/ppermute | solution.py:319
  23.6 7.5 %collective-permute-start.6 = (bf16[544,128]{1,0:T(8,128)(2,1)S(1)}, bf16[544,128]{1,0:T(8,128)(2,1)S(1)}, u32[]{:S(2)}, u32[]{:S(2)}) collective-permute-start(bf16[544,128]{1,0:T(8,128)(2,1)S(1)} %get-tuple-element.51), channel_id=1, source_target_pairs={{0,16},{1,17},{2,10},{3,11},{4,20},{5,21},{6,14},{7,15},{8,24},{9,... | collective-permute-start | bytes 417800 | tf_op jit(solution)/shard_map/ppermute | solution.py:319
  31.4 1.4 %collective-permute-start.8 = (bf16[512,128]{1,0:T(8,128)(2,1)S(1)}, bf16[512,128]{1,0:T(8,128)(2,1)S(1)}, u32[]{:S(2)}, u32[]{:S(2)}) collective-permute-start(bf16[512,128]{1,0:T(8,128)(2,1)S(1)} %merge.9.half_ref), channel_id=1, source_target_pairs={{0,2},{1,3},{2,0},{3,1},{4,6},{5,7},{6,4},{7,5},{8,10},{9,11},{10,... | collective-permute-start | bytes 393224 | tf_op jit(solution)/shard_map/ppermute | solution.py:319

commit v4 on v3

--- a/solution.py
+++ b/solution.py
@@ -64,8 +64,9 @@
     offset = half.astype(jnp.float32) * 0.25
     state_ref[...] = jnp.zeros_like(state_ref)
     state_ref[nb : nb + 1, :] = mean
-    for b in range(nb):
-        at = slice(b * LANES, (b + 1) * LANES)
+    block = min(kvec, 128)
+    for start in range(0, kvec, block):
+        at = slice(start, start + block)
         turns = lax.dot_general(k16[:, at], x16, (((0,), (0,)), ((), ())), preferred_element_type=jnp.float32)
         turns = turns - offset
         turns = turns - jnp.round(turns)
@@ -73,12 +74,15 @@
         table_ref[at, :] = table
         total = jnp.dot(table, sums_rhs(), preferred_element_type=jnp.float32)
         count = total[:, LANES:]
-        state_ref[b : b + 1, :] = jnp.transpose(count)[0:1]
+        for b in range(block // LANES):
+            part = jnp.transpose(count[b * LANES : (b + 1) * LANES])[0:1]
+            state_ref[start // LANES + b : start // LANES + b + 1, :] = part
         store(at, total[:, :LANES] - count * mean)
 
 
 def sent_kernel(
-    nx, ny, frac_hbm, kidx_hbm, emb_hbm, table_ref, send_ref, k16_ref, x16_ref, rhs, mean_ref, frac_ref,
+    nx, ny, frac_hbm, kidx_hbm, emb_hbm, in_hbm, charge_hbm, weight_hbm,
+    table_ref, send_ref, k16_ref, x16_ref, rhs, mean_ref, frac_ref, in_ref, charge_ref, weight_ref,
     kf32, xf32, state, kidx_ref, sems,
 ):
     rows, _, cols, atoms = frac_ref.shape
@@ -88,6 +92,9 @@
         pltpu.make_async_copy(kidx_hbm, kidx_ref, sems.at[0]),
         pltpu.make_async_copy(frac_hbm, frac_ref, sems.at[1]),
         pltpu.make_async_copy(emb_hbm, rhs.at[:, 0:LANES], sems.at[2]),
+        pltpu.make_async_copy(in_hbm, in_ref, sems.at[3]),
+        pltpu.make_async_copy(charge_hbm, charge_ref, sems.at[4]),
+        pltpu.make_async_copy(weight_hbm, weight_ref, sems.at[5]),
     ]
     for fetch in fetches:
         fetch.start()
@@ -125,6 +132,8 @@
 
     half_table(1 - lax.rem(me_x, 2), k16, x16, lambda: rhs[...], mean, state, table_ref, store)
     put_message(send_ref, kvec, state[...])
+    for fetch in fetches[3:]:
+        fetch.wait()
 
 
 def kept_kernel(k16_ref, x16_ref, rhs_ref, mean_ref, table_ref, acc_ref, state_ref):
@@ -322,16 +331,24 @@
     send_out = ((kvec + TAIL, channels), bf16)
     table_out = ((kvec, cells * atoms), bf16)
     k16, x16 = (16, kvec), (16, cells * atoms)
-    table_theirs, send, *operands, parts = call(
+    table_theirs, send, k16_in, x16_in, embedded, mean, parts, w_near, charge_near, weight_near = call(
         functools.partial(sent_kernel, rows * size_x, cols * size_y), "sent_half",
-        [in_hbm(jnp.transpose(frac, (0, 2, 1, 3))), in_hbm(k_index), in_hbm(embed.reshape(-1, channels))],
+        [
+            in_hbm(x)
+            for x in (
+                jnp.transpose(frac, (0, 2, 1, 3)), k_index, embed.reshape(-1, channels), w_in, w_charge,
+                k_weight.reshape(1, kvec),
+            )
+        ],
         [table_out, send_out, (k16, bf16), (x16, bf16), ((cells * atoms, 2 * LANES), bf16), state_out,
-         ((rows, frac.shape[2], cols, atoms), bf16)],
-        [(k16, f32), (x16, f32), state_out, (k_index.shape, jnp.int32), pltpu.SemaphoreType.DMA((3,))],
-        hbm=3, us=2.5,
-    )
-    embedded = operands[2]
-    table_mine, acc, state = call(kept_kernel, "kept_half", operands, [table_out, acc_out, state_out], us=2.5)
+         ((rows, frac.shape[2], cols, atoms), bf16), (w_in.shape, bf16), (w_charge.shape, bf16), ((1, kvec), f32)],
+        [(k16, f32), (x16, f32), state_out, (k_index.shape, jnp.int32), pltpu.SemaphoreType.DMA((6,))],
+        hbm=6, us=2.5,
+    )
+
+    table_mine, acc, state = call(
+        kept_kernel, "kept_half", [k16_in, x16_in, embedded, mean], [table_out, acc_out, state_out], us=2.5
+    )
 
     def merge(acc, state, got, after, last=False):
         outs = [((kvec, channels), bf16)] if last else [send_out, acc_out, state_out]
@@ -340,8 +357,8 @@
     core_bit = size_y
     along_y = [1 << b for b in range(size_y.bit_length() - 1)]
     along_x = [core_bit << b for b in range(1, size_x.bit_length() - 1)]
-    masks = [along_x[1], along_x[0], *along_y, *along_x[2:]]
-    swapped = [along_x[0], *along_x[2:], *along_y, along_x[1]]
+    masks = [along_x[0], *along_y, *along_x[:0:-1]]
+    swapped = [*along_x[1:], along_x[0], *along_y]
 
     def cross(send, t):
         return exchange(send, lambda i: swapped[t] if i & core_bit else masks[t])
@@ -351,7 +368,7 @@
     got = cross(send, 0)
     packed, charge_t, weight = call(
         functools.partial(feats_kernel, 1.0 / math.sqrt(cells * count * atoms * kvec)), "feats",
-        [parts, embedded, w_in, w_charge, k_weight.reshape(1, kvec)],
+        [parts, embedded, w_near, charge_near, weight_near],
         [((rows, cols, atoms + FRAC_ROWS, channels), bf16), (w_charge.shape, bf16), ((1, kvec), f32)], after=state,
     )
     if size_y == 2:

time: 34.3 us -> 32.4 us (0.945)
  waiting for transfers between devices: 5.32 us -> 3.71 us
  local copies, waits for them, and re-layouts: 0.76 us -> 0.08 us
  starting transfers between devices: 12.4 us -> 12.8 us
    ppermute x6, waiting for transfers between devices: 3.71 us -> 2.71 us  [exchange(): lax.ppermute(values, ('gx', 'gy'), [(i, i ^ mask_of(i)) for i in range(co...]
    unnamed x10 -> x4, local copies, waits for them, and re-layouts: 0.69 us -> 0.01 us
    ppermute x6, starting transfers between devices: 8.22 us -> 8.86 us  [exchange(): lax.ppermute(values, ('gx', 'gy'), [(i, i ^ mask_of(i)) for i in range(co...]
    ppermute x1, waiting for transfers between devices: 1.6 us -> 1 us  [shards(): lax.ppermute(jnp.stack([packed[:, -1], packed[:, 0]], axis=1), 'gy', [(0,...]
  transfers between devices with their start and end apart: 9 -> 9, of which waited for: 5 -> 4; matrix products, arithmetic and copies ran while one was open for 0% -> 0% of each run, Pallas kernels for 33% -> 35%
where the time goes in v4:
time: 32.4 us; the launch traced here: 32.2 us
  Pallas kernels  15.4 us (48%)
  starting transfers between devices  12.8 us (40%)
  waiting for transfers between devices  3.71 us (11%)
    pallas_call x12, Pallas kernels, call(): pl.pallas_call(body, out_shape=[jax.ShapeDtypeStruct(*o) for o in outs],...  15.4 us
    ppermute x6, starting transfers between devices, exchange(): lax.ppermute(values, ('gx', 'gy'), [(i, i ^ mask_of(i)) for i in range(co...  8.86 us
    ppermute x6, waiting for transfers between devices, exchange(): lax.ppermute(values, ('gx', 'gy'), [(i, i ^ mask_of(i)) for i in range(co...  2.71 us
    ppermute x1, starting transfers between devices, shards(): lax.ppermute(toward_2, 'gx', [(i, (i - 1) % size_x if i % 2 == 0 else (i...  2.42 us
    ppermute x1, starting transfers between devices, shards(): lax.ppermute(jnp.stack([packed[:, -1], packed[:, 0]], axis=1), 'gy', [(0,...  1.55 us
    ppermute x1, waiting for transfers between devices, shards(): lax.ppermute(jnp.stack([packed[:, -1], packed[:, 0]], axis=1), 'gy', [(0,...  1 us
  transfers between devices with their start and end apart: 9, of which 4 were waited for; matrix products, arithmetic and copies ran while one was open for 0% of the time, Pallas kernels for 35%

profile of v4, /device:TPU:0, one launch (start us, length us, event | category | flops | bytes accessed | tf_op | source)
XLA Modules:
  0.0 32.2 jit_solution(2994908869434489436)
XLA Ops:
  0.0 2.4 %sent_half.1 = (bf16[512,1024]{1,0:T(8,128)(2,1)S(1)}, bf16[544,128]{1,0:T(8,128)(2,1)S(1)}, bf16[16,512]{1,0:T(8,128)(2,1)S(1)}, bf16[16,1024]{1,0:T(8,128)(2,1...) custom-call(bf16[2,3,4,128]{3,2,1,0:T(4,128)(2,1)} %bitcast.9, ...), custom_call_target="tpu_custom_call" | custom-call | flops 2875000064 | tf_op jit(solution)/shard_map/sent_half/pallas_call | solution.py:316
  2.5 0.5 %collective-permute-start = (bf16[544,128]{1,0:T(8,128)(2,1)S(1)}, bf16[544,128]{1,0:T(8,128)(2,1)S(1)}, u32[]{:S(2)}, u32[]{:S(2)}) collective-permute-start(bf16[544,128]{1,0:T(8,128)(2,1)S(1)} %get-tuple-element.39), channel_id=1, source_target_pairs={{0,2},{1,3},{2,0},{3,1},{4,6},{5,7},{6,4},{7,5},{8,10},{9,11},{10,... | collective-permute-start | bytes 417800 | tf_op jit(solution)/shard_map/ppermute | solution.py:328
  3.0 1.4 %kept_half.1 = (bf16[512,1024]{1,0:T(8,128)(2,1)S(1)}, f32[512,128]{1,0:T(8,128)S(1)}, f32[8,128]{1,0:T(8,128)S(1)}) custom-call(bf16[16,512]{1,0:T(8,128)(2,1)S(1)} %get-tuple-element.33.k16_ref, bf16[16,1024]{1,0:T(8,128)(2,1)S(1)} %get-tuple-element.34.x16_ref, bf16[1024,256]{1,0:T(8,128)(2,1)S(1)} %get-tuple-element.35.rhs_ref.emb_ref, ...), custom_call_target="tpu_custom_call" | custom-call | flops 2875000064 | tf_op jit(solution)/shard_map/kept_half/pallas_call | solution.py:316
  4.4 0.0 collective-permute-done.got_ref
  4.4 0.3 merge.5
  4.6 2.6 %collective-permute-start.1 = (bf16[544,128]{1,0:T(8,128)(2,1)S(1)}, bf16[544,128]{1,0:T(8,128)(2,1)S(1)}, u32[]{:S(2)}, u32[]{:S(2)}) collective-permute-start(bf16[544,128]{1,0:T(8,128)(2,1)S(1)} %get-tuple-element.43), channel_id=1, source_target_pairs={{0,4},{1,5},{2,10},{3,11},{4,0},{5,1},{6,14},{7,15},{8,12},{9,13},... | collective-permute-start | bytes 417800 | tf_op jit(solution)/shard_map/ppermute | solution.py:328
  7.2 0.2 feats.1
  7.5 1.6 %collective-permute-start.3 = (bf16[2,2,144,128]{3,2,1,0:T(8,128)(2,1)S(1)}, bf16[2,2,144,128]{3,2,1,0:T(8,128)(2,1)S(1)}, u32[]{:S(2)}, u32[]{:S(2)}) collective-permute-start(bf16[2,2,144,128]{3,2,1,0:T(8,128)(2,1)S(1)} %pad_maximum_fusion.1), channel_id=1, source_target_pairs={{0,1},{1,0},{2,3},{3,2},{4,5},{5,4},{6,7},{7,6},{8,9},{9,8},{10,11... | collective-permute-start | bytes 442376 | tf_op jit(solution)/shard_map/ppermute | solution.py:375
  9.1 1.2 %collective-permute-done.1.got_ref = bf16[544,128]{1,0:T(8,128)(2,1)S(1)} collective-permute-done((bf16[544,128]{1,0:T(8,128)(2,1)S(1)}, bf16[544,128]{1,0:T(8,128)(2,1)S(1)}, u32[]{:S(2)}, u32[]{:S(2)}) %collective-permute-start.1) | collective-permute-done | bytes 139296 | tf_op jit(solution)/shard_map/ppermute | solution.py:328
  10.3 0.2 merge.6
  10.5 2.1 %collective-permute-start.2 = (bf16[544,128]{1,0:T(8,128)(2,1)S(1)}, bf16[544,128]{1,0:T(8,128)(2,1)S(1)}, u32[]{:S(2)}, u32[]{:S(2)}) collective-permute-start(bf16[544,128]{1,0:T(8,128)(2,1)S(1)} %get-tuple-element.51), channel_id=1, source_target_pairs={{0,1},{1,0},{2,18},{3,19},{4,5},{5,4},{6,22},{7,23},{8,9},{9,8},{1... | collective-permute-start | bytes 417800 | tf_op jit(solution)/shard_map/ppermute | solution.py:328
  12.6 1.0 %collective-permute-done.3 = bf16[2,2,144,128]{3,2,1,0:T(8,128)(2,1)S(1)} collective-permute-done((bf16[2,2,144,128]{3,2,1,0:T(8,128)(2,1)S(1)}, bf16[2,2,144,128]{3,2,1,0:T(8,128)(2,1)S(1)}, u32[]{:S(2)}, u32[]{:S(2)}) %collective-permute-start.3) | collective-permute-done | bytes 147488 | tf_op jit(solution)/shard_map/ppermute | solution.py:375
  13.6 0.1 pad_maximum_fusion.after_ref.ext_ref
  13.7 2.4 %collective-permute-start.7 = (bf16[6,144,128]{2,1,0:T(8,128)(2,1)S(1)}, bf16[6,144,128]{2,1,0:T(8,128)(2,1)S(1)}, u32[]{:S(2)}, u32[]{:S(2)}) collective-permute-start(bf16[6,144,128]{2,1,0:T(8,128)(2,1)S(1)} %get-tuple-element.61), channel_id=1, source_target_pairs={{0,30},{2,4},{4,2},{6,8},{8,6},{10,12},{12,10},{14,16},{16,14},{18... | collective-permute-start | bytes 663560 | tf_op jit(solution)/shard_map/ppermute | solution.py:388
  16.1 0.0 collective-permute-start.5
  16.1 0.0 collective-permute-done.2.got_ref
  16.1 0.0 copy-start.1
  16.1 0.2 merge.7
  16.4 2.6 %collective-permute-start.4 = (bf16[544,128]{1,0:T(8,128)(2,1)S(1)}, bf16[544,128]{1,0:T(8,128)(2,1)S(1)}, u32[]{:S(2)}, u32[]{:S(2)}) collective-permute-start(bf16[544,128]{1,0:T(8,128)(2,1)S(1)} %get-tuple-element.54), channel_id=1, source_target_pairs={{0,16},{1,17},{2,6},{3,7},{4,20},{5,21},{6,2},{7,3},{8,24},{9,25},... | collective-permute-start | bytes 417800 | tf_op jit(solution)/shard_map/ppermute | solution.py:328
  19.0 0.0 collective-permute-done.5.got_ref
  19.1 4.1 %pairs.2.after_ref.msg1_ref = f32[4,128,128]{2,1,0:T(8,128)S(1)} custom-call(s32[2,4,5]{2,1,0:T(4,128)S(1)} %copy-done, bf16[2,6,144,128]{3,2,1,0:T(8,128)(2,1)S(1)} %pad_maximum_fusion.after_ref.ext_ref, bf16[6,144,128]{2,1,0:T(8,128)(2,1)S(1)} %collective-permute-done.5.got_ref, f32[8,128]{1,0:T(8,128)S(1)} %copy-done.1, ...), custom_call_target="tpu_custom_call" | custom-call | flops 4600000000 | tf_op jit(solution)/shard_map/pairs/pallas_call | solution.py:316
  23.2 0.7 %collective-permute-done.4.got_ref = bf16[544,128]{1,0:T(8,128)(2,1)S(1)} collective-permute-done((bf16[544,128]{1,0:T(8,128)(2,1)S(1)}, bf16[544,128]{1,0:T(8,128)(2,1)S(1)}, u32[]{:S(2)}, u32[]{:S(2)}) %collective-permute-start.4) | collective-permute-done | bytes 139296 | tf_op jit(solution)/shard_map/ppermute | solution.py:328
  23.9 0.2 merge.8
  24.2 1.0 %collective-permute-start.6 = (bf16[544,128]{1,0:T(8,128)(2,1)S(1)}, bf16[544,128]{1,0:T(8,128)(2,1)S(1)}, u32[]{:S(2)}, u32[]{:S(2)}) collective-permute-start(bf16[544,128]{1,0:T(8,128)(2,1)S(1)} %get-tuple-element.57), channel_id=1, source_target_pairs={{0,8},{1,9},{2,3},{3,2},{4,12},{5,13},{6,7},{7,6},{8,0},{9,1},{10,... | collective-permute-start | bytes 417800 | tf_op jit(solution)/shard_map/ppermute | solution.py:328
  25.1 0.0 collective-permute-done.7.got_ref
  25.1 4.1 %pairs.3.after_ref.msg2_ref = f32[4,128,128]{2,1,0:T(8,128)S(1)} custom-call(s32[2,4,5]{2,1,0:T(4,128)S(1)} %copy-done, bf16[2,6,144,128]{3,2,1,0:T(8,128)(2,1)S(1)} %pad_maximum_fusion.after_ref.ext_ref, bf16[6,144,128]{2,1,0:T(8,128)(2,1)S(1)} %collective-permute-done.7.got_ref, f32[8,128]{1,0:T(8,128)S(1)} %copy-done.1, ...), custom_call_target="tpu_custom_call" | custom-call | flops 4600000000 | tf_op jit(solution)/shard_map/pairs/pallas_call | solution.py:316
  29.3 0.0 collective-permute-done.6.got_ref
  29.3 0.2 merge.9.half_ref
  29.5 0.1 collective-permute-start.8
  29.6 0.6 %own_field.1.part_ref = f32[8,128,128]{2,1,0:T(8,128)S(1)} custom-call(bf16[512,128]{1,0:T(8,128)(2,1)S(1)} %merge.9.half_ref, f32[1,512]{1,0:T(1,128)S(1)} %get-tuple-element.58.weight_ref, bf16[128,128]{1,0:T(8,128)(2,1)S(1)} %get-tuple-element.59.charge_t_ref, bf16[512,1024]{1,0:T(8,128)(2,1)S(1)} %get-tuple-element.40.after_ref.table_ref, ...), custom_call_target="tpu_custom_call" | custom-call | flops 1150000000 | tf_op jit(solution)/shard_map/own_field/pallas_call | solution.py:316
  30.2 0.8 %collective-permute-done.8.half_ref = bf16[512,128]{1,0:T(8,128)(2,1)S(1)} collective-permute-done((bf16[512,128]{1,0:T(8,128)(2,1)S(1)}, bf16[512,128]{1,0:T(8,128)(2,1)S(1)}, u32[]{:S(2)}, u32[]{:S(2)}) %collective-permute-start.8) | collective-permute-done | bytes 131104 | tf_op jit(solution)/shard_map/ppermute | solution.py:328
  30.9 1.3 %other_field.1 = f32[8,128,128]{2,1,0:T(8,128)} custom-call(bf16[512,128]{1,0:T(8,128)(2,1)S(1)} %collective-permute-done.8.half_ref, f32[1,512]{1,0:T(1,128)S(1)} %get-tuple-element.58.weight_ref, bf16[128,128]{1,0:T(8,128)(2,1)S(1)} %get-tuple-element.59.charge_t_ref, bf16[512,1024]{1,0:T(8,128)(2,1)S(1)} %get-tuple-element.60.table_ref, ...), custom_call_target="tpu_custom_call" | custom-call | flops 1150000000 | tf_op jit(solution)/shard_map/other_field/pallas_call | solution.py:316
  (7 shorter events, 0.1 us)
Async XLA Ops:
  2.5 1.9 %collective-permute-start = (bf16[544,128]{1,0:T(8,128)(2,1)S(1)}, bf16[544,128]{1,0:T(8,128)(2,1)S(1)}, u32[]{:S(2)}, u32[]{:S(2)}) collective-permute-start(bf16[544,128]{1,0:T(8,128)(2,1)S(1)} %get-tuple-element.39), channel_id=1, source_target_pairs={{0,2},{1,3},{2,0},{3,1},{4,6},{5,7},{6,4},{7,5},{8,10},{9,11},{10,... | collective-permute-start | bytes 417800 | tf_op jit(solution)/shard_map/ppermute | solution.py:328
  4.6 5.6 %collective-permute-start.1 = (bf16[544,128]{1,0:T(8,128)(2,1)S(1)}, bf16[544,128]{1,0:T(8,128)(2,1)S(1)}, u32[]{:S(2)}, u32[]{:S(2)}) collective-permute-start(bf16[544,128]{1,0:T(8,128)(2,1)S(1)} %get-tuple-element.43), channel_id=1, source_target_pairs={{0,4},{1,5},{2,10},{3,11},{4,0},{5,1},{6,14},{7,15},{8,12},{9,13},... | collective-permute-start | bytes 417800 | tf_op jit(solution)/shard_map/ppermute | solution.py:328
  7.5 6.1 %collective-permute-start.3 = (bf16[2,2,144,128]{3,2,1,0:T(8,128)(2,1)S(1)}, bf16[2,2,144,128]{3,2,1,0:T(8,128)(2,1)S(1)}, u32[]{:S(2)}, u32[]{:S(2)}) collective-permute-start(bf16[2,2,144,128]{3,2,1,0:T(8,128)(2,1)S(1)} %pad_maximum_fusion.1), channel_id=1, source_target_pairs={{0,1},{1,0},{2,3},{3,2},{4,5},{5,4},{6,7},{7,6},{8,9},{9,8},{10,11... | collective-permute-start | bytes 442376 | tf_op jit(solution)/shard_map/ppermute | solution.py:375
  10.5 5.6 %collective-permute-start.2 = (bf16[544,128]{1,0:T(8,128)(2,1)S(1)}, bf16[544,128]{1,0:T(8,128)(2,1)S(1)}, u32[]{:S(2)}, u32[]{:S(2)}) collective-permute-start(bf16[544,128]{1,0:T(8,128)(2,1)S(1)} %get-tuple-element.51), channel_id=1, source_target_pairs={{0,1},{1,0},{2,18},{3,19},{4,5},{5,4},{6,22},{7,23},{8,9},{9,8},{1... | collective-permute-start | bytes 417800 | tf_op jit(solution)/shard_map/ppermute | solution.py:328
  13.7 11.4 %collective-permute-start.7 = (bf16[6,144,128]{2,1,0:T(8,128)(2,1)S(1)}, bf16[6,144,128]{2,1,0:T(8,128)(2,1)S(1)}, u32[]{:S(2)}, u32[]{:S(2)}) collective-permute-start(bf16[6,144,128]{2,1,0:T(8,128)(2,1)S(1)} %get-tuple-element.61), channel_id=1, source_target_pairs={{0,30},{2,4},{4,2},{6,8},{8,6},{10,12},{12,10},{14,16},{16,14},{18... | collective-permute-start | bytes 663560 | tf_op jit(solution)/shard_map/ppermute | solution.py:388
  16.1 2.9 %collective-permute-start.5 = (bf16[6,144,128]{2,1,0:T(8,128)(2,1)S(1)}, bf16[6,144,128]{2,1,0:T(8,128)(2,1)S(1)}, u32[]{:S(2)}, u32[]{:S(2)}) collective-permute-start(bf16[6,144,128]{2,1,0:T(8,128)(2,1)S(1)} %get-tuple-element.62), channel_id=1, source_target_pairs={{0,2},{2,0},{4,6},{6,4},{8,10},{10,8},{12,14},{14,12},{16,18},{18,... | collective-permute-start | bytes 663560 | tf_op jit(solution)/shard_map/ppermute | solution.py:387
  16.1 2.9 %copy-start = (s32[2,4,5]{2,1,0:T(4,128)S(1)}, s32[2,4,5]{2,1,0:T(4,128)}, u32[]{:S(2)}) copy-start(s32[2,4,5]{2,1,0:T(4,128)} %codes_ref.3) | copy-start | bytes 484
  16.1 2.9 %copy-start.1 = (f32[8,128]{1,0:T(8,128)S(1)}, f32[8,128]{1,0:T(8,128)}, u32[]{:S(2)}) copy-start(f32[8,128]{1,0:T(8,128)} %mix_ref.3) | copy-start | bytes 12292
  16.4 7.5 %collective-permute-start.4 = (bf16[544,128]{1,0:T(8,128)(2,1)S(1)}, bf16[544,128]{1,0:T(8,128)(2,1)S(1)}, u32[]{:S(2)}, u32[]{:S(2)}) collective-permute-start(bf16[544,128]{1,0:T(8,128)(2,1)S(1)} %get-tuple-element.54), channel_id=1, source_target_pairs={{0,16},{1,17},{2,6},{3,7},{4,20},{5,21},{6,2},{7,3},{8,24},{9,25},... | collective-permute-start | bytes 417800 | tf_op jit(solution)/shard_map/ppermute | solution.py:328
  24.2 5.1 %collective-permute-start.6 = (bf16[544,128]{1,0:T(8,128)(2,1)S(1)}, bf16[544,128]{1,0:T(8,128)(2,1)S(1)}, u32[]{:S(2)}, u32[]{:S(2)}) collective-permute-start(bf16[544,128]{1,0:T(8,128)(2,1)S(1)} %get-tuple-element.57), channel_id=1, source_target_pairs={{0,8},{1,9},{2,3},{3,2},{4,12},{5,13},{6,7},{7,6},{8,0},{9,1},{10,... | collective-permute-start | bytes 417800 | tf_op jit(solution)/shard_map/ppermute | solution.py:328
  29.5 1.4 %collective-permute-start.8 = (bf16[512,128]{1,0:T(8,128)(2,1)S(1)}, bf16[512,128]{1,0:T(8,128)(2,1)S(1)}, u32[]{:S(2)}, u32[]{:S(2)}) collective-permute-start(bf16[512,128]{1,0:T(8,128)(2,1)S(1)} %merge.9.half_ref), channel_id=1, source_target_pairs={{0,2},{1,3},{2,0},{3,1},{4,6},{5,7},{6,4},{7,5},{8,10},{9,11},{10,... | collective-permute-start | bytes 393224 | tf_op jit(solution)/shard_map/ppermute | solution.py:328

commit v5 on v4

--- a/solution.py
+++ b/solution.py
@@ -62,11 +62,10 @@
     kvec = table_ref.shape[0]
     nb = kvec // LANES
     offset = half.astype(jnp.float32) * 0.25
-    state_ref[...] = jnp.zeros_like(state_ref)
-    state_ref[nb : nb + 1, :] = mean
-    block = min(kvec, 128)
-    for start in range(0, kvec, block):
-        at = slice(start, start + block)
+    lane = lax.broadcasted_iota(jnp.int32, (LANES, LANES), 1)
+    counts = jnp.zeros((LANES, LANES), jnp.float32)
+    for b in range(nb):
+        at = slice(b * LANES, (b + 1) * LANES)
         turns = lax.dot_general(k16[:, at], x16, (((0,), (0,)), ((), ())), preferred_element_type=jnp.float32)
         turns = turns - offset
         turns = turns - jnp.round(turns)
@@ -74,10 +73,10 @@
         table_ref[at, :] = table
         total = jnp.dot(table, sums_rhs(), preferred_element_type=jnp.float32)
         count = total[:, LANES:]
-        for b in range(block // LANES):
-            part = jnp.transpose(count[b * LANES : (b + 1) * LANES])[0:1]
-            state_ref[start // LANES + b : start // LANES + b + 1, :] = part
+        counts = jnp.where(lane == b, count, counts)
         store(at, total[:, :LANES] - count * mean)
+    row = lax.broadcasted_iota(jnp.int32, (8, LANES), 0)
+    state_ref[...] = jnp.where(row == nb, jnp.broadcast_to(mean, (8, LANES)), jnp.transpose(counts)[0:8])
 
 
 def sent_kernel(
@@ -255,18 +254,18 @@
         out_ref[c] = total
 
 
-def field_part(half_ref, weight_ref, charge_t_ref, table_ref):
+def field_factors(half_ref, weight_ref, charge_t_ref):
     factors = lax.dot_general(
         charge_t_ref[...], half_ref[...], (((1,), (1,)), ((), ())), preferred_element_type=jnp.float32
     )
-    factors = (factors * weight_ref[...]).astype(jnp.bfloat16)
-    return jnp.dot(factors, table_ref[...], preferred_element_type=jnp.float32)
+    return (factors * weight_ref[...]).astype(jnp.bfloat16)
 
 
 def own_field_kernel(half_ref, weight_ref, charge_t_ref, table_ref, emb_ref, msg1_ref, msg2_ref, out_ref):
     cols, atoms, _ = msg1_ref.shape
     row1 = 1 - lax.rem(lax.axis_index("gx"), 2)
-    total = field_part(half_ref, weight_ref, charge_t_ref, table_ref)
+    factors = field_factors(half_ref, weight_ref, charge_t_ref)
+    total = jnp.dot(factors, table_ref[...], preferred_element_type=jnp.float32)
     for r in range(2):
         for c in range(cols):
             i = r * cols + c
@@ -277,10 +276,13 @@
 
 def other_field_kernel(half_ref, weight_ref, charge_t_ref, table_ref, part_ref, out_ref, done, sems):
     cells, atoms, _ = done.shape
-    total = field_part(half_ref, weight_ref, charge_t_ref, table_ref)
+    factors = field_factors(half_ref, weight_ref, charge_t_ref)
     copies = []
     for i in range(cells):
-        done[i] = part_ref[i] + jnp.transpose(total[:, i * atoms : (i + 1) * atoms])
+        if i % 2 == 0:
+            at = slice(i * atoms, (i + 2) * atoms)
+            total = jnp.dot(factors, table_ref[:, at], preferred_element_type=jnp.float32)
+        done[i] = part_ref[i] + jnp.transpose(total[:, (i % 2) * atoms : (i % 2 + 1) * atoms])
         copy = pltpu.make_async_copy(done.at[i], out_ref.at[i], sems.at[i])
         copy.start()
         copies.append(copy)

time: 32.4 us -> 32.4 us (level)
  no operation moved by 1% of the time
where the time goes in v5:
time: 32.4 us; the launch traced here: 32.2 us
  Pallas kernels  15.4 us (48%)
  starting transfers between devices  12.8 us (40%)
  waiting for transfers between devices  3.72 us (11%)
    pallas_call x12, Pallas kernels, call(): pl.pallas_call(body, out_shape=[jax.ShapeDtypeStruct(*o) for o in outs],...  15.4 us
    ppermute x6, starting transfers between devices, exchange(): lax.ppermute(values, ('gx', 'gy'), [(i, i ^ mask_of(i)) for i in range(co...  8.85 us
    ppermute x6, waiting for transfers between devices, exchange(): lax.ppermute(values, ('gx', 'gy'), [(i, i ^ mask_of(i)) for i in range(co...  2.71 us
    ppermute x1, starting transfers between devices, shards(): lax.ppermute(toward_2, 'gx', [(i, (i - 1) % size_x if i % 2 == 0 else (i...  2.42 us
    ppermute x1, starting transfers between devices, shards(): lax.ppermute(jnp.stack([packed[:, -1], packed[:, 0]], axis=1), 'gy', [(0,...  1.55 us
    ppermute x1, waiting for transfers between devices, shards(): lax.ppermute(jnp.stack([packed[:, -1], packed[:, 0]], axis=1), 'gy', [(0,...  1 us
  transfers between devices with their start and end apart: 9, of which 4 were waited for; matrix products, arithmetic and copies ran while one was open for 0% of the time, Pallas kernels for 35%

profile of v5, /device:TPU:0, one launch (start us, length us, event | category | flops | bytes accessed | tf_op | source)
XLA Modules:
  0.0 32.2 jit_solution(13820457966746290341)
XLA Ops:
  0.0 2.5 %sent_half.1 = (bf16[512,1024]{1,0:T(8,128)(2,1)S(1)}, bf16[544,128]{1,0:T(8,128)(2,1)S(1)}, bf16[16,512]{1,0:T(8,128)(2,1)S(1)}, bf16[16,1024]{1,0:T(8,128)(2,1...) custom-call(bf16[2,3,4,128]{3,2,1,0:T(4,128)(2,1)} %bitcast.9, ...), custom_call_target="tpu_custom_call" | custom-call | flops 2875000064 | tf_op jit(solution)/shard_map/sent_half/pallas_call | solution.py:318
  2.5 0.5 %collective-permute-start = (bf16[544,128]{1,0:T(8,128)(2,1)S(1)}, bf16[544,128]{1,0:T(8,128)(2,1)S(1)}, u32[]{:S(2)}, u32[]{:S(2)}) collective-permute-start(bf16[544,128]{1,0:T(8,128)(2,1)S(1)} %get-tuple-element.39), channel_id=1, source_target_pairs={{0,2},{1,3},{2,0},{3,1},{4,6},{5,7},{6,4},{7,5},{8,10},{9,11},{10,... | collective-permute-start | bytes 417800 | tf_op jit(solution)/shard_map/ppermute | solution.py:330
  3.0 1.4 %kept_half.1 = (bf16[512,1024]{1,0:T(8,128)(2,1)S(1)}, f32[512,128]{1,0:T(8,128)S(1)}, f32[8,128]{1,0:T(8,128)S(1)}) custom-call(bf16[16,512]{1,0:T(8,128)(2,1)S(1)} %get-tuple-element.33.k16_ref, bf16[16,1024]{1,0:T(8,128)(2,1)S(1)} %get-tuple-element.34.x16_ref, bf16[1024,256]{1,0:T(8,128)(2,1)S(1)} %get-tuple-element.35.rhs_ref.emb_ref, ...), custom_call_target="tpu_custom_call" | custom-call | flops 2875000064 | tf_op jit(solution)/shard_map/kept_half/pallas_call | solution.py:318
  4.4 0.0 collective-permute-done.got_ref
  4.4 0.2 merge.5
  4.6 2.6 %collective-permute-start.1 = (bf16[544,128]{1,0:T(8,128)(2,1)S(1)}, bf16[544,128]{1,0:T(8,128)(2,1)S(1)}, u32[]{:S(2)}, u32[]{:S(2)}) collective-permute-start(bf16[544,128]{1,0:T(8,128)(2,1)S(1)} %get-tuple-element.43), channel_id=1, source_target_pairs={{0,4},{1,5},{2,10},{3,11},{4,0},{5,1},{6,14},{7,15},{8,12},{9,13},... | collective-permute-start | bytes 417800 | tf_op jit(solution)/shard_map/ppermute | solution.py:330
  7.3 0.2 feats.1
  7.5 1.6 %collective-permute-start.3 = (bf16[2,2,144,128]{3,2,1,0:T(8,128)(2,1)S(1)}, bf16[2,2,144,128]{3,2,1,0:T(8,128)(2,1)S(1)}, u32[]{:S(2)}, u32[]{:S(2)}) collective-permute-start(bf16[2,2,144,128]{3,2,1,0:T(8,128)(2,1)S(1)} %pad_maximum_fusion.1), channel_id=1, source_target_pairs={{0,1},{1,0},{2,3},{3,2},{4,5},{5,4},{6,7},{7,6},{8,9},{9,8},{10,11... | collective-permute-start | bytes 442376 | tf_op jit(solution)/shard_map/ppermute | solution.py:377
  9.1 1.2 %collective-permute-done.1.got_ref = bf16[544,128]{1,0:T(8,128)(2,1)S(1)} collective-permute-done((bf16[544,128]{1,0:T(8,128)(2,1)S(1)}, bf16[544,128]{1,0:T(8,128)(2,1)S(1)}, u32[]{:S(2)}, u32[]{:S(2)}) %collective-permute-start.1) | collective-permute-done | bytes 139296 | tf_op jit(solution)/shard_map/ppermute | solution.py:330
  10.3 0.2 merge.6
  10.5 2.1 %collective-permute-start.2 = (bf16[544,128]{1,0:T(8,128)(2,1)S(1)}, bf16[544,128]{1,0:T(8,128)(2,1)S(1)}, u32[]{:S(2)}, u32[]{:S(2)}) collective-permute-start(bf16[544,128]{1,0:T(8,128)(2,1)S(1)} %get-tuple-element.51), channel_id=1, source_target_pairs={{0,1},{1,0},{2,18},{3,19},{4,5},{5,4},{6,22},{7,23},{8,9},{9,8},{1... | collective-permute-start | bytes 417800 | tf_op jit(solution)/shard_map/ppermute | solution.py:330
  12.6 1.0 %collective-permute-done.3 = bf16[2,2,144,128]{3,2,1,0:T(8,128)(2,1)S(1)} collective-permute-done((bf16[2,2,144,128]{3,2,1,0:T(8,128)(2,1)S(1)}, bf16[2,2,144,128]{3,2,1,0:T(8,128)(2,1)S(1)}, u32[]{:S(2)}, u32[]{:S(2)}) %collective-permute-start.3) | collective-permute-done | bytes 147488 | tf_op jit(solution)/shard_map/ppermute | solution.py:377
  13.6 0.1 pad_maximum_fusion.after_ref.ext_ref
  13.7 2.4 %collective-permute-start.7 = (bf16[6,144,128]{2,1,0:T(8,128)(2,1)S(1)}, bf16[6,144,128]{2,1,0:T(8,128)(2,1)S(1)}, u32[]{:S(2)}, u32[]{:S(2)}) collective-permute-start(bf16[6,144,128]{2,1,0:T(8,128)(2,1)S(1)} %get-tuple-element.61), channel_id=1, source_target_pairs={{0,30},{2,4},{4,2},{6,8},{8,6},{10,12},{12,10},{14,16},{16,14},{18... | collective-permute-start | bytes 663560 | tf_op jit(solution)/shard_map/ppermute | solution.py:390
  16.1 0.0 collective-permute-start.5
  16.1 0.0 collective-permute-done.2.got_ref
  16.2 0.0 copy-start.1
  16.2 0.2 merge.7
  16.4 2.6 %collective-permute-start.4 = (bf16[544,128]{1,0:T(8,128)(2,1)S(1)}, bf16[544,128]{1,0:T(8,128)(2,1)S(1)}, u32[]{:S(2)}, u32[]{:S(2)}) collective-permute-start(bf16[544,128]{1,0:T(8,128)(2,1)S(1)} %get-tuple-element.54), channel_id=1, source_target_pairs={{0,16},{1,17},{2,6},{3,7},{4,20},{5,21},{6,2},{7,3},{8,24},{9,25},... | collective-permute-start | bytes 417800 | tf_op jit(solution)/shard_map/ppermute | solution.py:330
  19.1 0.0 collective-permute-done.5.got_ref
  19.1 4.1 %pairs.2.after_ref.msg1_ref = f32[4,128,128]{2,1,0:T(8,128)S(1)} custom-call(s32[2,4,5]{2,1,0:T(4,128)S(1)} %copy-done, bf16[2,6,144,128]{3,2,1,0:T(8,128)(2,1)S(1)} %pad_maximum_fusion.after_ref.ext_ref, bf16[6,144,128]{2,1,0:T(8,128)(2,1)S(1)} %collective-permute-done.5.got_ref, f32[8,128]{1,0:T(8,128)S(1)} %copy-done.1, ...), custom_call_target="tpu_custom_call" | custom-call | flops 4600000000 | tf_op jit(solution)/shard_map/pairs/pallas_call | solution.py:318
  23.2 0.7 %collective-permute-done.4.got_ref = bf16[544,128]{1,0:T(8,128)(2,1)S(1)} collective-permute-done((bf16[544,128]{1,0:T(8,128)(2,1)S(1)}, bf16[544,128]{1,0:T(8,128)(2,1)S(1)}, u32[]{:S(2)}, u32[]{:S(2)}) %collective-permute-start.4) | collective-permute-done | bytes 139296 | tf_op jit(solution)/shard_map/ppermute | solution.py:330
  23.9 0.2 merge.8
  24.2 1.0 %collective-permute-start.6 = (bf16[544,128]{1,0:T(8,128)(2,1)S(1)}, bf16[544,128]{1,0:T(8,128)(2,1)S(1)}, u32[]{:S(2)}, u32[]{:S(2)}) collective-permute-start(bf16[544,128]{1,0:T(8,128)(2,1)S(1)} %get-tuple-element.57), channel_id=1, source_target_pairs={{0,8},{1,9},{2,3},{3,2},{4,12},{5,13},{6,7},{7,6},{8,0},{9,1},{10,... | collective-permute-start | bytes 417800 | tf_op jit(solution)/shard_map/ppermute | solution.py:330
  25.1 0.0 collective-permute-done.7.got_ref
  25.1 4.1 %pairs.3.after_ref.msg2_ref = f32[4,128,128]{2,1,0:T(8,128)S(1)} custom-call(s32[2,4,5]{2,1,0:T(4,128)S(1)} %copy-done, bf16[2,6,144,128]{3,2,1,0:T(8,128)(2,1)S(1)} %pad_maximum_fusion.after_ref.ext_ref, bf16[6,144,128]{2,1,0:T(8,128)(2,1)S(1)} %collective-permute-done.7.got_ref, f32[8,128]{1,0:T(8,128)S(1)} %copy-done.1, ...), custom_call_target="tpu_custom_call" | custom-call | flops 4600000000 | tf_op jit(solution)/shard_map/pairs/pallas_call | solution.py:318
  29.3 0.0 collective-permute-done.6.got_ref
  29.3 0.2 merge.9.half_ref
  29.5 0.1 collective-permute-start.8
  29.6 0.6 %own_field.1.part_ref = f32[8,128,128]{2,1,0:T(8,128)S(1)} custom-call(bf16[512,128]{1,0:T(8,128)(2,1)S(1)} %merge.9.half_ref, f32[1,512]{1,0:T(1,128)S(1)} %get-tuple-element.58.weight_ref, bf16[128,128]{1,0:T(8,128)(2,1)S(1)} %get-tuple-element.59.charge_t_ref, bf16[512,1024]{1,0:T(8,128)(2,1)S(1)} %get-tuple-element.40.after_ref.table_ref, ...), custom_call_target="tpu_custom_call" | custom-call | flops 1150000000 | tf_op jit(solution)/shard_map/own_field/pallas_call | solution.py:318
  30.2 0.8 %collective-permute-done.8.half_ref = bf16[512,128]{1,0:T(8,128)(2,1)S(1)} collective-permute-done((bf16[512,128]{1,0:T(8,128)(2,1)S(1)}, bf16[512,128]{1,0:T(8,128)(2,1)S(1)}, u32[]{:S(2)}, u32[]{:S(2)}) %collective-permute-start.8) | collective-permute-done | bytes 131104 | tf_op jit(solution)/shard_map/ppermute | solution.py:330
  31.0 1.3 %other_field.1 = f32[8,128,128]{2,1,0:T(8,128)} custom-call(bf16[512,128]{1,0:T(8,128)(2,1)S(1)} %collective-permute-done.8.half_ref, f32[1,512]{1,0:T(1,128)S(1)} %get-tuple-element.58.weight_ref, bf16[128,128]{1,0:T(8,128)(2,1)S(1)} %get-tuple-element.59.charge_t_ref, bf16[512,1024]{1,0:T(8,128)(2,1)S(1)} %get-tuple-element.60.table_ref, ...), custom_call_target="tpu_custom_call" | custom-call | flops 1150000000 | tf_op jit(solution)/shard_map/other_field/pallas_call | solution.py:318
  (7 shorter events, 0.1 us)
Async XLA Ops:
  2.5 1.9 %collective-permute-start = (bf16[544,128]{1,0:T(8,128)(2,1)S(1)}, bf16[544,128]{1,0:T(8,128)(2,1)S(1)}, u32[]{:S(2)}, u32[]{:S(2)}) collective-permute-start(bf16[544,128]{1,0:T(8,128)(2,1)S(1)} %get-tuple-element.39), channel_id=1, source_target_pairs={{0,2},{1,3},{2,0},{3,1},{4,6},{5,7},{6,4},{7,5},{8,10},{9,11},{10,... | collective-permute-start | bytes 417800 | tf_op jit(solution)/shard_map/ppermute | solution.py:330
  4.6 5.6 %collective-permute-start.1 = (bf16[544,128]{1,0:T(8,128)(2,1)S(1)}, bf16[544,128]{1,0:T(8,128)(2,1)S(1)}, u32[]{:S(2)}, u32[]{:S(2)}) collective-permute-start(bf16[544,128]{1,0:T(8,128)(2,1)S(1)} %get-tuple-element.43), channel_id=1, source_target_pairs={{0,4},{1,5},{2,10},{3,11},{4,0},{5,1},{6,14},{7,15},{8,12},{9,13},... | collective-permute-start | bytes 417800 | tf_op jit(solution)/shard_map/ppermute | solution.py:330
  7.5 6.1 %collective-permute-start.3 = (bf16[2,2,144,128]{3,2,1,0:T(8,128)(2,1)S(1)}, bf16[2,2,144,128]{3,2,1,0:T(8,128)(2,1)S(1)}, u32[]{:S(2)}, u32[]{:S(2)}) collective-permute-start(bf16[2,2,144,128]{3,2,1,0:T(8,128)(2,1)S(1)} %pad_maximum_fusion.1), channel_id=1, source_target_pairs={{0,1},{1,0},{2,3},{3,2},{4,5},{5,4},{6,7},{7,6},{8,9},{9,8},{10,11... | collective-permute-start | bytes 442376 | tf_op jit(solution)/shard_map/ppermute | solution.py:377
  10.5 5.6 %collective-permute-start.2 = (bf16[544,128]{1,0:T(8,128)(2,1)S(1)}, bf16[544,128]{1,0:T(8,128)(2,1)S(1)}, u32[]{:S(2)}, u32[]{:S(2)}) collective-permute-start(bf16[544,128]{1,0:T(8,128)(2,1)S(1)} %get-tuple-element.51), channel_id=1, source_target_pairs={{0,1},{1,0},{2,18},{3,19},{4,5},{5,4},{6,22},{7,23},{8,9},{9,8},{1... | collective-permute-start | bytes 417800 | tf_op jit(solution)/shard_map/ppermute | solution.py:330
  13.7 11.4 %collective-permute-start.7 = (bf16[6,144,128]{2,1,0:T(8,128)(2,1)S(1)}, bf16[6,144,128]{2,1,0:T(8,128)(2,1)S(1)}, u32[]{:S(2)}, u32[]{:S(2)}) collective-permute-start(bf16[6,144,128]{2,1,0:T(8,128)(2,1)S(1)} %get-tuple-element.61), channel_id=1, source_target_pairs={{0,30},{2,4},{4,2},{6,8},{8,6},{10,12},{12,10},{14,16},{16,14},{18... | collective-permute-start | bytes 663560 | tf_op jit(solution)/shard_map/ppermute | solution.py:390
  16.1 2.9 %collective-permute-start.5 = (bf16[6,144,128]{2,1,0:T(8,128)(2,1)S(1)}, bf16[6,144,128]{2,1,0:T(8,128)(2,1)S(1)}, u32[]{:S(2)}, u32[]{:S(2)}) collective-permute-start(bf16[6,144,128]{2,1,0:T(8,128)(2,1)S(1)} %get-tuple-element.62), channel_id=1, source_target_pairs={{0,2},{2,0},{4,6},{6,4},{8,10},{10,8},{12,14},{14,12},{16,18},{18,... | collective-permute-start | bytes 663560 | tf_op jit(solution)/shard_map/ppermute | solution.py:389
  16.1 2.9 %copy-start = (s32[2,4,5]{2,1,0:T(4,128)S(1)}, s32[2,4,5]{2,1,0:T(4,128)}, u32[]{:S(2)}) copy-start(s32[2,4,5]{2,1,0:T(4,128)} %codes_ref.3) | copy-start | bytes 484
  16.2 2.9 %copy-start.1 = (f32[8,128]{1,0:T(8,128)S(1)}, f32[8,128]{1,0:T(8,128)}, u32[]{:S(2)}) copy-start(f32[8,128]{1,0:T(8,128)} %mix_ref.3) | copy-start | bytes 12292
  16.4 7.5 %collective-permute-start.4 = (bf16[544,128]{1,0:T(8,128)(2,1)S(1)}, bf16[544,128]{1,0:T(8,128)(2,1)S(1)}, u32[]{:S(2)}, u32[]{:S(2)}) collective-permute-start(bf16[544,128]{1,0:T(8,128)(2,1)S(1)} %get-tuple-element.54), channel_id=1, source_target_pairs={{0,16},{1,17},{2,6},{3,7},{4,20},{5,21},{6,2},{7,3},{8,24},{9,25},... | collective-permute-start | bytes 417800 | tf_op jit(solution)/shard_map/ppermute | solution.py:330
  24.2 5.1 %collective-permute-start.6 = (bf16[544,128]{1,0:T(8,128)(2,1)S(1)}, bf16[544,128]{1,0:T(8,128)(2,1)S(1)}, u32[]{:S(2)}, u32[]{:S(2)}) collective-permute-start(bf16[544,128]{1,0:T(8,128)(2,1)S(1)} %get-tuple-element.57), channel_id=1, source_target_pairs={{0,8},{1,9},{2,3},{3,2},{4,12},{5,13},{6,7},{7,6},{8,0},{9,1},{10,... | collective-permute-start | bytes 417800 | tf_op jit(solution)/shard_map/ppermute | solution.py:330
  29.5 1.4 %collective-permute-start.8 = (bf16[512,128]{1,0:T(8,128)(2,1)S(1)}, bf16[512,128]{1,0:T(8,128)(2,1)S(1)}, u32[]{:S(2)}, u32[]{:S(2)}) collective-permute-start(bf16[512,128]{1,0:T(8,128)(2,1)S(1)} %merge.9.half_ref), channel_id=1, source_target_pairs={{0,2},{1,3},{2,0},{3,1},{4,6},{5,7},{6,4},{7,5},{8,10},{9,11},{10,... | collective-permute-start | bytes 393224 | tf_op jit(solution)/shard_map/ppermute | solution.py:330
